TPU v7x, 256 devices: a whole 4x4x8 slice. The times are simulated.
256 devices in a mesh: section: 16 (over y, z_hi), ctx: 16 (over x, z_lo, core).
Axes of the slice: x: 4, y: 4, z: 8 (z_hi: 4, z_lo: 2; z = z_hi * 2 + z_lo), core: 2. Of those that a mesh axis runs over, the one named last changes fastest.
Arguments:
- queries: bfloat16 [16, 2048, 4096], P('section', 'ctx'), may hold values from -50 to 50, as said below
- keys: bfloat16 [16, 2048, 512], P('section', 'ctx'), may hold values from -5 to 5
- values: bfloat16 [16, 2048, 512], P('section', 'ctx'), may hold values from -12 to 12
- residual: bfloat16 [2048, 4096], P('ctx'), may hold values from -6 to 6
- span_map: int32 [16], replicated, may hold values from 0 to 15, as said below
Outputs:
- hidden_states: bfloat16 [16, 2048, 4096], P('section', 'ctx')
Inputs may be any that keep to these rules, and one draw needn't show every extreme that they name: `queries`: queries of some rows may be large multiples of a visible key. `span_map`: each of the 16 spans appears exactly once.
All inputs are finite; a program needn't handle non-finite values.
Results may differ from a plain program's by a relative error of at most 0.008.
Values may be sent and summed in bfloat16 or wider, within the bound.
No kernel may reach another device: no remote copies, remote signals or barrier semaphores. Data moves between devices by JAX's collectives and lax.ppermute only.
A program may use at most 128 MiB of HBM per device.

v0:
```python
import math

import jax
import jax.numpy as jnp
from jax import lax
from jax.sharding import PartitionSpec as P

QUERY_HEADS = 32
KEY_VALUE_HEADS = 4
HEAD_SIZE = 128


def carried_in(x, axis, join, neutral):
    place = lax.axis_index(axis)
    gathered = lax.all_gather(x.astype(jnp.bfloat16), axis)
    state = jnp.zeros_like(x) + jnp.asarray(neutral, x.dtype)

    def one(lap, state):
        return join(state, lax.dynamic_index_in_dim(gathered, lap, 0, False).astype(x.dtype))

    return lax.fori_loop(0, place, one, state)


def add_terms(earlier, later):
    return earlier + later


def body(queries, keys, values, residual, span_map):
    token_rows = queries.shape[1]
    q_width = queries.shape[2]
    query_groups = QUERY_HEADS // KEY_VALUE_HEADS
    span_count = lax.axis_size("ctx")
    span_ids = jnp.arange(span_count, dtype=jnp.int32)
    my_index = lax.axis_index("ctx")
    my_span = jnp.sum(jnp.where(span_ids == my_index, span_map, 0))
    q_positions = my_span * token_rows + jnp.arange(token_rows, dtype=jnp.int32)
    query_head_rows = queries[0].reshape(token_rows, KEY_VALUE_HEADS, query_groups, HEAD_SIZE)
    score_scale = 1.0 / math.sqrt(HEAD_SIZE)
    initial_peak = jnp.full((KEY_VALUE_HEADS, query_groups, token_rows), -1e30, jnp.float32)
    key_portion = lax.all_gather(keys[0], "ctx", axis=0, tiled=True)
    value_portion = lax.all_gather(values[0], "ctx", axis=0, tiled=True)
    portion_rows = key_portion.shape[0]
    key_row_block = jnp.arange(portion_rows, dtype=jnp.int32)
    key_owner = key_row_block // token_rows
    owner_span = jnp.sum(
        jnp.where(key_owner[:, None] == span_ids[None, :], span_map[None, :], 0), axis=1
    )
    key_positions = owner_span * token_rows + key_row_block % token_rows
    visible = key_positions[None, :] <= q_positions[:, None]
    scores = (
        jnp.einsum(
            "tkgd,pkd->kgtp",
            query_head_rows,
            key_portion.reshape(portion_rows, KEY_VALUE_HEADS, HEAD_SIZE),
            preferred_element_type=jnp.float32,
        )
        * score_scale
    )
    masked = jnp.where(visible, scores, jnp.float32(-1e30))
    new_peak = jnp.maximum(initial_peak, jnp.max(masked, axis=3))
    weights = jnp.where(visible, jnp.exp(masked - new_peak[..., None]), jnp.float32(0.0))
    totals = jnp.sum(weights, axis=3)
    weighted = jnp.einsum(
        "kgtp,pkd->kgtd",
        weights.astype(jnp.bfloat16),
        value_portion.reshape(portion_rows, KEY_VALUE_HEADS, HEAD_SIZE),
        preferred_element_type=jnp.float32,
    )
    final_peak, totals, weighted = (new_peak, totals, weighted)
    attention = (weighted / totals[..., None]).transpose(2, 0, 1, 3).reshape(token_rows, q_width)
    earlier_sum = carried_in(attention, "section", add_terms, jnp.zeros_like(attention))
    inclusive = earlier_sum + attention
    hidden_states = residual.astype(jnp.float32) + inclusive
    return hidden_states.astype(jnp.bfloat16)[None]


def solution(mesh):
    placed = (
        P("section", "ctx", None),
        P("section", "ctx", None),
        P("section", "ctx", None),
        P("ctx", None),
        P(),
    )
    return jax.shard_map(
        body, mesh=mesh, in_specs=placed, out_specs=P("section", "ctx", None), check_vma=False
    )
```

profile of v0, /device:TPU:217, one launch (start us, length us, event | category | flops | bytes accessed | tf_op | source)
XLA Modules:
  0.0 344.7 jit_solution(2603616520011390136)
XLA Ops:
  13.6 35.9 %all-gather.8.cloned.1.call-done = bf16[1,2048,512]{1,2,0:T(8,128)(2,1)} async-done(((bf16[1,128,512]{1,2,0:T(8,128)(2,1)}), bf16[1,2048,512]{1,2,0:T(8,128)(2,1)}) %all-gather.8.cloned.1.call-update) | async-done | bytes 2097168 | tf_op jit(solution)/shard_map/all_gather | solution.py:40
  49.5 15.4 %fusion = (f32[4,8,128]{2,1,0:T(8,128)S(1)}, f32[4,2048,128,8]{2,1,3,0:T(8,128)}) fusion(pred[128,2048]{0,1:T(8,128)(4,1)S(1)} %broadcast_compare_fusion, bf16[2048,4,128,1]{0,2,3,1:T(8,128)(2,1)} %bitcast.44, bf16[128,4,8,128]{3,2,1,0:T(8,128)(2,1)S(1)} %bitcast.43), kind=kOutput, calls=%fused_computation.3 | convolution fusion | flops 2172645376 | bytes 36978688 | tf_op jit(solution)/shard_map/tkgd,pkd->kgtp/dot_general | solution.py:51
  64.9 15.1 %fusion.1 = f32[4,8,128]{2,1,0:T(8,128)S(1)} fusion(f32[4,2048,128,8]{2,1,3,0:T(8,128)} %get-tuple-element.38, f32[4,8,128]{2,1,0:T(8,128)S(1)} %broadcast_maximum_fusion, pred[128,2048]{0,1:T(8,128)(4,1)S(1)} %broadcast_compare_fusion), kind=kLoop, calls=%fused_computation.4 | loop fusion | flops 41938944 | bytes 33849344 | tf_op jit(solution)/shard_map/reduce_sum | solution.py:62
  80.0 7.8 %all-gather.10.cloned.1.call-done = bf16[1,2048,512]{2,1,0:T(8,128)(2,1)} async-done(((bf16[1,128,512]{2,1,0:T(8,128)(2,1)}), bf16[1,2048,512]{2,1,0:T(8,128)(2,1)}) %all-gather.10.cloned.1.call-update) | async-done | bytes 2097168 | tf_op jit(solution)/shard_map/all_gather | solution.py:41
  87.8 4.0 %copy.28 = bf16[1,2048,512]{1,2,0:T(8,128)(2,1)} copy(bf16[1,2048,512]{2,1,0:T(8,128)(2,1)} %all-gather.10.cloned.1.call-done) | data formatting | bytes 4194304 | tf_op jit(solution)/shard_map/all_gather | solution.py:41
  91.8 15.2 %fusion.23 = (bf16[128,4,8,128]{0,3,2,1:T(8,128)(2,1)S(1)}, f32[128,4,8,128]{0,3,2,1:T(8,128)S(1)}) fusion(f32[128,4,8]{0,2,1:T(8,128)S(1)} %bitcast.49, bf16[2048,4,128,1]{0,2,3,1:T(8,128)(2,1)} %bitcast.46, f32[4,2048,128,8]{2,1,3,0:T(8,128)} %get-tuple-element.38, f32[4,8,128]{2,1,0:T(8,128)S(1)} %broadcast_maximum_fusion, ...), kind=kOutput, calls=%fused_computation.35 | convolution fusion | flops 2190475264 | bytes 39092224 | tf_op jit(solution)/shard_map/kgtp,pkd->kgtd/dot_general | solution.py:63
  108.4 1.8 copy.31
  110.2 199.0 %all-gather.6.cloned.1.call-done = bf16[16,128,4096]{2,1,0:T(8,128)(2,1)} async-done(((bf16[1,128,4096]{2,1,0:T(8,128)(2,1)}), bf16[16,128,4096]{2,1,0:T(8,128)(2,1)}) %all-gather.6.cloned.1.call-update) | async-done | bytes 16777232 | tf_op jit(solution)/shard_map/all_gather | solution.py:15
  309.4 25.8 %while.10 = (s32[]{:T(128)}, f32[128,4096]{1,0:T(8,128)S(1)}, s32[]{:T(128)}, bf16[16,128,4096]{2,1,0:T(8,128)(2,1)}, s32[]{:T(128)}, /*index=5*/s32[]{:T(128)}, s32[]{:T(128)}) while((s32[]{:T(128)}, f32[128,4096]{1,0:T(8,128)S(1)}, s32[]{:T(128)}, bf16[16,128,4096]{2,1,0:T(8,128)(2,1)}, s32[]{:T(128)}, /*index=5*/s32[]{:T(128)}, ...), condition=%wide.region_5.6_spmd, body=%wide.region_4.5_spmd.sunk | while | flops 1048581 | bytes 5242995 | solution.py:21
  309.4 1.7 convert_add_fusion.2
  311.2 1.7 convert_add_fusion.2
  312.9 1.7 convert_add_fusion.2
  314.6 1.7 convert_add_fusion.2
  316.3 1.7 convert_add_fusion.2
  318.1 1.7 convert_add_fusion.2
  319.8 1.7 convert_add_fusion.2
  321.5 1.7 convert_add_fusion.2
  323.2 1.7 convert_add_fusion.2
  324.9 1.7 convert_add_fusion.2
  326.7 1.7 convert_add_fusion.2
  328.4 1.7 convert_add_fusion.2
  330.1 1.7 convert_add_fusion.2
  331.8 1.7 convert_add_fusion.2
  335.3 2.9 fusion.8
  (20 shorter events, 9.6 us)
Async XLA Ops:
  6.5 43.0 %all-gather.8.cloned.1.call-start = ((), (), s32[]{:S(2)}) async-start(), calls=%async_computation.1 | async-start | bytes 2228224 | tf_op jit(solution)/shard_map/all_gather | solution.py:40
  8.2 79.6 %all-gather.10.cloned.1.call-start = ((), (), s32[]{:S(2)}) async-start(), calls=%async_computation.2 | async-start | bytes 2228224 | tf_op jit(solution)/shard_map/all_gather | solution.py:41
  9.0 300.2 %all-gather.6.cloned.1.call-start = ((), (), s32[]{:S(2)}) async-start(), calls=%async_computation | async-start | bytes 17825792 | tf_op jit(solution)/shard_map/all_gather | solution.py:15
  108.3 226.9 %copy-start = (bf16[128,4096]{1,0:T(8,128)(2,1)S(1)}, bf16[128,4096]{1,0:T(8,128)(2,1)}, u32[]{:S(2)}) copy-start(bf16[128,4096]{1,0:T(8,128)(2,1)} %param.10) | copy-start | bytes 3145732
Sparse Core Ops, SparseCore 0:
  9.1 40.3 all-gather.7
  51.4 36.4 all-gather.9
  108.5 200.6 all-gather.5
where the time goes:
time: 346 us; the launch traced here: 345 us
  waiting for transfers between devices  243 us (70%)
  other arithmetic  45.8 us (13%)
  matrix products  30.6 us (9%)
  between operations  13.8 us (4%)
  local copies, waits for them, and re-layouts  10.4 us (3%)
    all_gather x1, waiting for transfers between devices, carried_in(): gathered = lax.all_gather(x.astype(jnp.bfloat16), axis)  199 us
    all_gather x1, waiting for transfers between devices, body(): key_portion = lax.all_gather(keys[0], 'ctx', axis=0, tiled=True)  35.9 us
    add x15, other arithmetic, add_terms(): return earlier + later  25.4 us
    dot_general x1, matrix products, body(): jnp.einsum('tkgd,pkd->kgtp', query_head_rows, key_portion.reshape(portion...  15.4 us
    dot_general x1, matrix products, body(): jnp.einsum('kgtp,pkd->kgtd', weights.astype(jnp.bfloat16), value_portion....  15.2 us
    reduce_sum x1, other arithmetic, body(): totals = jnp.sum(weights, axis=3)  15.1 us
    all_gather x1, waiting for transfers between devices, body(): value_portion = lax.all_gather(values[0], 'ctx', axis=0, tiled=True)  7.84 us
  transfers between devices with their start and end apart: 3, of which 3 were waited for; matrix products, arithmetic and copies ran while one was open for 10% of the time, Pallas kernels for 0%

commit v1 on v0

v1 whole, which is shorter than its diff:
```python
import functools
import math

import jax
import jax.numpy as jnp
from jax import lax
from jax.experimental import pallas as pl
from jax.experimental.pallas import tpu as pltpu
from jax.sharding import PartitionSpec as P

KEY_VALUE_HEADS = 4
GROUP = 8
HEAD_SIZE = 128
TOK = 128
SPANS = 16
LAYERS = 16
TRACE = SPANS * TOK
EXP2_SCALE = math.log2(math.e) / math.sqrt(HEAD_SIZE)
HIDDEN = -1e30
VMEM_LIMIT = 48 * 2**20


def attention_kernel(meta, q_ref, k_ref, v_ref, o_ref, keys, vals, eye, *, heads):
    @pl.when(pl.program_id(0) == 0)
    def _():
        key_row = lax.broadcasted_iota(jnp.int32, (TOK, TOK), 0)
        query_row = lax.broadcasted_iota(jnp.int32, (TOK, TOK), 1)
        eye[...] = jnp.where(key_row == query_row, 1.0, 0.0).astype(jnp.bfloat16)
        vals[:, HEAD_SIZE:] = jnp.ones((TRACE, HEAD_SIZE), jnp.bfloat16)
        for block in range(SPANS):
            ahead = (meta[block] - meta[SPANS]) * TOK + key_row - query_row
            keys[block * TOK : (block + 1) * TOK, HEAD_SIZE:] = jnp.where(
                ahead > 0, HIDDEN, 0.0
            ).astype(jnp.bfloat16)

    keys[:, :HEAD_SIZE] = k_ref[...].reshape(TRACE, HEAD_SIZE)
    vals[:, :HEAD_SIZE] = v_ref[...].reshape(TRACE, HEAD_SIZE)
    one_hot = eye[...]
    for tile in range(GROUP // heads):
        first = tile * heads
        q = jnp.concatenate(
            [
                jnp.concatenate(
                    [q_ref[:, h * HEAD_SIZE : (h + 1) * HEAD_SIZE], one_hot], axis=1
                )
                for h in range(first, first + heads)
            ],
            axis=0,
        )
        scores = lax.dot_general(
            q, keys[...], (((1,), (1,)), ((), ())), preferred_element_type=jnp.float32
        )
        peak = jnp.max(scores, axis=1, keepdims=True)
        weights = jnp.exp2((scores - peak) * EXP2_SCALE).astype(jnp.bfloat16)
        mixed = jnp.dot(weights, vals[...], preferred_element_type=jnp.float32)
        result = (mixed[:, :HEAD_SIZE] / mixed[:, HEAD_SIZE:]).astype(jnp.bfloat16)
        for i in range(heads):
            h = first + i
            o_ref[h // 2, :, (h % 2) * HEAD_SIZE : (h % 2 + 1) * HEAD_SIZE] = result[
                i * TOK : (i + 1) * TOK
            ]


def attention(queries, kv, meta, heads=2):
    width = GROUP * HEAD_SIZE
    return pl.pallas_call(
        functools.partial(attention_kernel, heads=heads),
        grid_spec=pltpu.PrefetchScalarGridSpec(
            num_scalar_prefetch=1,
            grid=(KEY_VALUE_HEADS,),
            in_specs=[
                pl.BlockSpec((TOK, width), lambda g, m: (0, g)),
                pl.BlockSpec((SPANS, TOK, HEAD_SIZE), lambda g, m: (0, 0, g)),
                pl.BlockSpec((SPANS, TOK, HEAD_SIZE), lambda g, m: (0, 0, KEY_VALUE_HEADS + g)),
            ],
            out_specs=pl.BlockSpec((4, TOK, 2 * HEAD_SIZE), lambda g, m: (g, 0, 0)),
            scratch_shapes=[
                pltpu.VMEM((TRACE, 2 * HEAD_SIZE), jnp.bfloat16),
                pltpu.VMEM((TRACE, 2 * HEAD_SIZE), jnp.bfloat16),
                pltpu.VMEM((TOK, TOK), jnp.bfloat16),
            ],
        ),
        out_shape=jax.ShapeDtypeStruct((LAYERS, TOK, 2 * HEAD_SIZE), jnp.bfloat16),
        compiler_params=pltpu.CompilerParams(vmem_limit_bytes=VMEM_LIMIT),
        name="attention",
    )(meta, queries, kv, kv)


def prefix_kernel(place, x_ref, residual_ref, o_ref):
    state = residual_ref[...].astype(jnp.float32)
    for layer in range(LAYERS):
        state = state + x_ref[layer].astype(jnp.float32)
        o_ref[layer] = state.astype(jnp.bfloat16)


def prefix(layers, residual, place):
    rows = 32
    width = 2 * HEAD_SIZE
    block = pl.BlockSpec((LAYERS, rows, width), lambda r, s: (0, r, 0))
    return pl.pallas_call(
        prefix_kernel,
        grid_spec=pltpu.PrefetchScalarGridSpec(
            num_scalar_prefetch=1,
            grid=(TOK // rows,),
            in_specs=[block, pl.BlockSpec((rows, width), lambda r, s: (r, s[0]))],
            out_specs=block,
        ),
        out_shape=jax.ShapeDtypeStruct((LAYERS, TOK, width), jnp.bfloat16),
        name="prefix",
    )(place, layers, residual)


def assemble_kernel(x_ref, o_ref):
    width = 2 * HEAD_SIZE
    for slab in range(LAYERS):
        o_ref[0, :, slab * width : (slab + 1) * width] = x_ref[slab]


def assemble(slabs):
    rows = 32
    width = LAYERS * 2 * HEAD_SIZE
    return pl.pallas_call(
        assemble_kernel,
        grid=(TOK // rows,),
        in_specs=[pl.BlockSpec((LAYERS, rows, 2 * HEAD_SIZE), lambda r: (0, r, 0))],
        out_specs=pl.BlockSpec((1, rows, width), lambda r: (0, r, 0)),
        out_shape=jax.ShapeDtypeStruct((1, TOK, width), jnp.bfloat16),
        name="assemble",
    )(slabs)


def body(queries, keys, values, residual, span_map):
    ctx = lax.axis_index("ctx")
    my_span = lax.dynamic_index_in_dim(span_map, ctx, 0, True)
    meta = jnp.concatenate([span_map, my_span])
    kv = lax.all_gather(jnp.concatenate([keys[0], values[0]], axis=1), "ctx")
    by_head = attention(queries[0], kv, meta)
    by_layer = lax.all_to_all(by_head, "section", 0, 0, tiled=True)
    summed = prefix(by_layer, residual, lax.axis_index("section")[None])
    mine = lax.all_to_all(summed, "section", 0, 0, tiled=True)
    return assemble(mine)


def solution(mesh):
    placed = (
        P("section", "ctx", None),
        P("section", "ctx", None),
        P("section", "ctx", None),
        P("ctx", None),
        P(),
    )
    return jax.shard_map(
        body, mesh=mesh, in_specs=placed, out_specs=P("section", "ctx", None), check_vma=False
    )
```

time: 346 us -> 156 us (0.45)
  the two profiles are of different devices: /device:TPU:217 before, /device:TPU:2 now
where the time goes in v1:
time: 156 us
  waiting for transfers between devices  71.9 us (46%)
  blocking collectives  32 us (21%)
  Pallas kernels  22.9 us (15%)
  between operations  13.4 us (9%)
  starting transfers between devices  8.89 us (6%)
  local copies, waits for them, and re-layouts  3.44 us (2%)
  other arithmetic  3.03 us (2%)
    all_gather x1, waiting for transfers between devices, body(): kv = lax.all_gather(jnp.concatenate([keys[0], values[0]], axis=1), 'ctx')  41.2 us
    all_to_all x1, blocking collectives, body(): mine = lax.all_to_all(summed, 'section', 0, 0, tiled=True)  32 us
    all_to_all x1, waiting for transfers between devices, body(): by_layer = lax.all_to_all(by_head, 'section', 0, 0, tiled=True)  30.7 us
    pallas_call x1, Pallas kernels, attention(): pl.pallas_call(functools.partial(attention_kernel, heads=heads), grid_spe...  16.1 us
    all_to_all x1, starting transfers between devices, body(): by_layer = lax.all_to_all(by_head, 'section', 0, 0, tiled=True)  8.89 us
    pallas_call x1, Pallas kernels, prefix(): pl.pallas_call(prefix_kernel, grid_spec=pltpu.PrefetchScalarGridSpec(num_...  3.45 us
    pallas_call x1, Pallas kernels, assemble(): pl.pallas_call(assemble_kernel, grid=(TOK // rows,), in_specs=[pl.BlockSp...  3.36 us
  transfers between devices with their start and end apart: 2, of which 2 were waited for; matrix products, arithmetic and copies ran while one was open for 2% of the time, Pallas kernels for 0%

profile of v1, /device:TPU:2, one launch (start us, length us, event | category | flops | bytes accessed | tf_op | source)
XLA Modules:
  0.0 155.6 jit_solution(6823940369505769954)
XLA Ops:
  6.5 0.0 all-gather.3.cloned.1.call-start
  6.5 1.7 %pad_maximum_fusion = bf16[128,1024]{1,0:T(8,128)(2,1)} fusion(bf16[128,512]{1,0:T(8,128)(2,1)} %bitcast.8, bf16[128,512]{1,0:T(8,128)(2,1)} %bitcast.9), kind=kLoop, calls=%fused_computation | loop fusion | flops 524288 | bytes 524288 | tf_op jit(solution)/shard_map/concatenate | solution.py:136
  8.2 0.0 all-gather.3.cloned.1.call-update
  8.3 1.2 dynamic_slice.4
  9.5 1.3 pad_add_fusion.meta
  10.8 41.2 %all-gather.3.cloned.1.call-done = bf16[2048,1024]{1,0:T(8,128)(2,1)} async-done(((bf16[128,1024]{1,0:T(8,128)(2,1)}), bf16[2048,1024]{1,0:T(8,128)(2,1)}) %all-gather.3.cloned.1.call-update) | async-done | bytes 4194320 | tf_op jit(solution)/shard_map/all_gather | solution.py:136
  52.0 0.0 copy-start
  52.0 1.2 copy-done
  53.3 16.1 %attention.1 = bf16[16,128,256]{2,1,0:T(8,128)(2,1)} custom-call(s32[17]{0:T(128)S(1)} %pad_add_fusion.meta, bf16[128,4096]{1,0:T(8,128)(2,1)S(1)} %bitcast.5, bf16[16,128,1024]{2,1,0:T(8,128)(2,1)} %bitcast.6, bf16[16,128,1024]{2,1,0:T(8,128)(2,1)} %bitcast.7), custom_call_target="tpu_custom_call" | custom-call | tf_op jit(solution)/shard_map/attention/pallas_call | solution.py:66
  69.3 8.9 %all-to-all-start = ((bf16[16,128,256]{2,1,0:T(8,128)(2,1)}), bf16[16,128,256]{2,1,0:T(8,128)(2,1)S(1)}, u32[]{:S(2)}, u32[]{:S(2)}) async-start(bf16[16,128,256]{2,1,0:T(8,128)(2,1)} %attention.1), calls=%async_computation | async-start | bytes 2097152 | tf_op jit(solution)/shard_map/all_to_all | solution.py:138
  78.2 30.7 %all-to-all-done.x_ref = bf16[16,128,256]{2,1,0:T(8,128)(2,1)S(1)} async-done(((bf16[16,128,256]{2,1,0:T(8,128)(2,1)}), bf16[16,128,256]{2,1,0:T(8,128)(2,1)S(1)}, u32[]{:S(2)}, u32[]{:S(2)}) %all-to-all-start) | async-done | bytes 1048608 | tf_op jit(solution)/shard_map/all_to_all | solution.py:138
  108.9 0.0 copy-start.1
  108.9 1.0 copy-done.1
  109.9 3.4 %prefix.1 = bf16[16,128,256]{2,1,0:T(8,128)(2,1)} custom-call(s32[1]{0:T(128)} %bitcast.place, bf16[16,128,256]{2,1,0:T(8,128)(2,1)} %copy-done.1, bf16[128,4096]{1,0:T(8,128)(2,1)} %residual_ref.1), custom_call_target="tpu_custom_call" | custom-call | tf_op jit(solution)/shard_map/prefix/pallas_call | solution.py:100
  113.3 32.0 %all_to_all.10.x_ref = bf16[16,128,256]{2,1,0:T(8,128)(2,1)} all-to-all(bf16[16,128,256]{2,1,0:T(8,128)(2,1)} %prefix.1), channel_id=1, replica_groups=mesh['section'=16,'ctx'=16] {'section'}, dimensions={0} | all-to-all | bytes 2097152 | tf_op jit(solution)/shard_map/all_to_all | solution.py:140
  145.3 3.4 %assemble.1 = bf16[1,128,4096]{2,1,0:T(8,128)(2,1)} custom-call(bf16[16,128,256]{2,1,0:T(8,128)(2,1)} %all_to_all.10.x_ref), custom_call_target="tpu_custom_call" | custom-call | tf_op jit(solution)/shard_map/assemble/pallas_call | solution.py:122
Async XLA Ops:
  6.5 45.5 %all-gather.3.cloned.1.call-start = ((), (), s32[]{:S(2)}) async-start(), calls=%async_computation.2 | async-start | bytes 4456448 | tf_op jit(solution)/shard_map/all_gather | solution.py:136
  52.0 1.2 copy-start
  69.3 39.6 %all-to-all-start = ((bf16[16,128,256]{2,1,0:T(8,128)(2,1)}), bf16[16,128,256]{2,1,0:T(8,128)(2,1)S(1)}, u32[]{:S(2)}, u32[]{:S(2)}) async-start(bf16[16,128,256]{2,1,0:T(8,128)(2,1)} %attention.1), calls=%async_computation | async-start | bytes 2097152 | tf_op jit(solution)/shard_map/all_to_all | solution.py:138
  108.9 1.0 copy-start.1
Sparse Core Ops, SparseCore 0:
  9.2 42.7 all-gather.2

commit v2 on v1

v2 whole, which is shorter than its diff:
```python
import functools
import math

import jax
import jax.numpy as jnp
from jax import lax
from jax.experimental import pallas as pl
from jax.experimental.pallas import tpu as pltpu
from jax.sharding import PartitionSpec as P

KEY_VALUE_HEADS = 4
GROUP = 8
HEAD_SIZE = 128
TOK = 128
SPANS = 16
TRACE = SPANS * TOK
WIDTH = KEY_VALUE_HEADS * HEAD_SIZE
RING = 4
PAIR = 2 * HEAD_SIZE
EXP2_SCALE = math.log2(math.e) / math.sqrt(HEAD_SIZE)
HIDDEN = -1e30
VMEM_LIMIT = 40 * 2**20
CHUNKS = 2
PART = KEY_VALUE_HEADS // CHUNKS

UNITS = [(dx, dz, dc) for dc in range(2) for dz in range(2) for dx in range(4)]


def ctx_pairs(dx, dz, dc):
    pairs = []
    for i in range(SPANS):
        x, z, c = i // 4, i // 2 % 2, i % 2
        pairs.append((i, (x + dx) % 4 * 4 + (z ^ dz) * 2 + (c ^ dc)))
    return pairs


def ctx_move(unit, dx, dz, dc):
    return lax.ppermute(unit, "ctx", ctx_pairs(dx, dz, dc))


def turn_pairs(steps):
    return [(i, i // RING * RING + (i + steps) % RING) for i in range(RING * RING)]


def climb_pairs(steps):
    return [(i, i + RING * steps) for i in range(RING * (RING - steps))]


def join_kernel(k_ref, v_ref, o_ref):
    o_ref[:, :WIDTH] = k_ref[0]
    o_ref[:, WIDTH:] = v_ref[0]


def join(keys, values):
    return pl.pallas_call(
        join_kernel,
        out_shape=jax.ShapeDtypeStruct((TOK, 2 * WIDTH), jnp.bfloat16),
        name="join",
    )(keys, values)


def gather(keys, values):
    own = join(keys, values)
    held = {(0, 0, 0): own}
    held[0, 1, 0] = ctx_move(own, 0, 1, 0)
    for dx in (1, 3, 2):
        held[dx, 0, 0] = ctx_move(own, dx, 0, 0)
    for dx in (1, 3, 2):
        held[dx, 1, 0] = ctx_move(held[0, 1, 0], dx, 0, 0)
    for dz in range(2):
        for dx in range(4):
            held[dx, dz, 1] = ctx_move(held[dx, dz, 0], 0, 0, 1)
    return [held[unit] for unit in UNITS]


def attention_kernel(span_map, ctx, section, q_ref, *refs):
    k_refs, v_refs = refs[:SPANS], refs[SPANS : 2 * SPANS]
    o_refs = refs[2 * SPANS : 2 * SPANS + RING]
    keys, vals, eye = refs[2 * SPANS + RING :]

    @pl.when(pl.program_id(0) == 0)
    def _():
        key_row = lax.broadcasted_iota(jnp.int32, (TOK, TOK), 0)
        query_row = lax.broadcasted_iota(jnp.int32, (TOK, TOK), 1)
        eye[...] = jnp.where(key_row == query_row, 1.0, 0.0).astype(jnp.bfloat16)
        vals[:, HEAD_SIZE:] = jnp.ones((TRACE, HEAD_SIZE), jnp.bfloat16)
        me = ctx[0]
        my_span = span_map[me]
        x, z, c = me // 4, me // 2 % 2, me % 2
        for block, (dx, dz, dc) in enumerate(UNITS):
            source = (x + 4 - dx) % 4 * 4 + (z + dz) % 2 * 2 + (c + dc) % 2
            ahead = (span_map[source] - my_span) * TOK + key_row - query_row
            keys[block * TOK : (block + 1) * TOK, HEAD_SIZE:] = jnp.where(
                ahead > 0, HIDDEN, 0.0
            ).astype(jnp.bfloat16)

    for block in range(SPANS):
        rows = slice(block * TOK, (block + 1) * TOK)
        keys[rows, :HEAD_SIZE] = k_refs[block][...]
        vals[rows, :HEAD_SIZE] = v_refs[block][...]
    one_hot = eye[...]
    place = section[0] % RING
    for steps in range(RING):
        first = pl.multiple_of((place + steps) % RING * PAIR, PAIR)
        q = q_ref[:, pl.ds(first, PAIR)]
        q = jnp.concatenate(
            [
                jnp.concatenate([q[:, :HEAD_SIZE], one_hot], axis=1),
                jnp.concatenate([q[:, HEAD_SIZE:], one_hot], axis=1),
            ],
            axis=0,
        )
        scores = lax.dot_general(
            q, keys[...], (((1,), (1,)), ((), ())), preferred_element_type=jnp.float32
        )
        peak = jnp.max(scores, axis=1, keepdims=True)
        weights = jnp.exp2((scores - peak) * EXP2_SCALE).astype(jnp.bfloat16)
        mixed = jnp.dot(weights, vals[...], preferred_element_type=jnp.float32)
        result = (mixed[:, :HEAD_SIZE] / mixed[:, HEAD_SIZE:]).astype(jnp.bfloat16)
        o_refs[steps][:, :HEAD_SIZE] = result[:TOK]
        o_refs[steps][:, HEAD_SIZE:] = result[TOK:]


def attention(span_map, ctx, section, queries, units, chunk):
    base = chunk * PART
    slab = jax.ShapeDtypeStruct((TOK, PART * PAIR), jnp.bfloat16)
    return pl.pallas_call(
        attention_kernel,
        grid_spec=pltpu.PrefetchScalarGridSpec(
            num_scalar_prefetch=3,
            grid=(PART,),
            in_specs=[pl.BlockSpec((TOK, GROUP * HEAD_SIZE), lambda g, *_: (0, base + g))]
            + [pl.BlockSpec((TOK, HEAD_SIZE), lambda g, *_: (0, base + g))] * SPANS
            + [pl.BlockSpec((TOK, HEAD_SIZE), lambda g, *_: (0, KEY_VALUE_HEADS + base + g))]
            * SPANS,
            out_specs=[pl.BlockSpec((TOK, PAIR), lambda g, *_: (0, g))] * RING,
            scratch_shapes=[
                pltpu.VMEM((TRACE, PAIR), jnp.bfloat16),
                pltpu.VMEM((TRACE, PAIR), jnp.bfloat16),
                pltpu.VMEM((TOK, TOK), jnp.bfloat16),
            ],
        ),
        out_shape=[slab] * RING,
        compiler_params=pltpu.CompilerParams(vmem_limit_bytes=VMEM_LIMIT),
        cost_estimate=pl.CostEstimate(
            flops=PART * GROUP * TOK * TRACE * PAIR * 2 * 2,
            bytes_accessed=PART * (TRACE * PAIR + GROUP * TOK * PAIR) * 2,
            transcendentals=PART * GROUP * TOK * TRACE,
        ),
        name="attention",
    )(span_map, ctx, section, queries, *units, *units)


def total_kernel(a, b, c, d, o_ref):
    f32 = jnp.float32
    o_ref[...] = (
        a[...].astype(f32) + b[...].astype(f32) + (c[...].astype(f32) + d[...].astype(f32))
    ).astype(jnp.bfloat16)


def row_total(slabs):
    return pl.pallas_call(
        total_kernel,
        out_shape=jax.ShapeDtypeStruct((TOK, PART * PAIR), jnp.bfloat16),
        name="row_total",
    )(*slabs)


def prefix_kernel(chunk, section, residual_ref, *refs):
    slabs, below, outs = refs[:RING], refs[RING : 2 * RING - 1], refs[2 * RING - 1 : 3 * RING - 1]
    ordered, summed = refs[3 * RING - 1 :]
    place = section[0] % RING
    for steps in range(RING):
        ordered[(place + RING - steps) % RING] = slabs[steps][...]
    for part in range(PART):
        columns = slice(part * PAIR, (part + 1) * PAIR)
        first = (chunk * PART + part) * GROUP * HEAD_SIZE + place * PAIR
        state = residual_ref[:, pl.ds(pl.multiple_of(first, PAIR), PAIR)].astype(jnp.float32)
        for rows in below:
            state = state + rows[:, columns].astype(jnp.float32)
        for layer in range(RING):
            state = state + ordered[layer, :, columns].astype(jnp.float32)
            summed[layer, :, columns] = state.astype(jnp.bfloat16)
    for steps in range(RING):
        outs[steps][...] = summed[(place + steps) % RING]


def prefix(section, residual, slabs, below, chunk):
    slab = jax.ShapeDtypeStruct((TOK, PART * PAIR), jnp.bfloat16)
    whole = pl.BlockSpec(memory_space=pltpu.VMEM)
    return pl.pallas_call(
        functools.partial(prefix_kernel, chunk),
        in_specs=[pl.BlockSpec(memory_space=pltpu.SMEM)] + [whole] * (2 * RING),
        out_specs=[whole] * RING,
        out_shape=[slab] * RING,
        scratch_shapes=[
            pltpu.VMEM((RING, TOK, PART * PAIR), jnp.bfloat16),
            pltpu.VMEM((RING, TOK, PART * PAIR), jnp.bfloat16),
        ],
        name="prefix",
    )(section, residual, *slabs, *below)


def assemble_kernel(section, *refs):
    slabs, o_ref = refs[:-1], refs[-1]
    place = section[0] % RING
    for chunk in range(CHUNKS):
        for steps in range(RING):
            column = (place + RING - steps) % RING * PAIR
            for part in range(PART):
                first = (chunk * PART + part) * GROUP * HEAD_SIZE + column
                o_ref[0, :, pl.ds(pl.multiple_of(first, PAIR), PAIR)] = slabs[
                    chunk * RING + steps
                ][:, part * PAIR : (part + 1) * PAIR]


def assemble(section, slabs):
    whole = pl.BlockSpec(memory_space=pltpu.VMEM)
    width = KEY_VALUE_HEADS * GROUP * HEAD_SIZE
    return pl.pallas_call(
        assemble_kernel,
        in_specs=[pl.BlockSpec(memory_space=pltpu.SMEM)] + [whole] * len(slabs),
        out_specs=whole,
        out_shape=jax.ShapeDtypeStruct((1, TOK, width), jnp.bfloat16),
        name="assemble",
    )(section, *slabs)


def turn(slabs):
    return [slabs[0]] + [
        lax.ppermute(slabs[steps], "section", turn_pairs(steps)) for steps in range(1, RING)
    ]


def body(queries, keys, values, residual, span_map):
    ctx = lax.axis_index("ctx")[None]
    section = lax.axis_index("section")[None]
    units = gather(keys, values)
    finished = []
    for chunk in range(CHUNKS):
        slabs = turn(attention(span_map, ctx, section, queries[0], units, chunk))
        total = row_total(slabs)
        below = [lax.ppermute(total, "section", climb_pairs(s)) for s in range(1, RING)]
        finished += turn(prefix(section, residual, slabs, below, chunk))
    return assemble(section, finished)


def solution(mesh):
    placed = (
        P("section", "ctx", None),
        P("section", "ctx", None),
        P("section", "ctx", None),
        P("ctx", None),
        P(),
    )
    return jax.shard_map(
        body, mesh=mesh, in_specs=placed, out_specs=P("section", "ctx", None), check_vma=False
    )
```

time: 156 us -> 130 us (0.83)
  the two profiles are of different devices: /device:TPU:2 before, /device:TPU:1 now
where the time goes in v2:
time: 130 us; the launch traced here: 129 us
  starting transfers between devices  62.4 us (48%)
  Pallas kernels  30.7 us (24%)
  waiting for transfers between devices  26.7 us (21%)
  local copies, waits for them, and re-layouts  9.23 us (7%)
    ppermute x12, starting transfers between devices, turn(): lax.ppermute(slabs[steps], 'section', turn_pairs(steps))  26.6 us
    ppermute x15, starting transfers between devices, ctx_move(): return lax.ppermute(unit, 'ctx', ctx_pairs(dx, dz, dc))  19 us
    pallas_call x2, Pallas kernels, attention(): pl.pallas_call(attention_kernel, grid_spec=pltpu.PrefetchScalarGridSpec(n...  17.9 us
    ppermute x6, starting transfers between devices, body(): lax.ppermute(total, 'section', climb_pairs(s))  16.8 us
    ppermute x15, waiting for transfers between devices, ctx_move(): return lax.ppermute(unit, 'ctx', ctx_pairs(dx, dz, dc))  15.9 us
    ppermute x12, waiting for transfers between devices, turn(): lax.ppermute(slabs[steps], 'section', turn_pairs(steps))  10.8 us
    unnamed x46, local copies, waits for them, and re-layouts  9.23 us
    pallas_call x2, Pallas kernels, prefix(): pl.pallas_call(functools.partial(prefix_kernel, chunk), in_specs=[pl.Bloc...  5.1 us
  transfers between devices with their start and end apart: 33, of which 10 were waited for; matrix products, arithmetic and copies ran while one was open for 0% of the time, Pallas kernels for 14%

profile of v2, /device:TPU:1, one launch (start us, length us, event | category | flops | bytes accessed | tf_op | source)
XLA Modules:
  0.0 129.4 jit_solution(2165374152352062243)
XLA Ops:
  1.7 2.5 %collective-permute-start.3 = (bf16[128,1024]{1,0:T(8,128)(2,1)}, bf16[128,1024]{1,0:T(8,128)(2,1)S(1)}, u32[]{:S(2)}, u32[]{:S(2)}) collective-permute-start(bf16[128,1024]{1,0:T(8,128)(2,1)} %join.1.refs_0_.refs_16_), channel_id=1, source_target_pairs={{0,2},{1,3},{2,0},{3,1},{4,6},{5,7},{6,4},{7,5},{8,10},{9,11},{10,... | collective-permute-start | bytes 786440 | tf_op jit(solution)/shard_map/ppermute | solution.py:38
  5.1 2.5 %collective-permute-start.2 = (bf16[128,1024]{1,0:T(8,128)(2,1)}, bf16[128,1024]{1,0:T(8,128)(2,1)S(1)}, u32[]{:S(2)}, u32[]{:S(2)}) collective-permute-start(bf16[128,1024]{1,0:T(8,128)(2,1)} %join.1.refs_0_.refs_16_), channel_id=1, source_target_pairs={{0,12},{1,13},{2,14},{3,15},{4,0},{5,1},{6,2},{7,3},{8,4},{9,5},{1... | collective-permute-start | bytes 786440 | tf_op jit(solution)/shard_map/ppermute | solution.py:38
  11.6 2.5 %collective-permute-start.6 = (bf16[128,1024]{1,0:T(8,128)(2,1)S(1)}, bf16[128,1024]{1,0:T(8,128)(2,1)S(1)}, u32[]{:S(2)}, u32[]{:S(2)}) collective-permute-start(bf16[128,1024]{1,0:T(8,128)(2,1)S(1)} %collective-permute-done.3.refs_4_.refs_20_), channel_id=1, source_target_pairs={{0,12},{1,13},{2,14},{3,15},{4,0},{5,1},{6,2},{7,3},{8,4},{9,5},{1... | collective-permute-start | bytes 786440 | tf_op jit(solution)/shard_map/ppermute | solution.py:38
  14.1 5.0 %collective-permute-done.2.refs_3_.refs_19_ = bf16[128,1024]{1,0:T(8,128)(2,1)S(1)} collective-permute-done((bf16[128,1024]{1,0:T(8,128)(2,1)}, bf16[128,1024]{1,0:T(8,128)(2,1)S(1)}, u32[]{:S(2)}, u32[]{:S(2)}) %collective-permute-start.2) | collective-permute-done | bytes 262176 | tf_op jit(solution)/shard_map/ppermute | solution.py:38
  19.1 4.0 %collective-permute-start.4 = (bf16[128,1024]{1,0:T(8,128)(2,1)S(1)}, bf16[128,1024]{1,0:T(8,128)(2,1)S(1)}, u32[]{:S(2)}, u32[]{:S(2)}) collective-permute-start(bf16[128,1024]{1,0:T(8,128)(2,1)S(1)} %collective-permute-done.3.refs_4_.refs_20_), channel_id=1, source_target_pairs={{0,4},{1,5},{2,6},{3,7},{4,8},{5,9},{6,10},{7,11},{8,12},{9,13},{1... | collective-permute-start | bytes 786440 | tf_op jit(solution)/shard_map/ppermute | solution.py:38
  25.0 5.3 %collective-permute-done.6.refs_7_.refs_23_ = bf16[128,1024]{1,0:T(8,128)(2,1)S(1)} collective-permute-done((bf16[128,1024]{1,0:T(8,128)(2,1)S(1)}, bf16[128,1024]{1,0:T(8,128)(2,1)S(1)}, u32[]{:S(2)}, u32[]{:S(2)}) %collective-permute-start.6) | collective-permute-done | bytes 262176 | tf_op jit(solution)/shard_map/ppermute | solution.py:38
  31.2 3.3 %collective-permute-done.4.refs_5_.refs_21_ = bf16[128,1024]{1,0:T(8,128)(2,1)S(1)} collective-permute-done((bf16[128,1024]{1,0:T(8,128)(2,1)S(1)}, bf16[128,1024]{1,0:T(8,128)(2,1)S(1)}, u32[]{:S(2)}, u32[]{:S(2)}) %collective-permute-start.4) | collective-permute-done | bytes 262176 | tf_op jit(solution)/shard_map/ppermute | solution.py:38
  39.5 8.7 %attention.3 = (bf16[128,512]{1,0:T(8,128)(2,1)S(1)}, bf16[128,512]{1,0:T(8,128)(2,1)S(1)}, bf16[128,512]{1,0:T(8,128)(2,1)S(1)}, bf16[128,512]{1,0:T(8,128)(2,1)S(1)}) custom-call(s32[16]{0:T(128)S(1)} %copy-done.4, s32[1]{0:T(128)} %bitcast.1.ctx, s32[1]{0:T(128)} %bitcast.section, bf16[128,4096]{1,0:T(8,128)(2,1)S(1)} %bitcast.3, ...), custom_call_target="tpu_custom_call" | custom-call | flops 4294967296 | bytes 3145728 | tf_op jit(solution)/shard_map/attention/pallas_call | solution.py:127
  48.8 3.0 %collective-permute-start.24 = (bf16[128,512]{1,0:T(8,128)(2,1)S(1)}, bf16[128,512]{1,0:T(8,128)(2,1)S(1)}, u32[]{:S(2)}, u32[]{:S(2)}) collective-permute-start(bf16[128,512]{1,0:T(8,128)(2,1)S(1)} %get-tuple-element.30), channel_id=1, source_target_pairs={{0,16},{16,32},{32,48},{48,0},{64,80},{80,96},{96,112},{112,64},{1... | collective-permute-start | bytes 393224 | tf_op jit(solution)/shard_map/ppermute | solution.py:231
  51.8 4.2 %collective-permute-start.25 = (bf16[128,512]{1,0:T(8,128)(2,1)S(1)}, bf16[128,512]{1,0:T(8,128)(2,1)S(1)}, u32[]{:S(2)}, u32[]{:S(2)}) collective-permute-start(bf16[128,512]{1,0:T(8,128)(2,1)S(1)} %get-tuple-element.31), channel_id=1, source_target_pairs={{0,32},{16,48},{32,0},{48,16},{64,96},{80,112},{96,64},{112,80},{1... | collective-permute-start | bytes 393224 | tf_op jit(solution)/shard_map/ppermute | solution.py:231
  56.0 2.4 %collective-permute-start.26 = (bf16[128,512]{1,0:T(8,128)(2,1)S(1)}, bf16[128,512]{1,0:T(8,128)(2,1)S(1)}, u32[]{:S(2)}, u32[]{:S(2)}) collective-permute-start(bf16[128,512]{1,0:T(8,128)(2,1)S(1)} %get-tuple-element.32), channel_id=1, source_target_pairs={{0,48},{16,0},{32,16},{48,32},{64,112},{80,64},{96,80},{112,96},{1... | collective-permute-start | bytes 393224 | tf_op jit(solution)/shard_map/ppermute | solution.py:231
  58.4 9.3 %attention.2 = (bf16[128,512]{1,0:T(8,128)(2,1)S(1)}, bf16[128,512]{1,0:T(8,128)(2,1)}, bf16[128,512]{1,0:T(8,128)(2,1)}, bf16[128,512]{1,0:T(8,128)(2,1)S(1)}) custom-call(s32[16]{0:T(128)S(1)} %copy-done.4, s32[1]{0:T(128)} %bitcast.1.ctx, s32[1]{0:T(128)} %bitcast.section, bf16[128,4096]{1,0:T(8,128)(2,1)S(1)} %bitcast.4, ...), custom_call_target="tpu_custom_call" | custom-call | flops 4294967296 | bytes 3145728 | tf_op jit(solution)/shard_map/attention/pallas_call | solution.py:127
  70.4 2.4 %collective-permute-start.17 = (bf16[128,512]{1,0:T(8,128)(2,1)S(1)}, bf16[128,512]{1,0:T(8,128)(2,1)S(1)}, u32[]{:S(2)}, u32[]{:S(2)}) collective-permute-start(bf16[128,512]{1,0:T(8,128)(2,1)S(1)} %get-tuple-element.24), channel_id=1, source_target_pairs={{0,48},{16,0},{32,16},{48,32},{64,112},{80,64},{96,80},{112,96},{1... | collective-permute-start | bytes 393224 | tf_op jit(solution)/shard_map/ppermute | solution.py:231
  75.9 4.6 %collective-permute-start.29 = (bf16[128,512]{1,0:T(8,128)(2,1)}, bf16[128,512]{1,0:T(8,128)(2,1)S(1)}, u32[]{:S(2)}, u32[]{:S(2)}) collective-permute-start(bf16[128,512]{1,0:T(8,128)(2,1)} %row_total.3), channel_id=1, source_target_pairs={{0,192},{16,208},{32,224},{48,240},{1,193},{17,209},{33,225},{49,2... | collective-permute-start | bytes 393224 | tf_op jit(solution)/shard_map/ppermute | solution.py:243
  81.9 2.5 %collective-permute-start.27 = (bf16[128,512]{1,0:T(8,128)(2,1)}, bf16[128,512]{1,0:T(8,128)(2,1)S(1)}, u32[]{:S(2)}, u32[]{:S(2)}) collective-permute-start(bf16[128,512]{1,0:T(8,128)(2,1)} %row_total.3), channel_id=1, source_target_pairs={{0,64},{16,80},{32,96},{48,112},{64,128},{80,144},{96,160},{112,17... | collective-permute-start | bytes 393224 | tf_op jit(solution)/shard_map/ppermute | solution.py:243
  88.4 4.6 %collective-permute-start.20 = (bf16[128,512]{1,0:T(8,128)(2,1)}, bf16[128,512]{1,0:T(8,128)(2,1)S(1)}, u32[]{:S(2)}, u32[]{:S(2)}) collective-permute-start(bf16[128,512]{1,0:T(8,128)(2,1)} %row_total.2), channel_id=1, source_target_pairs={{0,192},{16,208},{32,224},{48,240},{1,193},{17,209},{33,225},{49,2... | collective-permute-start | bytes 393224 | tf_op jit(solution)/shard_map/ppermute | solution.py:243
  94.3 2.5 %collective-permute-start.18 = (bf16[128,512]{1,0:T(8,128)(2,1)}, bf16[128,512]{1,0:T(8,128)(2,1)S(1)}, u32[]{:S(2)}, u32[]{:S(2)}) collective-permute-start(bf16[128,512]{1,0:T(8,128)(2,1)} %row_total.2), channel_id=1, source_target_pairs={{0,64},{16,80},{32,96},{48,112},{64,128},{80,144},{96,160},{112,17... | collective-permute-start | bytes 393224 | tf_op jit(solution)/shard_map/ppermute | solution.py:243
  98.1 2.5 %prefix.3 = (bf16[128,512]{1,0:T(8,128)(2,1)}, bf16[128,512]{1,0:T(8,128)(2,1)}, bf16[128,512]{1,0:T(8,128)(2,1)}, bf16[128,512]{1,0:T(8,128)(2,1)}) custom-call(s32[1]{0:T(128)} %bitcast.section, bf16[128,4096]{1,0:T(8,128)(2,1)} %residual_ref.3, bf16[128,512]{1,0:T(8,128)(2,1)} %copy-done.1, bf16[128,512]{1,0:T(8,128)(2,1)} %copy-done.5, ...), custom_call_target="tpu_custom_call" | custom-call | tf_op jit(solution)/shard_map/prefix/pallas_call | solution.py:191
  103.7 2.6 %collective-permute-start.32 = (bf16[128,512]{1,0:T(8,128)(2,1)}, bf16[128,512]{1,0:T(8,128)(2,1)S(1)}, u32[]{:S(2)}, u32[]{:S(2)}) collective-permute-start(bf16[128,512]{1,0:T(8,128)(2,1)} %get-tuple-element.36), channel_id=1, source_target_pairs={{0,48},{16,0},{32,16},{48,32},{64,112},{80,64},{96,80},{112,96},{1... | collective-permute-start | bytes 393224 | tf_op jit(solution)/shard_map/ppermute | solution.py:231
  107.6 2.5 %prefix.2 = (bf16[128,512]{1,0:T(8,128)(2,1)}, bf16[128,512]{1,0:T(8,128)(2,1)}, bf16[128,512]{1,0:T(8,128)(2,1)}, bf16[128,512]{1,0:T(8,128)(2,1)}) custom-call(s32[1]{0:T(128)} %bitcast.section, bf16[128,4096]{1,0:T(8,128)(2,1)} %residual_ref.3, bf16[128,512]{1,0:T(8,128)(2,1)} %copy-done, bf16[128,512]{1,0:T(8,128)(2,1)} %copy-done.6, ...), custom_call_target="tpu_custom_call" | custom-call | tf_op jit(solution)/shard_map/prefix/pallas_call | solution.py:191
  110.2 3.3 %collective-permute-start.22 = (bf16[128,512]{1,0:T(8,128)(2,1)}, bf16[128,512]{1,0:T(8,128)(2,1)S(1)}, u32[]{:S(2)}, u32[]{:S(2)}) collective-permute-start(bf16[128,512]{1,0:T(8,128)(2,1)} %get-tuple-element.27), channel_id=1, source_target_pairs={{0,32},{16,48},{32,0},{48,16},{64,96},{80,112},{96,64},{112,80},{1... | collective-permute-start | bytes 393224 | tf_op jit(solution)/shard_map/ppermute | solution.py:231
  113.5 3.5 %collective-permute-start.23 = (bf16[128,512]{1,0:T(8,128)(2,1)}, bf16[128,512]{1,0:T(8,128)(2,1)S(1)}, u32[]{:S(2)}, u32[]{:S(2)}) collective-permute-start(bf16[128,512]{1,0:T(8,128)(2,1)} %get-tuple-element.28), channel_id=1, source_target_pairs={{0,48},{16,0},{32,16},{48,32},{64,112},{80,64},{96,80},{112,96},{1... | collective-permute-start | bytes 393224 | tf_op jit(solution)/shard_map/ppermute | solution.py:231
  119.3 5.1 %collective-permute-done.22.refs_2_ = bf16[128,512]{1,0:T(8,128)(2,1)S(1)} collective-permute-done((bf16[128,512]{1,0:T(8,128)(2,1)}, bf16[128,512]{1,0:T(8,128)(2,1)S(1)}, u32[]{:S(2)}, u32[]{:S(2)}) %collective-permute-start.22) | collective-permute-done | bytes 131104 | tf_op jit(solution)/shard_map/ppermute | solution.py:231
  127.0 2.4 %assemble.1 = bf16[1,128,4096]{2,1,0:T(8,128)(2,1)} custom-call(s32[1]{0:T(128)} %bitcast.section, bf16[128,512]{1,0:T(8,128)(2,1)} %get-tuple-element.25.refs_0_, bf16[128,512]{1,0:T(8,128)(2,1)} %copy-done.20, bf16[128,512]{1,0:T(8,128)(2,1)} %copy-done.21, bf16[128,512]{1,0:T(8,128)(2,1)} %copy-done.22, bf16[128,512]{1,0:T(8,128)(2,1)} %get-tuple-element.33.refs_4_, ...), custom_call_target="tpu_custom_call" | custom-call | tf_op jit(solution)/shard_map/assemble/pallas_call | solution.py:220
  (96 shorter events, 38.0 us)
Async XLA Ops:
  5.1 14.0 %collective-permute-start.2 = (bf16[128,1024]{1,0:T(8,128)(2,1)}, bf16[128,1024]{1,0:T(8,128)(2,1)S(1)}, u32[]{:S(2)}, u32[]{:S(2)}) collective-permute-start(bf16[128,1024]{1,0:T(8,128)(2,1)} %join.1.refs_0_.refs_16_), channel_id=1, source_target_pairs={{0,12},{1,13},{2,14},{3,15},{4,0},{5,1},{6,2},{7,3},{8,4},{9,5},{1... | collective-permute-start | bytes 786440 | tf_op jit(solution)/shard_map/ppermute | solution.py:38
  8.1 15.0 %collective-permute-start = (bf16[128,1024]{1,0:T(8,128)(2,1)}, bf16[128,1024]{1,0:T(8,128)(2,1)S(1)}, u32[]{:S(2)}, u32[]{:S(2)}) collective-permute-start(bf16[128,1024]{1,0:T(8,128)(2,1)} %join.1.refs_0_.refs_16_), channel_id=1, source_target_pairs={{0,4},{1,5},{2,6},{3,7},{4,8},{5,9},{6,10},{7,11},{8,12},{9,13},{1... | collective-permute-start | bytes 786440 | tf_op jit(solution)/shard_map/ppermute | solution.py:38
  9.4 15.4 %collective-permute-start.11 = (bf16[128,1024]{1,0:T(8,128)(2,1)S(1)}, bf16[128,1024]{1,0:T(8,128)(2,1)S(1)}, u32[]{:S(2)}, u32[]{:S(2)}) collective-permute-start(bf16[128,1024]{1,0:T(8,128)(2,1)S(1)} %collective-permute-done.3.refs_4_.refs_20_), channel_id=1, source_target_pairs={{0,1},{1,0},{2,3},{3,2},{4,5},{5,4},{6,7},{7,6},{8,9},{9,8},{10,11... | collective-permute-start | bytes 786440 | tf_op jit(solution)/shard_map/ppermute | solution.py:38
  11.6 18.6 %collective-permute-start.6 = (bf16[128,1024]{1,0:T(8,128)(2,1)S(1)}, bf16[128,1024]{1,0:T(8,128)(2,1)S(1)}, u32[]{:S(2)}, u32[]{:S(2)}) collective-permute-start(bf16[128,1024]{1,0:T(8,128)(2,1)S(1)} %collective-permute-done.3.refs_4_.refs_20_), channel_id=1, source_target_pairs={{0,12},{1,13},{2,14},{3,15},{4,0},{5,1},{6,2},{7,3},{8,4},{9,5},{1... | collective-permute-start | bytes 786440 | tf_op jit(solution)/shard_map/ppermute | solution.py:38
  19.1 12.1 %collective-permute-start.5 = (bf16[128,1024]{1,0:T(8,128)(2,1)S(1)}, bf16[128,1024]{1,0:T(8,128)(2,1)S(1)}, u32[]{:S(2)}, u32[]{:S(2)}) collective-permute-start(bf16[128,1024]{1,0:T(8,128)(2,1)S(1)} %collective-permute-done.3.refs_4_.refs_20_), channel_id=1, source_target_pairs={{0,8},{1,9},{2,10},{3,11},{4,12},{5,13},{6,14},{7,15},{8,0},{9,1},... | collective-permute-start | bytes 786440 | tf_op jit(solution)/shard_map/ppermute | solution.py:38
  19.1 15.3 %collective-permute-start.4 = (bf16[128,1024]{1,0:T(8,128)(2,1)S(1)}, bf16[128,1024]{1,0:T(8,128)(2,1)S(1)}, u32[]{:S(2)}, u32[]{:S(2)}) collective-permute-start(bf16[128,1024]{1,0:T(8,128)(2,1)S(1)} %collective-permute-done.3.refs_4_.refs_20_), channel_id=1, source_target_pairs={{0,4},{1,5},{2,6},{3,7},{4,8},{5,9},{6,10},{7,11},{8,12},{9,13},{1... | collective-permute-start | bytes 786440 | tf_op jit(solution)/shard_map/ppermute | solution.py:38
  23.2 11.8 %collective-permute-start.10 = (bf16[128,1024]{1,0:T(8,128)(2,1)S(1)}, bf16[128,1024]{1,0:T(8,128)(2,1)S(1)}, u32[]{:S(2)}, u32[]{:S(2)}) collective-permute-start(bf16[128,1024]{1,0:T(8,128)(2,1)S(1)} %collective-permute-done.2.refs_3_.refs_19_), channel_id=1, source_target_pairs={{0,1},{1,0},{2,3},{3,2},{4,5},{5,4},{6,7},{7,6},{8,9},{9,8},{10,11... | collective-permute-start | bytes 786440 | tf_op jit(solution)/shard_map/ppermute | solution.py:38
  48.8 21.6 %collective-permute-start.24 = (bf16[128,512]{1,0:T(8,128)(2,1)S(1)}, bf16[128,512]{1,0:T(8,128)(2,1)S(1)}, u32[]{:S(2)}, u32[]{:S(2)}) collective-permute-start(bf16[128,512]{1,0:T(8,128)(2,1)S(1)} %get-tuple-element.30), channel_id=1, source_target_pairs={{0,16},{16,32},{32,48},{48,0},{64,80},{80,96},{96,112},{112,64},{1... | collective-permute-start | bytes 393224 | tf_op jit(solution)/shard_map/ppermute | solution.py:231
  51.8 21.0 %collective-permute-start.25 = (bf16[128,512]{1,0:T(8,128)(2,1)S(1)}, bf16[128,512]{1,0:T(8,128)(2,1)S(1)}, u32[]{:S(2)}, u32[]{:S(2)}) collective-permute-start(bf16[128,512]{1,0:T(8,128)(2,1)S(1)} %get-tuple-element.31), channel_id=1, source_target_pairs={{0,32},{16,48},{32,0},{48,16},{64,96},{80,112},{96,64},{112,80},{1... | collective-permute-start | bytes 393224 | tf_op jit(solution)/shard_map/ppermute | solution.py:231
  56.0 16.8 %collective-permute-start.26 = (bf16[128,512]{1,0:T(8,128)(2,1)S(1)}, bf16[128,512]{1,0:T(8,128)(2,1)S(1)}, u32[]{:S(2)}, u32[]{:S(2)}) collective-permute-start(bf16[128,512]{1,0:T(8,128)(2,1)S(1)} %get-tuple-element.32), channel_id=1, source_target_pairs={{0,48},{16,0},{32,16},{48,32},{64,112},{80,64},{96,80},{112,96},{1... | collective-permute-start | bytes 393224 | tf_op jit(solution)/shard_map/ppermute | solution.py:231
  68.3 13.6 %collective-permute-start.15 = (bf16[128,512]{1,0:T(8,128)(2,1)}, bf16[128,512]{1,0:T(8,128)(2,1)S(1)}, u32[]{:S(2)}, u32[]{:S(2)}) collective-permute-start(bf16[128,512]{1,0:T(8,128)(2,1)} %get-tuple-element.22), channel_id=1, source_target_pairs={{0,16},{16,32},{32,48},{48,0},{64,80},{80,96},{96,112},{112,64},{1... | collective-permute-start | bytes 393224 | tf_op jit(solution)/shard_map/ppermute | solution.py:231
  68.3 16.1 %collective-permute-start.16 = (bf16[128,512]{1,0:T(8,128)(2,1)}, bf16[128,512]{1,0:T(8,128)(2,1)S(1)}, u32[]{:S(2)}, u32[]{:S(2)}) collective-permute-start(bf16[128,512]{1,0:T(8,128)(2,1)} %get-tuple-element.23), channel_id=1, source_target_pairs={{0,32},{16,48},{32,0},{48,16},{64,96},{80,112},{96,64},{112,80},{1... | collective-permute-start | bytes 393224 | tf_op jit(solution)/shard_map/ppermute | solution.py:231
  70.4 15.5 %collective-permute-start.17 = (bf16[128,512]{1,0:T(8,128)(2,1)S(1)}, bf16[128,512]{1,0:T(8,128)(2,1)S(1)}, u32[]{:S(2)}, u32[]{:S(2)}) collective-permute-start(bf16[128,512]{1,0:T(8,128)(2,1)S(1)} %get-tuple-element.24), channel_id=1, source_target_pairs={{0,48},{16,0},{32,16},{48,32},{64,112},{80,64},{96,80},{112,96},{1... | collective-permute-start | bytes 393224 | tf_op jit(solution)/shard_map/ppermute | solution.py:231
  75.9 18.4 %collective-permute-start.29 = (bf16[128,512]{1,0:T(8,128)(2,1)}, bf16[128,512]{1,0:T(8,128)(2,1)S(1)}, u32[]{:S(2)}, u32[]{:S(2)}) collective-permute-start(bf16[128,512]{1,0:T(8,128)(2,1)} %row_total.3), channel_id=1, source_target_pairs={{0,192},{16,208},{32,224},{48,240},{1,193},{17,209},{33,225},{49,2... | collective-permute-start | bytes 393224 | tf_op jit(solution)/shard_map/ppermute | solution.py:243
  80.5 16.3 %collective-permute-start.28 = (bf16[128,512]{1,0:T(8,128)(2,1)}, bf16[128,512]{1,0:T(8,128)(2,1)S(1)}, u32[]{:S(2)}, u32[]{:S(2)}) collective-permute-start(bf16[128,512]{1,0:T(8,128)(2,1)} %row_total.3), channel_id=1, source_target_pairs={{0,128},{16,144},{32,160},{48,176},{64,192},{80,208},{96,224},{112... | collective-permute-start | bytes 393224 | tf_op jit(solution)/shard_map/ppermute | solution.py:243
  81.9 15.0 %collective-permute-start.27 = (bf16[128,512]{1,0:T(8,128)(2,1)}, bf16[128,512]{1,0:T(8,128)(2,1)S(1)}, u32[]{:S(2)}, u32[]{:S(2)}) collective-permute-start(bf16[128,512]{1,0:T(8,128)(2,1)} %row_total.3), channel_id=1, source_target_pairs={{0,64},{16,80},{32,96},{48,112},{64,128},{80,144},{96,160},{112,17... | collective-permute-start | bytes 393224 | tf_op jit(solution)/shard_map/ppermute | solution.py:243
  88.4 15.3 %collective-permute-start.20 = (bf16[128,512]{1,0:T(8,128)(2,1)}, bf16[128,512]{1,0:T(8,128)(2,1)S(1)}, u32[]{:S(2)}, u32[]{:S(2)}) collective-permute-start(bf16[128,512]{1,0:T(8,128)(2,1)} %row_total.2), channel_id=1, source_target_pairs={{0,192},{16,208},{32,224},{48,240},{1,193},{17,209},{33,225},{49,2... | collective-permute-start | bytes 393224 | tf_op jit(solution)/shard_map/ppermute | solution.py:243
  93.0 13.3 %collective-permute-start.19 = (bf16[128,512]{1,0:T(8,128)(2,1)}, bf16[128,512]{1,0:T(8,128)(2,1)S(1)}, u32[]{:S(2)}, u32[]{:S(2)}) collective-permute-start(bf16[128,512]{1,0:T(8,128)(2,1)} %row_total.2), channel_id=1, source_target_pairs={{0,128},{16,144},{32,160},{48,176},{64,192},{80,208},{96,224},{112... | collective-permute-start | bytes 393224 | tf_op jit(solution)/shard_map/ppermute | solution.py:243
  94.3 12.0 %collective-permute-start.18 = (bf16[128,512]{1,0:T(8,128)(2,1)}, bf16[128,512]{1,0:T(8,128)(2,1)S(1)}, u32[]{:S(2)}, u32[]{:S(2)}) collective-permute-start(bf16[128,512]{1,0:T(8,128)(2,1)} %row_total.2), channel_id=1, source_target_pairs={{0,64},{16,80},{32,96},{48,112},{64,128},{80,144},{96,160},{112,17... | collective-permute-start | bytes 393224 | tf_op jit(solution)/shard_map/ppermute | solution.py:243
  100.7 12.9 %collective-permute-start.30 = (bf16[128,512]{1,0:T(8,128)(2,1)}, bf16[128,512]{1,0:T(8,128)(2,1)S(1)}, u32[]{:S(2)}, u32[]{:S(2)}) collective-permute-start(bf16[128,512]{1,0:T(8,128)(2,1)} %get-tuple-element.34), channel_id=1, source_target_pairs={{0,16},{16,32},{32,48},{48,0},{64,80},{80,96},{96,112},{112,64},{1... | collective-permute-start | bytes 393224 | tf_op jit(solution)/shard_map/ppermute | solution.py:231
  101.5 15.6 %collective-permute-start.31 = (bf16[128,512]{1,0:T(8,128)(2,1)}, bf16[128,512]{1,0:T(8,128)(2,1)S(1)}, u32[]{:S(2)}, u32[]{:S(2)}) collective-permute-start(bf16[128,512]{1,0:T(8,128)(2,1)} %get-tuple-element.35), channel_id=1, source_target_pairs={{0,32},{16,48},{32,0},{48,16},{64,96},{80,112},{96,64},{112,80},{1... | collective-permute-start | bytes 393224 | tf_op jit(solution)/shard_map/ppermute | solution.py:231
  103.7 13.4 %collective-permute-start.32 = (bf16[128,512]{1,0:T(8,128)(2,1)}, bf16[128,512]{1,0:T(8,128)(2,1)S(1)}, u32[]{:S(2)}, u32[]{:S(2)}) collective-permute-start(bf16[128,512]{1,0:T(8,128)(2,1)} %get-tuple-element.36), channel_id=1, source_target_pairs={{0,48},{16,0},{32,16},{48,32},{64,112},{80,64},{96,80},{112,96},{1... | collective-permute-start | bytes 393224 | tf_op jit(solution)/shard_map/ppermute | solution.py:231
  110.2 14.2 %collective-permute-start.22 = (bf16[128,512]{1,0:T(8,128)(2,1)}, bf16[128,512]{1,0:T(8,128)(2,1)S(1)}, u32[]{:S(2)}, u32[]{:S(2)}) collective-permute-start(bf16[128,512]{1,0:T(8,128)(2,1)} %get-tuple-element.27), channel_id=1, source_target_pairs={{0,32},{16,48},{32,0},{48,16},{64,96},{80,112},{96,64},{112,80},{1... | collective-permute-start | bytes 393224 | tf_op jit(solution)/shard_map/ppermute | solution.py:231
  113.5 12.8 %collective-permute-start.23 = (bf16[128,512]{1,0:T(8,128)(2,1)}, bf16[128,512]{1,0:T(8,128)(2,1)S(1)}, u32[]{:S(2)}, u32[]{:S(2)}) collective-permute-start(bf16[128,512]{1,0:T(8,128)(2,1)} %get-tuple-element.28), channel_id=1, source_target_pairs={{0,48},{16,0},{32,16},{48,32},{64,112},{80,64},{96,80},{112,96},{1... | collective-permute-start | bytes 393224 | tf_op jit(solution)/shard_map/ppermute | solution.py:231
  (32 other events, 120.9 us)

commit v3 on v0

v3 whole, which is shorter than its diff:
```python
import functools
import math

import jax
import jax.numpy as jnp
from jax import lax
from jax.experimental import pallas as pl
from jax.experimental.pallas import tpu as pltpu
from jax.sharding import PartitionSpec as P

KEY_VALUE_HEADS = 4
GROUP = 8
HEAD_SIZE = 128
TOK = 128
SPANS = 16
TRACE = SPANS * TOK
WIDTH = KEY_VALUE_HEADS * HEAD_SIZE
LAYERS = 16
EXP2_SCALE = math.log2(math.e) / math.sqrt(HEAD_SIZE)
HIDDEN = -1e30
VMEM_LIMIT = 40 * 2**20
CHUNKS = 2
PART = KEY_VALUE_HEADS // CHUNKS

UNITS = [(dx, dz, dc) for dc in range(2) for dz in range(2) for dx in range(4)]


def ctx_pairs(dx, dz, dc):
    pairs = []
    for i in range(SPANS):
        x, z, c = i // 4, i // 2 % 2, i % 2
        pairs.append((i, (x + dx) % 4 * 4 + (z ^ dz) * 2 + (c ^ dc)))
    return pairs


def ctx_move(unit, dx, dz, dc):
    return lax.ppermute(unit, "ctx", ctx_pairs(dx, dz, dc))


def join_kernel(k_ref, v_ref, o_ref, sems):
    copies = [
        pltpu.make_async_copy(k_ref.at[0], o_ref.at[:, :WIDTH], sems.at[0]),
        pltpu.make_async_copy(v_ref.at[0], o_ref.at[:, WIDTH:], sems.at[1]),
    ]
    for copy in copies:
        copy.start()
    for copy in copies:
        copy.wait()


def join(keys, values):
    return pl.pallas_call(
        join_kernel,
        in_specs=[pl.BlockSpec(memory_space=pltpu.HBM)] * 2,
        out_specs=pl.BlockSpec(memory_space=pltpu.VMEM),
        out_shape=jax.ShapeDtypeStruct((TOK, 2 * WIDTH), jnp.bfloat16),
        scratch_shapes=[pltpu.SemaphoreType.DMA((2,))],
        name="join",
    )(keys, values)


def gather(keys, values):
    held = {(0, 0, 0): join(keys, values)}
    for dx, dz, source in (
        (0, 1, (0, 0, 0)),
        (1, 0, (0, 0, 0)),
        (3, 0, (0, 0, 0)),
        (0, 1, (1, 0, 0)),
        (1, 0, (1, 0, 0)),
        (3, 0, (0, 1, 0)),
        (0, 1, (2, 0, 0)),
    ):
        target = ((source[0] + dx) % 4, source[1] ^ dz, 0)
        held[target] = ctx_move(held[source], dx, dz, 0)
    for dz in range(2):
        for dx in range(4):
            held[dx, dz, 1] = ctx_move(held[dx, dz, 0], 0, 0, 1)
    return [held[unit] for unit in UNITS]


def attention_kernel(base, span_map, ctx, q_hbm, *refs):
    units, o_ref = refs[:SPANS], refs[SPANS]
    q_ref, keys, vals, eye, sems = refs[SPANS + 1 :]
    head_columns = pl.ds(base * GROUP * HEAD_SIZE, PART * GROUP * HEAD_SIZE)
    copies = [[pltpu.make_async_copy(q_hbm.at[:, head_columns], q_ref, sems.at[PART, 0])]]
    for part in range(PART):
        group = []
        for block in range(SPANS):
            for side, held in enumerate((keys, vals)):
                first = side * WIDTH + (base + part) * HEAD_SIZE
                group.append(
                    pltpu.make_async_copy(
                        units[block].at[:, pl.ds(first, HEAD_SIZE)],
                        held.at[part, pl.ds(block * TOK, TOK), pl.ds(0, HEAD_SIZE)],
                        sems.at[part, 2 * block + side],
                    )
                )
        copies.append(group)
    for group in copies:
        for copy in group:
            copy.start()

    key_row = lax.broadcasted_iota(jnp.int32, (TOK, TOK), 0)
    query_row = lax.broadcasted_iota(jnp.int32, (TOK, TOK), 1)
    eye[...] = jnp.where(key_row == query_row, 1.0, 0.0).astype(jnp.bfloat16)
    me = ctx[0]
    my_span = span_map[me]
    x, z, c = me // 4, me // 2 % 2, me % 2
    for block, (dx, dz, dc) in enumerate(UNITS):
        source = (x + 4 - dx) % 4 * 4 + (z + dz) % 2 * 2 + (c + dc) % 2
        ahead = (span_map[source] - my_span) * TOK + key_row - query_row
        mask = jnp.where(ahead > 0, HIDDEN, 0.0).astype(jnp.bfloat16)
        for part in range(PART):
            keys[part, block * TOK : (block + 1) * TOK, HEAD_SIZE:] = mask
    for part in range(PART):
        vals[part, :, HEAD_SIZE:] = jnp.ones((TRACE, HEAD_SIZE), jnp.bfloat16)

    copies[0][0].wait()
    one_hot = eye[...]
    for part in range(PART):
        for copy in copies[1 + part]:
            copy.wait()
        for head in range(part * GROUP, (part + 1) * GROUP, 2):
            q = q_ref[:, head * HEAD_SIZE : (head + 2) * HEAD_SIZE]
            q = jnp.concatenate(
                [
                    jnp.concatenate([q[:, :HEAD_SIZE], one_hot], axis=1),
                    jnp.concatenate([q[:, HEAD_SIZE:], one_hot], axis=1),
                ],
                axis=0,
            )
            scores = lax.dot_general(
                q, keys[part], (((1,), (1,)), ((), ())), preferred_element_type=jnp.float32
            )
            peak = jnp.max(scores, axis=1, keepdims=True)
            weights = jnp.exp2((scores - peak) * EXP2_SCALE).astype(jnp.bfloat16)
            mixed = jnp.dot(weights, vals[part], preferred_element_type=jnp.float32)
            result = (mixed[:, :HEAD_SIZE] / mixed[:, HEAD_SIZE:]).astype(jnp.bfloat16)
            o_ref[head] = result[:TOK]
            o_ref[head + 1] = result[TOK:]


def attention(span_map, ctx, queries, units, chunk):
    smem = pl.BlockSpec(memory_space=pltpu.SMEM)
    return pl.pallas_call(
        functools.partial(attention_kernel, chunk * PART),
        in_specs=[smem, smem, pl.BlockSpec(memory_space=pltpu.HBM)]
        + [pl.BlockSpec(memory_space=pltpu.HBM)] * SPANS,
        out_specs=pl.BlockSpec(memory_space=pltpu.VMEM),
        out_shape=jax.ShapeDtypeStruct((LAYERS, TOK, HEAD_SIZE), jnp.bfloat16),
        scratch_shapes=[
            pltpu.VMEM((TOK, PART * GROUP * HEAD_SIZE), jnp.bfloat16),
            pltpu.VMEM((PART, TRACE, 2 * HEAD_SIZE), jnp.bfloat16),
            pltpu.VMEM((PART, TRACE, 2 * HEAD_SIZE), jnp.bfloat16),
            pltpu.VMEM((TOK, TOK), jnp.bfloat16),
            pltpu.SemaphoreType.DMA((PART + 1, 2 * SPANS)),
        ],
        compiler_params=pltpu.CompilerParams(vmem_limit_bytes=VMEM_LIMIT),
        cost_estimate=pl.CostEstimate(
            flops=PART * GROUP * TOK * TRACE * 2 * HEAD_SIZE * 2 * 2,
            bytes_accessed=PART * (TRACE + GROUP * TOK) * 2 * HEAD_SIZE * 2,
            transcendentals=PART * GROUP * TOK * TRACE,
        ),
        name="attention",
    )(span_map, ctx, pltpu.with_memory_space_constraint(queries, pltpu.HBM), *[pltpu.with_memory_space_constraint(u, pltpu.HBM) for u in units])


def prefix_kernel(chunk, section, residual_hbm, x_ref, o_ref, first, sem):
    column = pl.multiple_of((chunk * LAYERS + section[0]) * HEAD_SIZE, HEAD_SIZE)
    copy = pltpu.make_async_copy(residual_hbm.at[:, pl.ds(column, HEAD_SIZE)], first, sem)
    copy.start()
    copy.wait()
    state = first[...].astype(jnp.float32)
    for layer in range(LAYERS):
        state = state + x_ref[layer].astype(jnp.float32)
        o_ref[layer] = state.astype(jnp.bfloat16)


def prefix(section, residual, layers, chunk):
    whole = pl.BlockSpec(memory_space=pltpu.VMEM)
    return pl.pallas_call(
        functools.partial(prefix_kernel, chunk),
        in_specs=[
            pl.BlockSpec(memory_space=pltpu.SMEM),
            pl.BlockSpec(memory_space=pltpu.HBM),
            whole,
        ],
        out_specs=whole,
        out_shape=jax.ShapeDtypeStruct((LAYERS, TOK, HEAD_SIZE), jnp.bfloat16),
        scratch_shapes=[pltpu.VMEM((TOK, HEAD_SIZE), jnp.bfloat16), pltpu.SemaphoreType.DMA(())],
        name="prefix",
    )(section, residual, layers)


def assemble_kernel(*refs):
    slabs, o_ref, sems = refs[:CHUNKS], refs[CHUNKS], refs[CHUNKS + 1]
    copies = []
    for chunk in range(CHUNKS):
        for slab in range(LAYERS):
            head = chunk * LAYERS + slab
            copies.append(
                pltpu.make_async_copy(
                    slabs[chunk].at[slab],
                    o_ref.at[0, :, pl.ds(head * HEAD_SIZE, HEAD_SIZE)],
                    sems.at[head],
                )
            )
    for copy in copies:
        copy.start()
    for copy in copies:
        copy.wait()


def assemble(slabs):
    heads = KEY_VALUE_HEADS * GROUP
    return pl.pallas_call(
        assemble_kernel,
        in_specs=[pl.BlockSpec(memory_space=pl.ANY)] * CHUNKS,
        out_specs=pl.BlockSpec(memory_space=pltpu.HBM),
        out_shape=jax.ShapeDtypeStruct((1, TOK, heads * HEAD_SIZE), jnp.bfloat16),
        scratch_shapes=[pltpu.SemaphoreType.DMA((heads,))],
        name="assemble",
    )(*slabs)


def body(queries, keys, values, residual, span_map):
    ctx = lax.axis_index("ctx")[None]
    section = lax.axis_index("section")[None]
    units = gather(keys, values)
    finished = []
    for chunk in range(CHUNKS):
        by_head = attention(span_map, ctx, queries[0], units, chunk)
        by_layer = lax.all_to_all(by_head, "section", 0, 0, tiled=True)
        summed = prefix(section, residual, by_layer, chunk)
        finished.append(lax.all_to_all(summed, "section", 0, 0, tiled=True))
    return assemble(finished)


def solution(mesh):
    placed = (
        P("section", "ctx", None),
        P("section", "ctx", None),
        P("section", "ctx", None),
        P("ctx", None),
        P(),
    )
    return jax.shard_map(
        body, mesh=mesh, in_specs=placed, out_specs=P("section", "ctx", None), check_vma=False
    )
```

time: 346 us -> 170 us (0.49)
  the two profiles are of different devices: /device:TPU:217 before, /device:TPU:1 now
where the time goes in v3:
time: 170 us; the launch traced here: 169 us
  Pallas kernels  60.3 us (35%)
  starting transfers between devices  43.6 us (26%)
  waiting for transfers between devices  42 us (25%)
  blocking collectives  20.7 us (12%)
  local copies, waits for them, and re-layouts  2.19 us (1%)
    pallas_call x1, Pallas kernels, assemble(): pl.pallas_call(assemble_kernel, in_specs=[pl.BlockSpec(memory_space=pl.AN...  33.1 us
    ppermute x15, starting transfers between devices, ctx_move(): return lax.ppermute(unit, 'ctx', ctx_pairs(dx, dz, dc))  23.3 us
    all_to_all x1, blocking collectives, body(): finished.append(lax.all_to_all(summed, 'section', 0, 0, tiled=True))  20.7 us
    all_to_all x2, waiting for transfers between devices, body(): by_layer = lax.all_to_all(by_head, 'section', 0, 0, tiled=True)  20.4 us
    pallas_call x2, Pallas kernels, attention(): pl.pallas_call(functools.partial(attention_kernel, chunk * PART), in_spec...  20.1 us
    all_to_all x2, starting transfers between devices, body(): by_layer = lax.all_to_all(by_head, 'section', 0, 0, tiled=True)  15.3 us
    all_to_all x1, waiting for transfers between devices, body(): finished.append(lax.all_to_all(summed, 'section', 0, 0, tiled=True))  14.9 us
    ppermute x15, waiting for transfers between devices, ctx_move(): return lax.ppermute(unit, 'ctx', ctx_pairs(dx, dz, dc))  6.83 us
  transfers between devices with their start and end apart: 18, of which 7 were waited for; matrix products, arithmetic and copies ran while one was open for 0% of the time, Pallas kernels for 9%

profile of v3, /device:TPU:1, one launch (start us, length us, event | category | flops | bytes accessed | tf_op | source)
XLA Modules:
  0.0 169.2 jit_solution(10694948672772680376)
XLA Ops:
  0.0 1.7 join.1.refs_0_
  1.7 2.1 %collective-permute-start = (bf16[128,1024]{1,0:T(8,128)(2,1)}, bf16[128,1024]{1,0:T(8,128)(2,1)S(1)}, u32[]{:S(2)}, u32[]{:S(2)}) collective-permute-start(bf16[128,1024]{1,0:T(8,128)(2,1)} %join.1.refs_0_), channel_id=1, source_target_pairs={{0,4},{1,5},{2,6},{3,7},{4,8},{5,9},{6,10},{7,11},{8,12},{9,13},{1... | collective-permute-start | bytes 786440 | tf_op jit(solution)/shard_map/ppermute | solution.py:37
  3.8 1.6 collective-permute-start.3
  5.4 1.5 collective-permute-start.2
  6.9 1.5 collective-permute-start.7
  9.0 1.9 %collective-permute-start.1 = (bf16[128,1024]{1,0:T(8,128)(2,1)S(1)}, bf16[128,1024]{1,0:T(8,128)(2,1)S(1)}, u32[]{:S(2)}, u32[]{:S(2)}) collective-permute-start(bf16[128,1024]{1,0:T(8,128)(2,1)S(1)} %collective-permute-done.refs_1_), channel_id=1, source_target_pairs={{0,4},{1,5},{2,6},{3,7},{4,8},{5,9},{6,10},{7,11},{8,12},{9,13},{1... | collective-permute-start | bytes 786440 | tf_op jit(solution)/shard_map/ppermute | solution.py:37
  10.9 2.1 %collective-permute-start.11 = (bf16[128,1024]{1,0:T(8,128)(2,1)S(1)}, bf16[128,1024]{1,0:T(8,128)(2,1)S(1)}, u32[]{:S(2)}, u32[]{:S(2)}) collective-permute-start(bf16[128,1024]{1,0:T(8,128)(2,1)S(1)} %collective-permute-done.3.refs_4_), channel_id=1, source_target_pairs={{0,1},{1,0},{2,3},{3,2},{4,5},{5,4},{6,7},{7,6},{8,9},{9,8},{10,11... | collective-permute-start | bytes 786440 | tf_op jit(solution)/shard_map/ppermute | solution.py:37
  13.0 2.8 %collective-permute-start.6 = (bf16[128,1024]{1,0:T(8,128)(2,1)S(1)}, bf16[128,1024]{1,0:T(8,128)(2,1)S(1)}, u32[]{:S(2)}, u32[]{:S(2)}) collective-permute-start(bf16[128,1024]{1,0:T(8,128)(2,1)S(1)} %collective-permute-done.3.refs_4_), channel_id=1, source_target_pairs={{0,12},{1,13},{2,14},{3,15},{4,0},{5,1},{6,2},{7,3},{8,4},{9,5},{1... | collective-permute-start | bytes 786440 | tf_op jit(solution)/shard_map/ppermute | solution.py:37
  16.1 1.6 collective-permute-start.4
  17.7 2.6 %collective-permute-start.5 = (bf16[128,1024]{1,0:T(8,128)(2,1)S(1)}, bf16[128,1024]{1,0:T(8,128)(2,1)S(1)}, u32[]{:S(2)}, u32[]{:S(2)}) collective-permute-start(bf16[128,1024]{1,0:T(8,128)(2,1)S(1)} %collective-permute-done.1.refs_2_), channel_id=1, source_target_pairs={{0,2},{1,3},{2,0},{3,1},{4,6},{5,7},{6,4},{7,5},{8,10},{9,11},{10,... | collective-permute-start | bytes 786440 | tf_op jit(solution)/shard_map/ppermute | solution.py:37
  20.3 2.7 %collective-permute-start.8 = (bf16[128,1024]{1,0:T(8,128)(2,1)S(1)}, bf16[128,1024]{1,0:T(8,128)(2,1)S(1)}, u32[]{:S(2)}, u32[]{:S(2)}) collective-permute-start(bf16[128,1024]{1,0:T(8,128)(2,1)S(1)} %collective-permute-done.refs_1_), channel_id=1, source_target_pairs={{0,1},{1,0},{2,3},{3,2},{4,5},{5,4},{6,7},{7,6},{8,9},{9,8},{10,11... | collective-permute-start | bytes 786440 | tf_op jit(solution)/shard_map/ppermute | solution.py:37
  25.4 4.3 %collective-permute-done.5.refs_6_ = bf16[128,1024]{1,0:T(8,128)(2,1)S(1)} collective-permute-done((bf16[128,1024]{1,0:T(8,128)(2,1)S(1)}, bf16[128,1024]{1,0:T(8,128)(2,1)S(1)}, u32[]{:S(2)}, u32[]{:S(2)}) %collective-permute-start.5) | collective-permute-done | bytes 262176 | tf_op jit(solution)/shard_map/ppermute | solution.py:37
  32.5 10.0 %attention.2 = bf16[16,128,128]{2,1,0:T(8,128)(2,1)} custom-call(s32[16]{0:T(128)S(1)} %copy-done, s32[1]{0:T(128)} %bitcast.1.ctx, bf16[128,4096]{1,0:T(8,128)(2,1)} %bitcast.3, bf16[128,1024]{1,0:T(8,128)(2,1)} %join.1.refs_0_, bf16[128,1024]{1,0:T(8,128)(2,1)} %copy-done.4, bf16[128,1024]{1,0:T(8,128)(2,1)} %copy-done.8, bf16[128,1024]{1,0:T(8,128)(2,1)} %copy-done.6, ...), custom_call_target="tpu_custom_call" | custom-call | flops 4294967296 | bytes 3145728 | tf_op jit(solution)/shard_map/attention/pallas_call | solution.py:145
  42.5 10.8 %all-to-all-start = ((bf16[16,128,128]{2,1,0:T(8,128)(2,1)}), bf16[16,128,128]{2,1,0:T(8,128)(2,1)S(1)}, u32[]{:S(2)}, u32[]{:S(2)}) async-start(bf16[16,128,128]{2,1,0:T(8,128)(2,1)} %attention.2), calls=%async_computation | async-start | bytes 1048576 | tf_op jit(solution)/shard_map/all_to_all | solution.py:233
  53.3 10.1 %attention.3 = bf16[16,128,128]{2,1,0:T(8,128)(2,1)} custom-call(s32[16]{0:T(128)S(1)} %copy-done, s32[1]{0:T(128)} %bitcast.1.ctx, bf16[128,4096]{1,0:T(8,128)(2,1)} %bitcast.4, bf16[128,1024]{1,0:T(8,128)(2,1)} %join.1.refs_0_, bf16[128,1024]{1,0:T(8,128)(2,1)} %copy-done.4, bf16[128,1024]{1,0:T(8,128)(2,1)} %copy-done.8, bf16[128,1024]{1,0:T(8,128)(2,1)} %copy-done.6, ...), custom_call_target="tpu_custom_call" | custom-call | flops 4294967296 | bytes 3145728 | tf_op jit(solution)/shard_map/attention/pallas_call | solution.py:145
  63.4 6.8 %all-to-all-done.x_ref = bf16[16,128,128]{2,1,0:T(8,128)(2,1)S(1)} async-done(((bf16[16,128,128]{2,1,0:T(8,128)(2,1)}), bf16[16,128,128]{2,1,0:T(8,128)(2,1)S(1)}, u32[]{:S(2)}, u32[]{:S(2)}) %all-to-all-start) | async-done | bytes 524320 | tf_op jit(solution)/shard_map/all_to_all | solution.py:233
  71.0 4.6 %all-to-all-start.2 = ((bf16[16,128,128]{2,1,0:T(8,128)(2,1)}), bf16[16,128,128]{2,1,0:T(8,128)(2,1)S(1)}, u32[]{:S(2)}, u32[]{:S(2)}) async-start(bf16[16,128,128]{2,1,0:T(8,128)(2,1)} %attention.3), calls=%async_computation.2 | async-start | bytes 1048576 | tf_op jit(solution)/shard_map/all_to_all | solution.py:233
  75.6 2.7 %prefix.2 = bf16[16,128,128]{2,1,0:T(8,128)(2,1)} custom-call(s32[1]{0:T(128)} %bitcast.section, bf16[128,4096]{1,0:T(8,128)(2,1)} %residual_hbm.3, bf16[16,128,128]{2,1,0:T(8,128)(2,1)} %copy-done.1), custom_call_target="tpu_custom_call" | custom-call | tf_op jit(solution)/shard_map/prefix/pallas_call | solution.py:181
  78.3 13.6 %all-to-all-done.2.x_ref = bf16[16,128,128]{2,1,0:T(8,128)(2,1)S(1)} async-done(((bf16[16,128,128]{2,1,0:T(8,128)(2,1)}), bf16[16,128,128]{2,1,0:T(8,128)(2,1)S(1)}, u32[]{:S(2)}, u32[]{:S(2)}) %all-to-all-start.2) | async-done | bytes 524320 | tf_op jit(solution)/shard_map/all_to_all | solution.py:233
  92.7 5.0 %all-to-all-start.1 = ((bf16[16,128,128]{2,1,0:T(8,128)(2,1)}), bf16[16,128,128]{2,1,0:T(8,128)(2,1)S(1)}, u32[]{:S(2)}, u32[]{:S(2)}) async-start(bf16[16,128,128]{2,1,0:T(8,128)(2,1)} %prefix.2), calls=%async_computation.1 | async-start | bytes 1048576 | tf_op jit(solution)/shard_map/all_to_all | solution.py:235
  97.6 2.7 %prefix.3 = bf16[16,128,128]{2,1,0:T(8,128)(2,1)} custom-call(s32[1]{0:T(128)} %bitcast.section, bf16[128,4096]{1,0:T(8,128)(2,1)} %residual_hbm.3, bf16[16,128,128]{2,1,0:T(8,128)(2,1)} %copy-done.2), custom_call_target="tpu_custom_call" | custom-call | tf_op jit(solution)/shard_map/prefix/pallas_call | solution.py:181
  100.3 14.9 %all-to-all-done.1.refs_0_ = bf16[16,128,128]{2,1,0:T(8,128)(2,1)S(1)} async-done(((bf16[16,128,128]{2,1,0:T(8,128)(2,1)}), bf16[16,128,128]{2,1,0:T(8,128)(2,1)S(1)}, u32[]{:S(2)}, u32[]{:S(2)}) %all-to-all-start.1) | async-done | bytes 524320 | tf_op jit(solution)/shard_map/all_to_all | solution.py:235
  115.2 20.7 %all_to_all.20.refs_1_ = bf16[16,128,128]{2,1,0:T(8,128)(2,1)} all-to-all(bf16[16,128,128]{2,1,0:T(8,128)(2,1)} %prefix.3), channel_id=1, replica_groups=mesh['section'=16,'ctx'=16] {'section'}, dimensions={0} | all-to-all | bytes 1048576 | tf_op jit(solution)/shard_map/all_to_all | solution.py:235
  135.9 33.1 %assemble.1 = bf16[1,128,4096]{2,1,0:T(8,128)(2,1)} custom-call(bf16[16,128,128]{2,1,0:T(8,128)(2,1)} %copy-done.3, bf16[16,128,128]{2,1,0:T(8,128)(2,1)} %all_to_all.20.refs_1_), custom_call_target="tpu_custom_call" | custom-call | tf_op jit(solution)/shard_map/assemble/pallas_call | solution.py:216
  (51 shorter events, 7.6 us)
Async XLA Ops:
  1.7 7.4 %collective-permute-start = (bf16[128,1024]{1,0:T(8,128)(2,1)}, bf16[128,1024]{1,0:T(8,128)(2,1)S(1)}, u32[]{:S(2)}, u32[]{:S(2)}) collective-permute-start(bf16[128,1024]{1,0:T(8,128)(2,1)} %join.1.refs_0_), channel_id=1, source_target_pairs={{0,4},{1,5},{2,6},{3,7},{4,8},{5,9},{6,10},{7,11},{8,12},{9,13},{1... | collective-permute-start | bytes 786440 | tf_op jit(solution)/shard_map/ppermute | solution.py:37
  3.8 7.1 %collective-permute-start.3 = (bf16[128,1024]{1,0:T(8,128)(2,1)}, bf16[128,1024]{1,0:T(8,128)(2,1)S(1)}, u32[]{:S(2)}, u32[]{:S(2)}) collective-permute-start(bf16[128,1024]{1,0:T(8,128)(2,1)} %join.1.refs_0_), channel_id=1, source_target_pairs={{0,2},{1,3},{2,0},{3,1},{4,6},{5,7},{6,4},{7,5},{8,10},{9,11},{10,... | collective-permute-start | bytes 786440 | tf_op jit(solution)/shard_map/ppermute | solution.py:37
  5.4 10.3 %collective-permute-start.2 = (bf16[128,1024]{1,0:T(8,128)(2,1)}, bf16[128,1024]{1,0:T(8,128)(2,1)S(1)}, u32[]{:S(2)}, u32[]{:S(2)}) collective-permute-start(bf16[128,1024]{1,0:T(8,128)(2,1)} %join.1.refs_0_), channel_id=1, source_target_pairs={{0,12},{1,13},{2,14},{3,15},{4,0},{5,1},{6,2},{7,3},{8,4},{9,5},{1... | collective-permute-start | bytes 786440 | tf_op jit(solution)/shard_map/ppermute | solution.py:37
  6.9 9.2 %collective-permute-start.7 = (bf16[128,1024]{1,0:T(8,128)(2,1)}, bf16[128,1024]{1,0:T(8,128)(2,1)S(1)}, u32[]{:S(2)}, u32[]{:S(2)}) collective-permute-start(bf16[128,1024]{1,0:T(8,128)(2,1)} %join.1.refs_0_), channel_id=1, source_target_pairs={{0,1},{1,0},{2,3},{3,2},{4,5},{5,4},{6,7},{7,6},{8,9},{9,8},{10,11... | collective-permute-start | bytes 786440 | tf_op jit(solution)/shard_map/ppermute | solution.py:37
  9.0 22.8 %copy-start.4 = (bf16[128,1024]{1,0:T(8,128)(2,1)}, bf16[128,1024]{1,0:T(8,128)(2,1)S(1)}, u32[]{:S(2)}) copy-start(bf16[128,1024]{1,0:T(8,128)(2,1)S(1)} %collective-permute-done.refs_1_) | copy-start | bytes 786436
  9.0 8.7 %collective-permute-start.1 = (bf16[128,1024]{1,0:T(8,128)(2,1)S(1)}, bf16[128,1024]{1,0:T(8,128)(2,1)S(1)}, u32[]{:S(2)}, u32[]{:S(2)}) collective-permute-start(bf16[128,1024]{1,0:T(8,128)(2,1)S(1)} %collective-permute-done.refs_1_), channel_id=1, source_target_pairs={{0,4},{1,5},{2,6},{3,7},{4,8},{5,9},{6,10},{7,11},{8,12},{9,13},{1... | collective-permute-start | bytes 786440 | tf_op jit(solution)/shard_map/ppermute | solution.py:37
  10.9 21.0 %copy-start.5 = (bf16[128,1024]{1,0:T(8,128)(2,1)}, bf16[128,1024]{1,0:T(8,128)(2,1)S(1)}, u32[]{:S(2)}) copy-start(bf16[128,1024]{1,0:T(8,128)(2,1)S(1)} %collective-permute-done.3.refs_4_) | copy-start | bytes 786436
  10.9 9.4 %collective-permute-start.11 = (bf16[128,1024]{1,0:T(8,128)(2,1)S(1)}, bf16[128,1024]{1,0:T(8,128)(2,1)S(1)}, u32[]{:S(2)}, u32[]{:S(2)}) collective-permute-start(bf16[128,1024]{1,0:T(8,128)(2,1)S(1)} %collective-permute-done.3.refs_4_), channel_id=1, source_target_pairs={{0,1},{1,0},{2,3},{3,2},{4,5},{5,4},{6,7},{7,6},{8,9},{9,8},{10,11... | collective-permute-start | bytes 786440 | tf_op jit(solution)/shard_map/ppermute | solution.py:37
  13.0 10.0 %collective-permute-start.6 = (bf16[128,1024]{1,0:T(8,128)(2,1)S(1)}, bf16[128,1024]{1,0:T(8,128)(2,1)S(1)}, u32[]{:S(2)}, u32[]{:S(2)}) collective-permute-start(bf16[128,1024]{1,0:T(8,128)(2,1)S(1)} %collective-permute-done.3.refs_4_), channel_id=1, source_target_pairs={{0,12},{1,13},{2,14},{3,15},{4,0},{5,1},{6,2},{7,3},{8,4},{9,5},{1... | collective-permute-start | bytes 786440 | tf_op jit(solution)/shard_map/ppermute | solution.py:37
  15.8 16.1 %copy-start.6 = (bf16[128,1024]{1,0:T(8,128)(2,1)}, bf16[128,1024]{1,0:T(8,128)(2,1)S(1)}, u32[]{:S(2)}) copy-start(bf16[128,1024]{1,0:T(8,128)(2,1)S(1)} %collective-permute-done.2.refs_3_) | copy-start | bytes 786436
  15.8 7.4 %collective-permute-start.10 = (bf16[128,1024]{1,0:T(8,128)(2,1)S(1)}, bf16[128,1024]{1,0:T(8,128)(2,1)S(1)}, u32[]{:S(2)}, u32[]{:S(2)}) collective-permute-start(bf16[128,1024]{1,0:T(8,128)(2,1)S(1)} %collective-permute-done.2.refs_3_), channel_id=1, source_target_pairs={{0,1},{1,0},{2,3},{3,2},{4,5},{5,4},{6,7},{7,6},{8,9},{9,8},{10,11... | collective-permute-start | bytes 786440 | tf_op jit(solution)/shard_map/ppermute | solution.py:37
  16.1 15.8 %copy-start.7 = (bf16[128,1024]{1,0:T(8,128)(2,1)}, bf16[128,1024]{1,0:T(8,128)(2,1)S(1)}, u32[]{:S(2)}) copy-start(bf16[128,1024]{1,0:T(8,128)(2,1)S(1)} %collective-permute-done.7.refs_8_) | copy-start | bytes 786436
  16.1 8.0 %collective-permute-start.4 = (bf16[128,1024]{1,0:T(8,128)(2,1)S(1)}, bf16[128,1024]{1,0:T(8,128)(2,1)S(1)}, u32[]{:S(2)}, u32[]{:S(2)}) collective-permute-start(bf16[128,1024]{1,0:T(8,128)(2,1)S(1)} %collective-permute-done.refs_1_), channel_id=1, source_target_pairs={{0,2},{1,3},{2,0},{3,1},{4,6},{5,7},{6,4},{7,5},{8,10},{9,11},{10,... | collective-permute-start | bytes 786440 | tf_op jit(solution)/shard_map/ppermute | solution.py:37
  17.7 14.2 %copy-start.8 = (bf16[128,1024]{1,0:T(8,128)(2,1)}, bf16[128,1024]{1,0:T(8,128)(2,1)S(1)}, u32[]{:S(2)}) copy-start(bf16[128,1024]{1,0:T(8,128)(2,1)S(1)} %collective-permute-done.1.refs_2_) | copy-start | bytes 786436
  17.7 12.0 %collective-permute-start.5 = (bf16[128,1024]{1,0:T(8,128)(2,1)S(1)}, bf16[128,1024]{1,0:T(8,128)(2,1)S(1)}, u32[]{:S(2)}, u32[]{:S(2)}) collective-permute-start(bf16[128,1024]{1,0:T(8,128)(2,1)S(1)} %collective-permute-done.1.refs_2_), channel_id=1, source_target_pairs={{0,2},{1,3},{2,0},{3,1},{4,6},{5,7},{6,4},{7,5},{8,10},{9,11},{10,... | collective-permute-start | bytes 786440 | tf_op jit(solution)/shard_map/ppermute | solution.py:37
  20.3 10.3 %collective-permute-start.8 = (bf16[128,1024]{1,0:T(8,128)(2,1)S(1)}, bf16[128,1024]{1,0:T(8,128)(2,1)S(1)}, u32[]{:S(2)}, u32[]{:S(2)}) collective-permute-start(bf16[128,1024]{1,0:T(8,128)(2,1)S(1)} %collective-permute-done.refs_1_), channel_id=1, source_target_pairs={{0,1},{1,0},{2,3},{3,2},{4,5},{5,4},{6,7},{7,6},{8,9},{9,8},{10,11... | collective-permute-start | bytes 786440 | tf_op jit(solution)/shard_map/ppermute | solution.py:37
  23.1 7.6 %collective-permute-start.9 = (bf16[128,1024]{1,0:T(8,128)(2,1)S(1)}, bf16[128,1024]{1,0:T(8,128)(2,1)S(1)}, u32[]{:S(2)}, u32[]{:S(2)}) collective-permute-start(bf16[128,1024]{1,0:T(8,128)(2,1)S(1)} %collective-permute-done.1.refs_2_), channel_id=1, source_target_pairs={{0,1},{1,0},{2,3},{3,2},{4,5},{5,4},{6,7},{7,6},{8,9},{9,8},{10,11... | collective-permute-start | bytes 786440 | tf_op jit(solution)/shard_map/ppermute | solution.py:37
  23.2 7.4 %collective-permute-start.14 = (bf16[128,1024]{1,0:T(8,128)(2,1)S(1)}, bf16[128,1024]{1,0:T(8,128)(2,1)}, u32[]{:S(2)}, u32[]{:S(2)}) collective-permute-start(bf16[128,1024]{1,0:T(8,128)(2,1)S(1)} %collective-permute-done.6.refs_7_), channel_id=1, source_target_pairs={{0,1},{1,0},{2,3},{3,2},{4,5},{5,4},{6,7},{7,6},{8,9},{9,8},{10,11... | collective-permute-start | bytes 786440 | tf_op jit(solution)/shard_map/ppermute | solution.py:37
  24.1 6.5 %collective-permute-start.12 = (bf16[128,1024]{1,0:T(8,128)(2,1)S(1)}, bf16[128,1024]{1,0:T(8,128)(2,1)}, u32[]{:S(2)}, u32[]{:S(2)}) collective-permute-start(bf16[128,1024]{1,0:T(8,128)(2,1)S(1)} %collective-permute-done.4.refs_5_), channel_id=1, source_target_pairs={{0,1},{1,0},{2,3},{3,2},{4,5},{5,4},{6,7},{7,6},{8,9},{9,8},{10,11... | collective-permute-start | bytes 786440 | tf_op jit(solution)/shard_map/ppermute | solution.py:37
  29.8 2.1 %collective-permute-start.13 = (bf16[128,1024]{1,0:T(8,128)(2,1)S(1)}, bf16[128,1024]{1,0:T(8,128)(2,1)}, u32[]{:S(2)}, u32[]{:S(2)}) collective-permute-start(bf16[128,1024]{1,0:T(8,128)(2,1)S(1)} %collective-permute-done.5.refs_6_), channel_id=1, source_target_pairs={{0,1},{1,0},{2,3},{3,2},{4,5},{5,4},{6,7},{7,6},{8,9},{9,8},{10,11... | collective-permute-start | bytes 786440 | tf_op jit(solution)/shard_map/ppermute | solution.py:37
  42.5 27.7 %all-to-all-start = ((bf16[16,128,128]{2,1,0:T(8,128)(2,1)}), bf16[16,128,128]{2,1,0:T(8,128)(2,1)S(1)}, u32[]{:S(2)}, u32[]{:S(2)}) async-start(bf16[16,128,128]{2,1,0:T(8,128)(2,1)} %attention.2), calls=%async_computation | async-start | bytes 1048576 | tf_op jit(solution)/shard_map/all_to_all | solution.py:233
  71.0 20.9 %all-to-all-start.2 = ((bf16[16,128,128]{2,1,0:T(8,128)(2,1)}), bf16[16,128,128]{2,1,0:T(8,128)(2,1)S(1)}, u32[]{:S(2)}, u32[]{:S(2)}) async-start(bf16[16,128,128]{2,1,0:T(8,128)(2,1)} %attention.3), calls=%async_computation.2 | async-start | bytes 1048576 | tf_op jit(solution)/shard_map/all_to_all | solution.py:233
  92.7 22.5 %all-to-all-start.1 = ((bf16[16,128,128]{2,1,0:T(8,128)(2,1)}), bf16[16,128,128]{2,1,0:T(8,128)(2,1)S(1)}, u32[]{:S(2)}, u32[]{:S(2)}) async-start(bf16[16,128,128]{2,1,0:T(8,128)(2,1)} %prefix.2), calls=%async_computation.1 | async-start | bytes 1048576 | tf_op jit(solution)/shard_map/all_to_all | solution.py:235
  115.2 20.7 %copy-start.3 = (bf16[16,128,128]{2,1,0:T(8,128)(2,1)}, bf16[16,128,128]{2,1,0:T(8,128)(2,1)S(1)}, u32[]{:S(2)}) copy-start(bf16[16,128,128]{2,1,0:T(8,128)(2,1)S(1)} %all-to-all-done.1.refs_0_) | copy-start | bytes 1572868
  (10 other events, 44.3 us)

commit v4 on v2

--- a/solution.py
+++ b/solution.py
@@ -19,7 +19,7 @@
 PAIR = 2 * HEAD_SIZE
 EXP2_SCALE = math.log2(math.e) / math.sqrt(HEAD_SIZE)
 HIDDEN = -1e30
-VMEM_LIMIT = 40 * 2**20
+VMEM_LIMIT = 20 * 2**20
 CHUNKS = 2
 PART = KEY_VALUE_HEADS // CHUNKS
 
@@ -46,6 +46,10 @@
     return [(i, i + RING * steps) for i in range(RING * (RING - steps))]
 
 
+def pinned(x):
+    return pltpu.with_memory_space_constraint(x, pltpu.HBM)
+
+
 def join_kernel(k_ref, v_ref, o_ref):
     o_ref[:, :WIDTH] = k_ref[0]
     o_ref[:, WIDTH:] = v_ref[0]
@@ -55,18 +59,24 @@
     return pl.pallas_call(
         join_kernel,
         out_shape=jax.ShapeDtypeStruct((TOK, 2 * WIDTH), jnp.bfloat16),
+        compiler_params=pltpu.CompilerParams(vmem_limit_bytes=2 * 2**20),
         name="join",
     )(keys, values)
 
 
 def gather(keys, values):
-    own = join(keys, values)
-    held = {(0, 0, 0): own}
-    held[0, 1, 0] = ctx_move(own, 0, 1, 0)
-    for dx in (1, 3, 2):
-        held[dx, 0, 0] = ctx_move(own, dx, 0, 0)
-    for dx in (1, 3, 2):
-        held[dx, 1, 0] = ctx_move(held[0, 1, 0], dx, 0, 0)
+    held = {(0, 0, 0): join(keys, values)}
+    for dx, dz, source in (
+        (0, 1, (0, 0, 0)),
+        (1, 0, (0, 0, 0)),
+        (3, 0, (0, 0, 0)),
+        (0, 1, (1, 0, 0)),
+        (1, 0, (1, 0, 0)),
+        (3, 0, (0, 1, 0)),
+        (0, 1, (2, 0, 0)),
+    ):
+        target = ((source[0] + dx) % 4, source[1] ^ dz, 0)
+        held[target] = ctx_move(held[source], dx, dz, 0)
     for dz in range(2):
         for dx in range(4):
             held[dx, dz, 1] = ctx_move(held[dx, dz, 0], 0, 0, 1)
@@ -148,7 +158,9 @@
             transcendentals=PART * GROUP * TOK * TRACE,
         ),
         name="attention",
-    )(span_map, ctx, section, queries, *units, *units)
+    )(
+        pinned(span_map), ctx, section, pinned(queries), *units, *units
+    )
 
 
 def total_kernel(a, b, c, d, o_ref):
@@ -161,7 +173,10 @@
 def row_total(slabs):
     return pl.pallas_call(
         total_kernel,
+        in_specs=[pl.BlockSpec(memory_space=pltpu.VMEM)] * RING,
+        out_specs=pl.BlockSpec(memory_space=pltpu.VMEM),
         out_shape=jax.ShapeDtypeStruct((TOK, PART * PAIR), jnp.bfloat16),
+        compiler_params=pltpu.CompilerParams(vmem_limit_bytes=4 * 2**20),
         name="row_total",
     )(*slabs)
 
@@ -197,6 +212,7 @@
             pltpu.VMEM((RING, TOK, PART * PAIR), jnp.bfloat16),
             pltpu.VMEM((RING, TOK, PART * PAIR), jnp.bfloat16),
         ],
+        compiler_params=pltpu.CompilerParams(vmem_limit_bytes=8 * 2**20),
         name="prefix",
     )(section, residual, *slabs, *below)
 
@@ -222,6 +238,7 @@
         in_specs=[pl.BlockSpec(memory_space=pltpu.SMEM)] + [whole] * len(slabs),
         out_specs=whole,
         out_shape=jax.ShapeDtypeStruct((1, TOK, width), jnp.bfloat16),
+        compiler_params=pltpu.CompilerParams(vmem_limit_bytes=8 * 2**20),
         name="assemble",
     )(section, *slabs)
 

time: 130 us -> 114 us (0.88)
  Pallas kernels: 30.7 us -> 19.3 us
  local copies, waits for them, and re-layouts: 9.23 us -> 1.81 us
  starting transfers between devices: 62.4 us -> 69.1 us
  waiting for transfers between devices: 26.7 us -> 23.5 us
    ppermute x15, waiting for transfers between devices: 15.9 us -> 6.32 us  [ctx_move(): return lax.ppermute(unit, 'ctx', ctx_pairs(dx, dz, dc))]
    unnamed x46 -> x6, local copies, waits for them, and re-layouts: 9.23 us -> 1.81 us
    ppermute x12, waiting for transfers between devices: 10.8 us -> 17.2 us  [turn(): lax.ppermute(slabs[steps], 'section', turn_pairs(steps))]
    pallas_call x2, Pallas kernels: 5.1 us -> 0.48 us  [prefix(): pl.pallas_call(functools.partial(prefix_kernel, chunk), in_specs=[pl.Bloc...]
    ppermute x15, starting transfers between devices: 19 us -> 23.6 us  [ctx_move(): return lax.ppermute(unit, 'ctx', ctx_pairs(dx, dz, dc))]
    pallas_call x2, Pallas kernels: 3.63 us -> 0.14 us  [row_total(): pl.pallas_call(total_kernel, in_specs=[pl.BlockSpec(memory_space=pltpu.VM...]
    pallas_call x1, Pallas kernels: 1.69 us -> 0.02 us  [join(): pl.pallas_call(join_kernel, out_shape=jax.ShapeDtypeStruct((TOK, 2 * WIDT...]
  transfers between devices with their start and end apart: 33 -> 33, of which waited for: 10 -> 8; matrix products, arithmetic and copies ran while one was open for 0% -> 0% of each run, Pallas kernels for 14% -> 8%
where the time goes in v4:
time: 114 us
  starting transfers between devices  69.1 us (61%)
  waiting for transfers between devices  23.5 us (21%)
  Pallas kernels  19.3 us (17%)
  local copies, waits for them, and re-layouts  1.81 us (2%)
    ppermute x12, starting transfers between devices, turn(): lax.ppermute(slabs[steps], 'section', turn_pairs(steps))  27.7 us
    ppermute x15, starting transfers between devices, ctx_move(): return lax.ppermute(unit, 'ctx', ctx_pairs(dx, dz, dc))  23.6 us
    ppermute x6, starting transfers between devices, body(): lax.ppermute(total, 'section', climb_pairs(s))  17.8 us
    pallas_call x2, Pallas kernels, attention(): pl.pallas_call(attention_kernel, grid_spec=pltpu.PrefetchScalarGridSpec(n...  17.6 us
    ppermute x12, waiting for transfers between devices, turn(): lax.ppermute(slabs[steps], 'section', turn_pairs(steps))  17.2 us
    ppermute x15, waiting for transfers between devices, ctx_move(): return lax.ppermute(unit, 'ctx', ctx_pairs(dx, dz, dc))  6.32 us
  transfers between devices with their start and end apart: 33, of which 8 were waited for; matrix products, arithmetic and copies ran while one was open for 0% of the time, Pallas kernels for 8%

profile of v4, /device:TPU:1, one launch (start us, length us, event | category | flops | bytes accessed | tf_op | source)
XLA Modules:
  0.0 113.9 jit_solution(13511631179288510180)
XLA Ops:
  1.8 2.1 %collective-permute-start = (bf16[128,1024]{1,0:T(8,128)(2,1)S(1)}, bf16[128,1024]{1,0:T(8,128)(2,1)S(1)}, u32[]{:S(2)}, u32[]{:S(2)}) collective-permute-start(bf16[128,1024]{1,0:T(8,128)(2,1)S(1)} %join.1.refs_0_.refs_16_), channel_id=1, source_target_pairs={{0,4},{1,5},{2,6},{3,7},{4,8},{5,9},{6,10},{7,11},{8,12},{9,13},{1... | collective-permute-start | bytes 786440 | tf_op jit(solution)/shard_map/ppermute | solution.py:38
  10.8 2.1 %collective-permute-start.11 = (bf16[128,1024]{1,0:T(8,128)(2,1)S(1)}, bf16[128,1024]{1,0:T(8,128)(2,1)S(1)}, u32[]{:S(2)}, u32[]{:S(2)}) collective-permute-start(bf16[128,1024]{1,0:T(8,128)(2,1)S(1)} %collective-permute-done.3.refs_4_.refs_20_), channel_id=1, source_target_pairs={{0,1},{1,0},{2,3},{3,2},{4,5},{5,4},{6,7},{7,6},{8,9},{9,8},{10,11... | collective-permute-start | bytes 786440 | tf_op jit(solution)/shard_map/ppermute | solution.py:38
  13.0 2.7 %collective-permute-start.6 = (bf16[128,1024]{1,0:T(8,128)(2,1)S(1)}, bf16[128,1024]{1,0:T(8,128)(2,1)S(1)}, u32[]{:S(2)}, u32[]{:S(2)}) collective-permute-start(bf16[128,1024]{1,0:T(8,128)(2,1)S(1)} %collective-permute-done.3.refs_4_.refs_20_), channel_id=1, source_target_pairs={{0,12},{1,13},{2,14},{3,15},{4,0},{5,1},{6,2},{7,3},{8,4},{9,5},{1... | collective-permute-start | bytes 786440 | tf_op jit(solution)/shard_map/ppermute | solution.py:38
  17.6 2.7 %collective-permute-start.5 = (bf16[128,1024]{1,0:T(8,128)(2,1)S(1)}, bf16[128,1024]{1,0:T(8,128)(2,1)S(1)}, u32[]{:S(2)}, u32[]{:S(2)}) collective-permute-start(bf16[128,1024]{1,0:T(8,128)(2,1)S(1)} %collective-permute-done.1.refs_2_.refs_18_), channel_id=1, source_target_pairs={{0,2},{1,3},{2,0},{3,1},{4,6},{5,7},{6,4},{7,5},{8,10},{9,11},{10,... | collective-permute-start | bytes 786440 | tf_op jit(solution)/shard_map/ppermute | solution.py:38
  20.2 2.7 %collective-permute-start.8 = (bf16[128,1024]{1,0:T(8,128)(2,1)S(1)}, bf16[128,1024]{1,0:T(8,128)(2,1)S(1)}, u32[]{:S(2)}, u32[]{:S(2)}) collective-permute-start(bf16[128,1024]{1,0:T(8,128)(2,1)S(1)} %collective-permute-done.refs_1_.refs_17_), channel_id=1, source_target_pairs={{0,1},{1,0},{2,3},{3,2},{4,5},{5,4},{6,7},{7,6},{8,9},{9,8},{10,11... | collective-permute-start | bytes 786440 | tf_op jit(solution)/shard_map/ppermute | solution.py:38
  25.3 4.2 %collective-permute-done.5.refs_6_.refs_22_ = bf16[128,1024]{1,0:T(8,128)(2,1)S(1)} collective-permute-done((bf16[128,1024]{1,0:T(8,128)(2,1)S(1)}, bf16[128,1024]{1,0:T(8,128)(2,1)S(1)}, u32[]{:S(2)}, u32[]{:S(2)}) %collective-permute-start.5) | collective-permute-done | bytes 262176 | tf_op jit(solution)/shard_map/ppermute | solution.py:38
  31.7 8.8 %attention.3 = (bf16[128,512]{1,0:T(8,128)(2,1)S(1)}, bf16[128,512]{1,0:T(8,128)(2,1)S(1)}, bf16[128,512]{1,0:T(8,128)(2,1)S(1)}, bf16[128,512]{1,0:T(8,128)(2,1)S(1)}) custom-call(s32[16]{0:T(128)} %span_map.3, s32[1]{0:T(128)} %bitcast.1.ctx, s32[1]{0:T(128)} %bitcast.section, bf16[128,4096]{1,0:T(8,128)(2,1)} %bitcast.3, ...), custom_call_target="tpu_custom_call" | custom-call | flops 4294967296 | bytes 3145728 | tf_op jit(solution)/shard_map/attention/pallas_call | solution.py:137
  40.5 3.1 %collective-permute-start.24 = (bf16[128,512]{1,0:T(8,128)(2,1)S(1)}, bf16[128,512]{1,0:T(8,128)(2,1)S(1)}, u32[]{:S(2)}, u32[]{:S(2)}) collective-permute-start(bf16[128,512]{1,0:T(8,128)(2,1)S(1)} %get-tuple-element.30), channel_id=1, source_target_pairs={{0,16},{16,32},{32,48},{48,0},{64,80},{80,96},{96,112},{112,64},{1... | collective-permute-start | bytes 393224 | tf_op jit(solution)/shard_map/ppermute | solution.py:248
  43.6 4.9 %collective-permute-start.25 = (bf16[128,512]{1,0:T(8,128)(2,1)S(1)}, bf16[128,512]{1,0:T(8,128)(2,1)S(1)}, u32[]{:S(2)}, u32[]{:S(2)}) collective-permute-start(bf16[128,512]{1,0:T(8,128)(2,1)S(1)} %get-tuple-element.31), channel_id=1, source_target_pairs={{0,32},{16,48},{32,0},{48,16},{64,96},{80,112},{96,64},{112,80},{1... | collective-permute-start | bytes 393224 | tf_op jit(solution)/shard_map/ppermute | solution.py:248
  48.5 2.4 %collective-permute-start.26 = (bf16[128,512]{1,0:T(8,128)(2,1)S(1)}, bf16[128,512]{1,0:T(8,128)(2,1)S(1)}, u32[]{:S(2)}, u32[]{:S(2)}) collective-permute-start(bf16[128,512]{1,0:T(8,128)(2,1)S(1)} %get-tuple-element.32), channel_id=1, source_target_pairs={{0,48},{16,0},{32,16},{48,32},{64,112},{80,64},{96,80},{112,96},{1... | collective-permute-start | bytes 393224 | tf_op jit(solution)/shard_map/ppermute | solution.py:248
  50.9 8.8 %attention.2 = (bf16[128,512]{1,0:T(8,128)(2,1)S(1)}, bf16[128,512]{1,0:T(8,128)(2,1)S(1)}, bf16[128,512]{1,0:T(8,128)(2,1)S(1)}, bf16[128,512]{1,0:T(8,128)(2,1)S(1)}) custom-call(s32[16]{0:T(128)} %span_map.3, s32[1]{0:T(128)} %bitcast.1.ctx, s32[1]{0:T(128)} %bitcast.section, bf16[128,4096]{1,0:T(8,128)(2,1)} %bitcast.4, ...), custom_call_target="tpu_custom_call" | custom-call | flops 4294967296 | bytes 3145728 | tf_op jit(solution)/shard_map/attention/pallas_call | solution.py:137
  59.8 2.1 %collective-permute-start.16 = (bf16[128,512]{1,0:T(8,128)(2,1)S(1)}, bf16[128,512]{1,0:T(8,128)(2,1)S(1)}, u32[]{:S(2)}, u32[]{:S(2)}) collective-permute-start(bf16[128,512]{1,0:T(8,128)(2,1)S(1)} %get-tuple-element.23), channel_id=1, source_target_pairs={{0,32},{16,48},{32,0},{48,16},{64,96},{80,112},{96,64},{112,80},{1... | collective-permute-start | bytes 393224 | tf_op jit(solution)/shard_map/ppermute | solution.py:248
  61.9 2.5 %collective-permute-start.17 = (bf16[128,512]{1,0:T(8,128)(2,1)S(1)}, bf16[128,512]{1,0:T(8,128)(2,1)S(1)}, u32[]{:S(2)}, u32[]{:S(2)}) collective-permute-start(bf16[128,512]{1,0:T(8,128)(2,1)S(1)} %get-tuple-element.24), channel_id=1, source_target_pairs={{0,48},{16,0},{32,16},{48,32},{64,112},{80,64},{96,80},{112,96},{1... | collective-permute-start | bytes 393224 | tf_op jit(solution)/shard_map/ppermute | solution.py:248
  64.5 4.9 %collective-permute-start.29 = (bf16[128,512]{1,0:T(8,128)(2,1)S(1)}, bf16[128,512]{1,0:T(8,128)(2,1)S(1)}, u32[]{:S(2)}, u32[]{:S(2)}) collective-permute-start(bf16[128,512]{1,0:T(8,128)(2,1)S(1)} %row_total.3), channel_id=1, source_target_pairs={{0,192},{16,208},{32,224},{48,240},{1,193},{17,209},{33,225},{49,2... | collective-permute-start | bytes 393224 | tf_op jit(solution)/shard_map/ppermute | solution.py:260
  72.1 3.2 %collective-permute-start.27 = (bf16[128,512]{1,0:T(8,128)(2,1)S(1)}, bf16[128,512]{1,0:T(8,128)(2,1)S(1)}, u32[]{:S(2)}, u32[]{:S(2)}) collective-permute-start(bf16[128,512]{1,0:T(8,128)(2,1)S(1)} %row_total.3), channel_id=1, source_target_pairs={{0,64},{16,80},{32,96},{48,112},{64,128},{80,144},{96,160},{112,17... | collective-permute-start | bytes 393224 | tf_op jit(solution)/shard_map/ppermute | solution.py:260
  75.4 2.2 %collective-permute-done.17.d.refs_3_ = bf16[128,512]{1,0:T(8,128)(2,1)S(1)} collective-permute-done((bf16[128,512]{1,0:T(8,128)(2,1)S(1)}, bf16[128,512]{1,0:T(8,128)(2,1)S(1)}, u32[]{:S(2)}, u32[]{:S(2)}) %collective-permute-start.17) | collective-permute-done | bytes 131104 | tf_op jit(solution)/shard_map/ppermute | solution.py:248
  77.6 4.6 %collective-permute-start.20 = (bf16[128,512]{1,0:T(8,128)(2,1)S(1)}, bf16[128,512]{1,0:T(8,128)(2,1)S(1)}, u32[]{:S(2)}, u32[]{:S(2)}) collective-permute-start(bf16[128,512]{1,0:T(8,128)(2,1)S(1)} %row_total.2), channel_id=1, source_target_pairs={{0,192},{16,208},{32,224},{48,240},{1,193},{17,209},{33,225},{49,2... | collective-permute-start | bytes 393224 | tf_op jit(solution)/shard_map/ppermute | solution.py:260
  83.6 2.5 %collective-permute-start.18 = (bf16[128,512]{1,0:T(8,128)(2,1)S(1)}, bf16[128,512]{1,0:T(8,128)(2,1)S(1)}, u32[]{:S(2)}, u32[]{:S(2)}) collective-permute-start(bf16[128,512]{1,0:T(8,128)(2,1)S(1)} %row_total.2), channel_id=1, source_target_pairs={{0,64},{16,80},{32,96},{48,112},{64,128},{80,144},{96,160},{112,17... | collective-permute-start | bytes 393224 | tf_op jit(solution)/shard_map/ppermute | solution.py:260
  87.2 2.0 %collective-permute-start.31 = (bf16[128,512]{1,0:T(8,128)(2,1)S(1)}, bf16[128,512]{1,0:T(8,128)(2,1)S(1)}, u32[]{:S(2)}, u32[]{:S(2)}) collective-permute-start(bf16[128,512]{1,0:T(8,128)(2,1)S(1)} %get-tuple-element.35), channel_id=1, source_target_pairs={{0,32},{16,48},{32,0},{48,16},{64,96},{80,112},{96,64},{112,80},{1... | collective-permute-start | bytes 393224 | tf_op jit(solution)/shard_map/ppermute | solution.py:248
  89.2 2.6 %collective-permute-start.32 = (bf16[128,512]{1,0:T(8,128)(2,1)S(1)}, bf16[128,512]{1,0:T(8,128)(2,1)S(1)}, u32[]{:S(2)}, u32[]{:S(2)}) collective-permute-start(bf16[128,512]{1,0:T(8,128)(2,1)S(1)} %get-tuple-element.36), channel_id=1, source_target_pairs={{0,48},{16,0},{32,16},{48,32},{64,112},{80,64},{96,80},{112,96},{1... | collective-permute-start | bytes 393224 | tf_op jit(solution)/shard_map/ppermute | solution.py:248
  92.4 3.4 %collective-permute-start.22 = (bf16[128,512]{1,0:T(8,128)(2,1)S(1)}, bf16[128,512]{1,0:T(8,128)(2,1)S(1)}, u32[]{:S(2)}, u32[]{:S(2)}) collective-permute-start(bf16[128,512]{1,0:T(8,128)(2,1)S(1)} %get-tuple-element.27), channel_id=1, source_target_pairs={{0,32},{16,48},{32,0},{48,16},{64,96},{80,112},{96,64},{112,80},{1... | collective-permute-start | bytes 393224 | tf_op jit(solution)/shard_map/ppermute | solution.py:248
  95.8 3.5 %collective-permute-start.23 = (bf16[128,512]{1,0:T(8,128)(2,1)S(1)}, bf16[128,512]{1,0:T(8,128)(2,1)S(1)}, u32[]{:S(2)}, u32[]{:S(2)}) collective-permute-start(bf16[128,512]{1,0:T(8,128)(2,1)S(1)} %get-tuple-element.28), channel_id=1, source_target_pairs={{0,48},{16,0},{32,16},{48,32},{64,112},{80,64},{96,80},{112,96},{1... | collective-permute-start | bytes 393224 | tf_op jit(solution)/shard_map/ppermute | solution.py:248
  99.3 10.7 %collective-permute-done.32.refs_7_ = bf16[128,512]{1,0:T(8,128)(2,1)S(1)} collective-permute-done((bf16[128,512]{1,0:T(8,128)(2,1)S(1)}, bf16[128,512]{1,0:T(8,128)(2,1)S(1)}, u32[]{:S(2)}, u32[]{:S(2)}) %collective-permute-start.32) | collective-permute-done | bytes 131104 | tf_op jit(solution)/shard_map/ppermute | solution.py:248
  110.0 2.8 %collective-permute-done.23.refs_3_ = bf16[128,512]{1,0:T(8,128)(2,1)S(1)} collective-permute-done((bf16[128,512]{1,0:T(8,128)(2,1)S(1)}, bf16[128,512]{1,0:T(8,128)(2,1)S(1)}, u32[]{:S(2)}, u32[]{:S(2)}) %collective-permute-start.23) | collective-permute-done | bytes 131104 | tf_op jit(solution)/shard_map/ppermute | solution.py:248
  (56 shorter events, 22.3 us)
Async XLA Ops:
  5.6 10.1 %collective-permute-start.2 = (bf16[128,1024]{1,0:T(8,128)(2,1)S(1)}, bf16[128,1024]{1,0:T(8,128)(2,1)S(1)}, u32[]{:S(2)}, u32[]{:S(2)}) collective-permute-start(bf16[128,1024]{1,0:T(8,128)(2,1)S(1)} %join.1.refs_0_.refs_16_), channel_id=1, source_target_pairs={{0,12},{1,13},{2,14},{3,15},{4,0},{5,1},{6,2},{7,3},{8,4},{9,5},{1... | collective-permute-start | bytes 786440 | tf_op jit(solution)/shard_map/ppermute | solution.py:38
  7.1 8.9 %collective-permute-start.7 = (bf16[128,1024]{1,0:T(8,128)(2,1)S(1)}, bf16[128,1024]{1,0:T(8,128)(2,1)S(1)}, u32[]{:S(2)}, u32[]{:S(2)}) collective-permute-start(bf16[128,1024]{1,0:T(8,128)(2,1)S(1)} %join.1.refs_0_.refs_16_), channel_id=1, source_target_pairs={{0,1},{1,0},{2,3},{3,2},{4,5},{5,4},{6,7},{7,6},{8,9},{9,8},{10,11... | collective-permute-start | bytes 786440 | tf_op jit(solution)/shard_map/ppermute | solution.py:38
  9.0 8.6 %collective-permute-start.1 = (bf16[128,1024]{1,0:T(8,128)(2,1)S(1)}, bf16[128,1024]{1,0:T(8,128)(2,1)S(1)}, u32[]{:S(2)}, u32[]{:S(2)}) collective-permute-start(bf16[128,1024]{1,0:T(8,128)(2,1)S(1)} %collective-permute-done.refs_1_.refs_17_), channel_id=1, source_target_pairs={{0,4},{1,5},{2,6},{3,7},{4,8},{5,9},{6,10},{7,11},{8,12},{9,13},{1... | collective-permute-start | bytes 786440 | tf_op jit(solution)/shard_map/ppermute | solution.py:38
  10.8 9.4 %collective-permute-start.11 = (bf16[128,1024]{1,0:T(8,128)(2,1)S(1)}, bf16[128,1024]{1,0:T(8,128)(2,1)S(1)}, u32[]{:S(2)}, u32[]{:S(2)}) collective-permute-start(bf16[128,1024]{1,0:T(8,128)(2,1)S(1)} %collective-permute-done.3.refs_4_.refs_20_), channel_id=1, source_target_pairs={{0,1},{1,0},{2,3},{3,2},{4,5},{5,4},{6,7},{7,6},{8,9},{9,8},{10,11... | collective-permute-start | bytes 786440 | tf_op jit(solution)/shard_map/ppermute | solution.py:38
  13.0 10.0 %collective-permute-start.6 = (bf16[128,1024]{1,0:T(8,128)(2,1)S(1)}, bf16[128,1024]{1,0:T(8,128)(2,1)S(1)}, u32[]{:S(2)}, u32[]{:S(2)}) collective-permute-start(bf16[128,1024]{1,0:T(8,128)(2,1)S(1)} %collective-permute-done.3.refs_4_.refs_20_), channel_id=1, source_target_pairs={{0,12},{1,13},{2,14},{3,15},{4,0},{5,1},{6,2},{7,3},{8,4},{9,5},{1... | collective-permute-start | bytes 786440 | tf_op jit(solution)/shard_map/ppermute | solution.py:38
  17.6 12.0 %collective-permute-start.5 = (bf16[128,1024]{1,0:T(8,128)(2,1)S(1)}, bf16[128,1024]{1,0:T(8,128)(2,1)S(1)}, u32[]{:S(2)}, u32[]{:S(2)}) collective-permute-start(bf16[128,1024]{1,0:T(8,128)(2,1)S(1)} %collective-permute-done.1.refs_2_.refs_18_), channel_id=1, source_target_pairs={{0,2},{1,3},{2,0},{3,1},{4,6},{5,7},{6,4},{7,5},{8,10},{9,11},{10,... | collective-permute-start | bytes 786440 | tf_op jit(solution)/shard_map/ppermute | solution.py:38
  20.2 10.2 %collective-permute-start.8 = (bf16[128,1024]{1,0:T(8,128)(2,1)S(1)}, bf16[128,1024]{1,0:T(8,128)(2,1)S(1)}, u32[]{:S(2)}, u32[]{:S(2)}) collective-permute-start(bf16[128,1024]{1,0:T(8,128)(2,1)S(1)} %collective-permute-done.refs_1_.refs_17_), channel_id=1, source_target_pairs={{0,1},{1,0},{2,3},{3,2},{4,5},{5,4},{6,7},{7,6},{8,9},{9,8},{10,11... | collective-permute-start | bytes 786440 | tf_op jit(solution)/shard_map/ppermute | solution.py:38
  40.5 21.4 %collective-permute-start.24 = (bf16[128,512]{1,0:T(8,128)(2,1)S(1)}, bf16[128,512]{1,0:T(8,128)(2,1)S(1)}, u32[]{:S(2)}, u32[]{:S(2)}) collective-permute-start(bf16[128,512]{1,0:T(8,128)(2,1)S(1)} %get-tuple-element.30), channel_id=1, source_target_pairs={{0,16},{16,32},{32,48},{48,0},{64,80},{80,96},{96,112},{112,64},{1... | collective-permute-start | bytes 393224 | tf_op jit(solution)/shard_map/ppermute | solution.py:248
  43.6 20.8 %collective-permute-start.25 = (bf16[128,512]{1,0:T(8,128)(2,1)S(1)}, bf16[128,512]{1,0:T(8,128)(2,1)S(1)}, u32[]{:S(2)}, u32[]{:S(2)}) collective-permute-start(bf16[128,512]{1,0:T(8,128)(2,1)S(1)} %get-tuple-element.31), channel_id=1, source_target_pairs={{0,32},{16,48},{32,0},{48,16},{64,96},{80,112},{96,64},{112,80},{1... | collective-permute-start | bytes 393224 | tf_op jit(solution)/shard_map/ppermute | solution.py:248
  48.5 15.9 %collective-permute-start.26 = (bf16[128,512]{1,0:T(8,128)(2,1)S(1)}, bf16[128,512]{1,0:T(8,128)(2,1)S(1)}, u32[]{:S(2)}, u32[]{:S(2)}) collective-permute-start(bf16[128,512]{1,0:T(8,128)(2,1)S(1)} %get-tuple-element.32), channel_id=1, source_target_pairs={{0,48},{16,0},{32,16},{48,32},{64,112},{80,64},{96,80},{112,96},{1... | collective-permute-start | bytes 393224 | tf_op jit(solution)/shard_map/ppermute | solution.py:248
  59.8 12.4 %collective-permute-start.15 = (bf16[128,512]{1,0:T(8,128)(2,1)S(1)}, bf16[128,512]{1,0:T(8,128)(2,1)S(1)}, u32[]{:S(2)}, u32[]{:S(2)}) collective-permute-start(bf16[128,512]{1,0:T(8,128)(2,1)S(1)} %get-tuple-element.22), channel_id=1, source_target_pairs={{0,16},{16,32},{32,48},{48,0},{64,80},{80,96},{96,112},{112,64},{1... | collective-permute-start | bytes 393224 | tf_op jit(solution)/shard_map/ppermute | solution.py:248
  59.8 15.5 %collective-permute-start.16 = (bf16[128,512]{1,0:T(8,128)(2,1)S(1)}, bf16[128,512]{1,0:T(8,128)(2,1)S(1)}, u32[]{:S(2)}, u32[]{:S(2)}) collective-permute-start(bf16[128,512]{1,0:T(8,128)(2,1)S(1)} %get-tuple-element.23), channel_id=1, source_target_pairs={{0,32},{16,48},{32,0},{48,16},{64,96},{80,112},{96,64},{112,80},{1... | collective-permute-start | bytes 393224 | tf_op jit(solution)/shard_map/ppermute | solution.py:248
  61.9 15.6 %collective-permute-start.17 = (bf16[128,512]{1,0:T(8,128)(2,1)S(1)}, bf16[128,512]{1,0:T(8,128)(2,1)S(1)}, u32[]{:S(2)}, u32[]{:S(2)}) collective-permute-start(bf16[128,512]{1,0:T(8,128)(2,1)S(1)} %get-tuple-element.24), channel_id=1, source_target_pairs={{0,48},{16,0},{32,16},{48,32},{64,112},{80,64},{96,80},{112,96},{1... | collective-permute-start | bytes 393224 | tf_op jit(solution)/shard_map/ppermute | solution.py:248
  64.5 19.1 %collective-permute-start.29 = (bf16[128,512]{1,0:T(8,128)(2,1)S(1)}, bf16[128,512]{1,0:T(8,128)(2,1)S(1)}, u32[]{:S(2)}, u32[]{:S(2)}) collective-permute-start(bf16[128,512]{1,0:T(8,128)(2,1)S(1)} %row_total.3), channel_id=1, source_target_pairs={{0,192},{16,208},{32,224},{48,240},{1,193},{17,209},{33,225},{49,2... | collective-permute-start | bytes 393224 | tf_op jit(solution)/shard_map/ppermute | solution.py:260
  69.4 16.7 %collective-permute-start.28 = (bf16[128,512]{1,0:T(8,128)(2,1)S(1)}, bf16[128,512]{1,0:T(8,128)(2,1)S(1)}, u32[]{:S(2)}, u32[]{:S(2)}) collective-permute-start(bf16[128,512]{1,0:T(8,128)(2,1)S(1)} %row_total.3), channel_id=1, source_target_pairs={{0,128},{16,144},{32,160},{48,176},{64,192},{80,208},{96,224},{112... | collective-permute-start | bytes 393224 | tf_op jit(solution)/shard_map/ppermute | solution.py:260
  72.1 14.0 %collective-permute-start.27 = (bf16[128,512]{1,0:T(8,128)(2,1)S(1)}, bf16[128,512]{1,0:T(8,128)(2,1)S(1)}, u32[]{:S(2)}, u32[]{:S(2)}) collective-permute-start(bf16[128,512]{1,0:T(8,128)(2,1)S(1)} %row_total.3), channel_id=1, source_target_pairs={{0,64},{16,80},{32,96},{48,112},{64,128},{80,144},{96,160},{112,17... | collective-permute-start | bytes 393224 | tf_op jit(solution)/shard_map/ppermute | solution.py:260
  77.6 11.6 %collective-permute-start.20 = (bf16[128,512]{1,0:T(8,128)(2,1)S(1)}, bf16[128,512]{1,0:T(8,128)(2,1)S(1)}, u32[]{:S(2)}, u32[]{:S(2)}) collective-permute-start(bf16[128,512]{1,0:T(8,128)(2,1)S(1)} %row_total.2), channel_id=1, source_target_pairs={{0,192},{16,208},{32,224},{48,240},{1,193},{17,209},{33,225},{49,2... | collective-permute-start | bytes 393224 | tf_op jit(solution)/shard_map/ppermute | solution.py:260
  82.3 9.5 %collective-permute-start.19 = (bf16[128,512]{1,0:T(8,128)(2,1)S(1)}, bf16[128,512]{1,0:T(8,128)(2,1)S(1)}, u32[]{:S(2)}, u32[]{:S(2)}) collective-permute-start(bf16[128,512]{1,0:T(8,128)(2,1)S(1)} %row_total.2), channel_id=1, source_target_pairs={{0,128},{16,144},{32,160},{48,176},{64,192},{80,208},{96,224},{112... | collective-permute-start | bytes 393224 | tf_op jit(solution)/shard_map/ppermute | solution.py:260
  86.4 9.5 %collective-permute-start.30 = (bf16[128,512]{1,0:T(8,128)(2,1)S(1)}, bf16[128,512]{1,0:T(8,128)(2,1)S(1)}, u32[]{:S(2)}, u32[]{:S(2)}) collective-permute-start(bf16[128,512]{1,0:T(8,128)(2,1)S(1)} %get-tuple-element.34), channel_id=1, source_target_pairs={{0,16},{16,32},{32,48},{48,0},{64,80},{80,96},{96,112},{112,64},{1... | collective-permute-start | bytes 393224 | tf_op jit(solution)/shard_map/ppermute | solution.py:248
  87.2 12.1 %collective-permute-start.31 = (bf16[128,512]{1,0:T(8,128)(2,1)S(1)}, bf16[128,512]{1,0:T(8,128)(2,1)S(1)}, u32[]{:S(2)}, u32[]{:S(2)}) collective-permute-start(bf16[128,512]{1,0:T(8,128)(2,1)S(1)} %get-tuple-element.35), channel_id=1, source_target_pairs={{0,32},{16,48},{32,0},{48,16},{64,96},{80,112},{96,64},{112,80},{1... | collective-permute-start | bytes 393224 | tf_op jit(solution)/shard_map/ppermute | solution.py:248
  89.2 20.8 %collective-permute-start.32 = (bf16[128,512]{1,0:T(8,128)(2,1)S(1)}, bf16[128,512]{1,0:T(8,128)(2,1)S(1)}, u32[]{:S(2)}, u32[]{:S(2)}) collective-permute-start(bf16[128,512]{1,0:T(8,128)(2,1)S(1)} %get-tuple-element.36), channel_id=1, source_target_pairs={{0,48},{16,0},{32,16},{48,32},{64,112},{80,64},{96,80},{112,96},{1... | collective-permute-start | bytes 393224 | tf_op jit(solution)/shard_map/ppermute | solution.py:248
  92.0 18.0 %collective-permute-start.21 = (bf16[128,512]{1,0:T(8,128)(2,1)S(1)}, bf16[128,512]{1,0:T(8,128)(2,1)S(1)}, u32[]{:S(2)}, u32[]{:S(2)}) collective-permute-start(bf16[128,512]{1,0:T(8,128)(2,1)S(1)} %get-tuple-element.26), channel_id=1, source_target_pairs={{0,16},{16,32},{32,48},{48,0},{64,80},{80,96},{96,112},{112,64},{1... | collective-permute-start | bytes 393224 | tf_op jit(solution)/shard_map/ppermute | solution.py:248
  92.4 17.6 %collective-permute-start.22 = (bf16[128,512]{1,0:T(8,128)(2,1)S(1)}, bf16[128,512]{1,0:T(8,128)(2,1)S(1)}, u32[]{:S(2)}, u32[]{:S(2)}) collective-permute-start(bf16[128,512]{1,0:T(8,128)(2,1)S(1)} %get-tuple-element.27), channel_id=1, source_target_pairs={{0,32},{16,48},{32,0},{48,16},{64,96},{80,112},{96,64},{112,80},{1... | collective-permute-start | bytes 393224 | tf_op jit(solution)/shard_map/ppermute | solution.py:248
  95.8 17.0 %collective-permute-start.23 = (bf16[128,512]{1,0:T(8,128)(2,1)S(1)}, bf16[128,512]{1,0:T(8,128)(2,1)S(1)}, u32[]{:S(2)}, u32[]{:S(2)}) collective-permute-start(bf16[128,512]{1,0:T(8,128)(2,1)S(1)} %get-tuple-element.28), channel_id=1, source_target_pairs={{0,48},{16,0},{32,16},{48,32},{64,112},{80,64},{96,80},{112,96},{1... | collective-permute-start | bytes 393224 | tf_op jit(solution)/shard_map/ppermute | solution.py:248
  (12 other events, 89.3 us)

commit v5 on v4

--- a/solution.py
+++ b/solution.py
@@ -43,7 +43,7 @@
 
 
 def climb_pairs(steps):
-    return [(i, i + RING * steps) for i in range(RING * (RING - steps))]
+    return [(i, (i + RING * steps) % (RING * RING)) for i in range(RING * RING)]
 
 
 def pinned(x):
@@ -184,15 +184,16 @@
 def prefix_kernel(chunk, section, residual_ref, *refs):
     slabs, below, outs = refs[:RING], refs[RING : 2 * RING - 1], refs[2 * RING - 1 : 3 * RING - 1]
     ordered, summed = refs[3 * RING - 1 :]
-    place = section[0] % RING
+    place, row = section[0] % RING, section[0] // RING
     for steps in range(RING):
         ordered[(place + RING - steps) % RING] = slabs[steps][...]
     for part in range(PART):
         columns = slice(part * PAIR, (part + 1) * PAIR)
         first = (chunk * PART + part) * GROUP * HEAD_SIZE + place * PAIR
         state = residual_ref[:, pl.ds(pl.multiple_of(first, PAIR), PAIR)].astype(jnp.float32)
-        for rows in below:
-            state = state + rows[:, columns].astype(jnp.float32)
+        for steps, rows in enumerate(below, 1):
+            earlier = rows[:, columns].astype(jnp.float32)
+            state = state + jnp.where(row >= steps, earlier, 0.0)
         for layer in range(RING):
             state = state + ordered[layer, :, columns].astype(jnp.float32)
             summed[layer, :, columns] = state.astype(jnp.bfloat16)
@@ -253,12 +254,19 @@
     ctx = lax.axis_index("ctx")[None]
     section = lax.axis_index("section")[None]
     units = gather(keys, values)
-    finished = []
+    slabs = [
+        turn(attention(span_map, ctx, section, queries[0], units, chunk))
+        for chunk in range(CHUNKS)
+    ]
+    finished, sums = [], None
     for chunk in range(CHUNKS):
-        slabs = turn(attention(span_map, ctx, section, queries[0], units, chunk))
-        total = row_total(slabs)
+        total = row_total(slabs[chunk])
+        if sums is not None:
+            total, *sums = lax.optimization_barrier((total, *sums))
+            finished += turn(sums)
         below = [lax.ppermute(total, "section", climb_pairs(s)) for s in range(1, RING)]
-        finished += turn(prefix(section, residual, slabs, below, chunk))
+        sums = prefix(section, residual, slabs[chunk], below, chunk)
+    finished += turn(sums)
     return assemble(section, finished)
 
 

time: 114 us -> 110 us (0.965)
  starting transfers between devices: 69.1 us -> 58.9 us
  waiting for transfers between devices: 23.5 us -> 29.4 us
    ppermute x6, starting transfers between devices: 17.8 us -> 8.53 us  [body(): lax.ppermute(total, 'section', climb_pairs(s))]
    ppermute x12, waiting for transfers between devices: 17.2 us -> 20.7 us  [turn(): lax.ppermute(slabs[steps], 'section', turn_pairs(steps))]
    ppermute x6, waiting for transfers between devices: 0.02 us -> 2.39 us  [body(): lax.ppermute(total, 'section', climb_pairs(s))]
  transfers between devices with their start and end apart: 33 -> 33, of which waited for: 8 -> 9; matrix products, arithmetic and copies ran while one was open for 0% -> 0% of each run, Pallas kernels for 8% -> 8%
where the time goes in v5:
time: 110 us
  starting transfers between devices  58.9 us (54%)
  waiting for transfers between devices  29.4 us (27%)
  Pallas kernels  19.4 us (18%)
  local copies, waits for them, and re-layouts  1.81 us (2%)
    ppermute x12, starting transfers between devices, turn(): lax.ppermute(slabs[steps], 'section', turn_pairs(steps))  26.8 us
    ppermute x15, starting transfers between devices, ctx_move(): return lax.ppermute(unit, 'ctx', ctx_pairs(dx, dz, dc))  23.6 us
    ppermute x12, waiting for transfers between devices, turn(): lax.ppermute(slabs[steps], 'section', turn_pairs(steps))  20.7 us
    pallas_call x2, Pallas kernels, attention(): pl.pallas_call(attention_kernel, grid_spec=pltpu.PrefetchScalarGridSpec(n...  17.6 us
    ppermute x6, starting transfers between devices, body(): lax.ppermute(total, 'section', climb_pairs(s))  8.53 us
    ppermute x15, waiting for transfers between devices, ctx_move(): return lax.ppermute(unit, 'ctx', ctx_pairs(dx, dz, dc))  6.32 us
    ppermute x6, waiting for transfers between devices, body(): lax.ppermute(total, 'section', climb_pairs(s))  2.39 us
  transfers between devices with their start and end apart: 33, of which 9 were waited for; matrix products, arithmetic and copies ran while one was open for 0% of the time, Pallas kernels for 8%

profile of v5, /device:TPU:1, one launch (start us, length us, event | category | flops | bytes accessed | tf_op | source)
XLA Modules:
  0.0 109.6 jit_solution(17467684537198936250)
XLA Ops:
  1.8 2.1 %collective-permute-start = (bf16[128,1024]{1,0:T(8,128)(2,1)S(1)}, bf16[128,1024]{1,0:T(8,128)(2,1)S(1)}, u32[]{:S(2)}, u32[]{:S(2)}) collective-permute-start(bf16[128,1024]{1,0:T(8,128)(2,1)S(1)} %join.1.refs_0_.refs_16_), channel_id=1, source_target_pairs={{0,4},{1,5},{2,6},{3,7},{4,8},{5,9},{6,10},{7,11},{8,12},{9,13},{1... | collective-permute-start | bytes 786440 | tf_op jit(solution)/shard_map/ppermute | solution.py:38
  9.0 1.9 %collective-permute-start.1 = (bf16[128,1024]{1,0:T(8,128)(2,1)S(1)}, bf16[128,1024]{1,0:T(8,128)(2,1)S(1)}, u32[]{:S(2)}, u32[]{:S(2)}) collective-permute-start(bf16[128,1024]{1,0:T(8,128)(2,1)S(1)} %collective-permute-done.refs_1_.refs_17_), channel_id=1, source_target_pairs={{0,4},{1,5},{2,6},{3,7},{4,8},{5,9},{6,10},{7,11},{8,12},{9,13},{1... | collective-permute-start | bytes 786440 | tf_op jit(solution)/shard_map/ppermute | solution.py:38
  10.8 2.1 %collective-permute-start.11 = (bf16[128,1024]{1,0:T(8,128)(2,1)S(1)}, bf16[128,1024]{1,0:T(8,128)(2,1)S(1)}, u32[]{:S(2)}, u32[]{:S(2)}) collective-permute-start(bf16[128,1024]{1,0:T(8,128)(2,1)S(1)} %collective-permute-done.3.refs_4_.refs_20_), channel_id=1, source_target_pairs={{0,1},{1,0},{2,3},{3,2},{4,5},{5,4},{6,7},{7,6},{8,9},{9,8},{10,11... | collective-permute-start | bytes 786440 | tf_op jit(solution)/shard_map/ppermute | solution.py:38
  13.0 2.7 %collective-permute-start.6 = (bf16[128,1024]{1,0:T(8,128)(2,1)S(1)}, bf16[128,1024]{1,0:T(8,128)(2,1)S(1)}, u32[]{:S(2)}, u32[]{:S(2)}) collective-permute-start(bf16[128,1024]{1,0:T(8,128)(2,1)S(1)} %collective-permute-done.3.refs_4_.refs_20_), channel_id=1, source_target_pairs={{0,12},{1,13},{2,14},{3,15},{4,0},{5,1},{6,2},{7,3},{8,4},{9,5},{1... | collective-permute-start | bytes 786440 | tf_op jit(solution)/shard_map/ppermute | solution.py:38
  17.6 2.7 %collective-permute-start.5 = (bf16[128,1024]{1,0:T(8,128)(2,1)S(1)}, bf16[128,1024]{1,0:T(8,128)(2,1)S(1)}, u32[]{:S(2)}, u32[]{:S(2)}) collective-permute-start(bf16[128,1024]{1,0:T(8,128)(2,1)S(1)} %collective-permute-done.1.refs_2_.refs_18_), channel_id=1, source_target_pairs={{0,2},{1,3},{2,0},{3,1},{4,6},{5,7},{6,4},{7,5},{8,10},{9,11},{10,... | collective-permute-start | bytes 786440 | tf_op jit(solution)/shard_map/ppermute | solution.py:38
  20.2 2.7 %collective-permute-start.8 = (bf16[128,1024]{1,0:T(8,128)(2,1)S(1)}, bf16[128,1024]{1,0:T(8,128)(2,1)S(1)}, u32[]{:S(2)}, u32[]{:S(2)}) collective-permute-start(bf16[128,1024]{1,0:T(8,128)(2,1)S(1)} %collective-permute-done.refs_1_.refs_17_), channel_id=1, source_target_pairs={{0,1},{1,0},{2,3},{3,2},{4,5},{5,4},{6,7},{7,6},{8,9},{9,8},{10,11... | collective-permute-start | bytes 786440 | tf_op jit(solution)/shard_map/ppermute | solution.py:38
  25.3 4.2 %collective-permute-done.5.refs_6_.refs_22_ = bf16[128,1024]{1,0:T(8,128)(2,1)S(1)} collective-permute-done((bf16[128,1024]{1,0:T(8,128)(2,1)S(1)}, bf16[128,1024]{1,0:T(8,128)(2,1)S(1)}, u32[]{:S(2)}, u32[]{:S(2)}) %collective-permute-start.5) | collective-permute-done | bytes 262176 | tf_op jit(solution)/shard_map/ppermute | solution.py:38
  31.7 8.8 %attention.3 = (bf16[128,512]{1,0:T(8,128)(2,1)S(1)}, bf16[128,512]{1,0:T(8,128)(2,1)S(1)}, bf16[128,512]{1,0:T(8,128)(2,1)S(1)}, bf16[128,512]{1,0:T(8,128)(2,1)S(1)}) custom-call(s32[16]{0:T(128)} %span_map.3, s32[1]{0:T(128)} %bitcast.1.ctx, s32[1]{0:T(128)} %bitcast.section, bf16[128,4096]{1,0:T(8,128)(2,1)} %bitcast.3, ...), custom_call_target="tpu_custom_call" | custom-call | flops 4294967296 | bytes 3145728 | tf_op jit(solution)/shard_map/attention/pallas_call | solution.py:137
  40.5 3.1 %collective-permute-start.18 = (bf16[128,512]{1,0:T(8,128)(2,1)S(1)}, bf16[128,512]{1,0:T(8,128)(2,1)S(1)}, u32[]{:S(2)}, u32[]{:S(2)}) collective-permute-start(bf16[128,512]{1,0:T(8,128)(2,1)S(1)} %get-tuple-element.31), channel_id=1, source_target_pairs={{0,16},{16,32},{32,48},{48,0},{64,80},{80,96},{96,112},{112,64},{1... | collective-permute-start | bytes 393224 | tf_op jit(solution)/shard_map/ppermute | solution.py:249
  43.6 4.9 %collective-permute-start.19 = (bf16[128,512]{1,0:T(8,128)(2,1)S(1)}, bf16[128,512]{1,0:T(8,128)(2,1)S(1)}, u32[]{:S(2)}, u32[]{:S(2)}) collective-permute-start(bf16[128,512]{1,0:T(8,128)(2,1)S(1)} %get-tuple-element.32), channel_id=1, source_target_pairs={{0,32},{16,48},{32,0},{48,16},{64,96},{80,112},{96,64},{112,80},{1... | collective-permute-start | bytes 393224 | tf_op jit(solution)/shard_map/ppermute | solution.py:249
  48.5 2.4 %collective-permute-start.20 = (bf16[128,512]{1,0:T(8,128)(2,1)S(1)}, bf16[128,512]{1,0:T(8,128)(2,1)S(1)}, u32[]{:S(2)}, u32[]{:S(2)}) collective-permute-start(bf16[128,512]{1,0:T(8,128)(2,1)S(1)} %get-tuple-element.33), channel_id=1, source_target_pairs={{0,48},{16,0},{32,16},{48,32},{64,112},{80,64},{96,80},{112,96},{1... | collective-permute-start | bytes 393224 | tf_op jit(solution)/shard_map/ppermute | solution.py:249
  50.9 8.8 %attention.2 = (bf16[128,512]{1,0:T(8,128)(2,1)S(1)}, bf16[128,512]{1,0:T(8,128)(2,1)S(1)}, bf16[128,512]{1,0:T(8,128)(2,1)S(1)}, bf16[128,512]{1,0:T(8,128)(2,1)S(1)}) custom-call(s32[16]{0:T(128)} %span_map.3, s32[1]{0:T(128)} %bitcast.1.ctx, s32[1]{0:T(128)} %bitcast.section, bf16[128,4096]{1,0:T(8,128)(2,1)} %bitcast.4, ...), custom_call_target="tpu_custom_call" | custom-call | flops 4294967296 | bytes 3145728 | tf_op jit(solution)/shard_map/attention/pallas_call | solution.py:137
  59.8 2.1 %collective-permute-start.16 = (bf16[128,512]{1,0:T(8,128)(2,1)S(1)}, bf16[128,512]{1,0:T(8,128)(2,1)S(1)}, u32[]{:S(2)}, u32[]{:S(2)}) collective-permute-start(bf16[128,512]{1,0:T(8,128)(2,1)S(1)} %get-tuple-element.28), channel_id=1, source_target_pairs={{0,32},{16,48},{32,0},{48,16},{64,96},{80,112},{96,64},{112,80},{1... | collective-permute-start | bytes 393224 | tf_op jit(solution)/shard_map/ppermute | solution.py:249
  61.9 2.5 %collective-permute-start.17 = (bf16[128,512]{1,0:T(8,128)(2,1)S(1)}, bf16[128,512]{1,0:T(8,128)(2,1)S(1)}, u32[]{:S(2)}, u32[]{:S(2)}) collective-permute-start(bf16[128,512]{1,0:T(8,128)(2,1)S(1)} %get-tuple-element.29), channel_id=1, source_target_pairs={{0,48},{16,0},{32,16},{48,32},{64,112},{80,64},{96,80},{112,96},{1... | collective-permute-start | bytes 393224 | tf_op jit(solution)/shard_map/ppermute | solution.py:249
  64.5 3.0 %collective-permute-start.23 = (bf16[128,512]{1,0:T(8,128)(2,1)S(1)}, bf16[128,512]{1,0:T(8,128)(2,1)S(1)}, u32[]{:S(2)}, u32[]{:S(2)}) collective-permute-start(bf16[128,512]{1,0:T(8,128)(2,1)S(1)} %row_total.3), channel_id=1, source_target_pairs={{0,192},{16,208},{32,224},{48,240},{64,0},{80,16},{96,32},{112,48}... | collective-permute-start | bytes 393224 | tf_op jit(solution)/shard_map/ppermute | solution.py:267
  67.9 4.3 %collective-permute-done.15.b.refs_1_ = bf16[128,512]{1,0:T(8,128)(2,1)S(1)} collective-permute-done((bf16[128,512]{1,0:T(8,128)(2,1)S(1)}, bf16[128,512]{1,0:T(8,128)(2,1)S(1)}, u32[]{:S(2)}, u32[]{:S(2)}) %collective-permute-start.15) | collective-permute-done | bytes 131104 | tf_op jit(solution)/shard_map/ppermute | solution.py:249
  73.4 4.1 %collective-permute-done.17.d.refs_3_ = bf16[128,512]{1,0:T(8,128)(2,1)S(1)} collective-permute-done((bf16[128,512]{1,0:T(8,128)(2,1)S(1)}, bf16[128,512]{1,0:T(8,128)(2,1)S(1)}, u32[]{:S(2)}, u32[]{:S(2)}) %collective-permute-start.17) | collective-permute-done | bytes 131104 | tf_op jit(solution)/shard_map/ppermute | solution.py:249
  77.9 2.8 %collective-permute-start.29 = (bf16[128,512]{1,0:T(8,128)(2,1)S(1)}, bf16[128,512]{1,0:T(8,128)(2,1)S(1)}, u32[]{:S(2)}, u32[]{:S(2)}) collective-permute-start(bf16[128,512]{1,0:T(8,128)(2,1)S(1)} %row_total.2), channel_id=1, source_target_pairs={{0,192},{16,208},{32,224},{48,240},{64,0},{80,16},{96,32},{112,48}... | collective-permute-start | bytes 393224 | tf_op jit(solution)/shard_map/ppermute | solution.py:267
  82.5 2.0 %collective-permute-start.25 = (bf16[128,512]{1,0:T(8,128)(2,1)S(1)}, bf16[128,512]{1,0:T(8,128)(2,1)S(1)}, u32[]{:S(2)}, u32[]{:S(2)}) collective-permute-start(bf16[128,512]{1,0:T(8,128)(2,1)S(1)} %get-tuple-element.40), channel_id=1, source_target_pairs={{0,32},{16,48},{32,0},{48,16},{64,96},{80,112},{96,64},{112,80},{1... | collective-permute-start | bytes 393224 | tf_op jit(solution)/shard_map/ppermute | solution.py:249
  84.6 2.6 %collective-permute-start.26 = (bf16[128,512]{1,0:T(8,128)(2,1)S(1)}, bf16[128,512]{1,0:T(8,128)(2,1)S(1)}, u32[]{:S(2)}, u32[]{:S(2)}) collective-permute-start(bf16[128,512]{1,0:T(8,128)(2,1)S(1)} %get-tuple-element.41), channel_id=1, source_target_pairs={{0,48},{16,0},{32,16},{48,32},{64,112},{80,64},{96,80},{112,96},{1... | collective-permute-start | bytes 393224 | tf_op jit(solution)/shard_map/ppermute | solution.py:249
  87.1 2.4 %collective-permute-done.27.refs_4_ = bf16[128,512]{1,0:T(8,128)(2,1)S(1)} collective-permute-done((bf16[128,512]{1,0:T(8,128)(2,1)S(1)}, bf16[128,512]{1,0:T(8,128)(2,1)S(1)}, u32[]{:S(2)}, u32[]{:S(2)}) %collective-permute-start.27) | collective-permute-done | bytes 131104 | tf_op jit(solution)/shard_map/ppermute | solution.py:267
  93.3 2.9 %collective-permute-start.32 = (bf16[128,512]{1,0:T(8,128)(2,1)S(1)}, bf16[128,512]{1,0:T(8,128)(2,1)S(1)}, u32[]{:S(2)}, u32[]{:S(2)}) collective-permute-start(bf16[128,512]{1,0:T(8,128)(2,1)S(1)} %get-tuple-element.46), channel_id=1, source_target_pairs={{0,48},{16,0},{32,16},{48,32},{64,112},{80,64},{96,80},{112,96},{1... | collective-permute-start | bytes 393224 | tf_op jit(solution)/shard_map/ppermute | solution.py:249
  96.2 9.5 %collective-permute-done.26.refs_3_ = bf16[128,512]{1,0:T(8,128)(2,1)S(1)} collective-permute-done((bf16[128,512]{1,0:T(8,128)(2,1)S(1)}, bf16[128,512]{1,0:T(8,128)(2,1)S(1)}, u32[]{:S(2)}, u32[]{:S(2)}) %collective-permute-start.26) | collective-permute-done | bytes 131104 | tf_op jit(solution)/shard_map/ppermute | solution.py:249
  105.7 2.8 %collective-permute-done.32.refs_7_ = bf16[128,512]{1,0:T(8,128)(2,1)S(1)} collective-permute-done((bf16[128,512]{1,0:T(8,128)(2,1)S(1)}, bf16[128,512]{1,0:T(8,128)(2,1)S(1)}, u32[]{:S(2)}, u32[]{:S(2)}) %collective-permute-start.32) | collective-permute-done | bytes 131104 | tf_op jit(solution)/shard_map/ppermute | solution.py:249
  (56 shorter events, 22.1 us)
Async XLA Ops:
  5.6 10.1 %collective-permute-start.2 = (bf16[128,1024]{1,0:T(8,128)(2,1)S(1)}, bf16[128,1024]{1,0:T(8,128)(2,1)S(1)}, u32[]{:S(2)}, u32[]{:S(2)}) collective-permute-start(bf16[128,1024]{1,0:T(8,128)(2,1)S(1)} %join.1.refs_0_.refs_16_), channel_id=1, source_target_pairs={{0,12},{1,13},{2,14},{3,15},{4,0},{5,1},{6,2},{7,3},{8,4},{9,5},{1... | collective-permute-start | bytes 786440 | tf_op jit(solution)/shard_map/ppermute | solution.py:38
  7.1 8.9 %collective-permute-start.7 = (bf16[128,1024]{1,0:T(8,128)(2,1)S(1)}, bf16[128,1024]{1,0:T(8,128)(2,1)S(1)}, u32[]{:S(2)}, u32[]{:S(2)}) collective-permute-start(bf16[128,1024]{1,0:T(8,128)(2,1)S(1)} %join.1.refs_0_.refs_16_), channel_id=1, source_target_pairs={{0,1},{1,0},{2,3},{3,2},{4,5},{5,4},{6,7},{7,6},{8,9},{9,8},{10,11... | collective-permute-start | bytes 786440 | tf_op jit(solution)/shard_map/ppermute | solution.py:38
  9.0 8.6 %collective-permute-start.1 = (bf16[128,1024]{1,0:T(8,128)(2,1)S(1)}, bf16[128,1024]{1,0:T(8,128)(2,1)S(1)}, u32[]{:S(2)}, u32[]{:S(2)}) collective-permute-start(bf16[128,1024]{1,0:T(8,128)(2,1)S(1)} %collective-permute-done.refs_1_.refs_17_), channel_id=1, source_target_pairs={{0,4},{1,5},{2,6},{3,7},{4,8},{5,9},{6,10},{7,11},{8,12},{9,13},{1... | collective-permute-start | bytes 786440 | tf_op jit(solution)/shard_map/ppermute | solution.py:38
  10.8 9.4 %collective-permute-start.11 = (bf16[128,1024]{1,0:T(8,128)(2,1)S(1)}, bf16[128,1024]{1,0:T(8,128)(2,1)S(1)}, u32[]{:S(2)}, u32[]{:S(2)}) collective-permute-start(bf16[128,1024]{1,0:T(8,128)(2,1)S(1)} %collective-permute-done.3.refs_4_.refs_20_), channel_id=1, source_target_pairs={{0,1},{1,0},{2,3},{3,2},{4,5},{5,4},{6,7},{7,6},{8,9},{9,8},{10,11... | collective-permute-start | bytes 786440 | tf_op jit(solution)/shard_map/ppermute | solution.py:38
  13.0 10.0 %collective-permute-start.6 = (bf16[128,1024]{1,0:T(8,128)(2,1)S(1)}, bf16[128,1024]{1,0:T(8,128)(2,1)S(1)}, u32[]{:S(2)}, u32[]{:S(2)}) collective-permute-start(bf16[128,1024]{1,0:T(8,128)(2,1)S(1)} %collective-permute-done.3.refs_4_.refs_20_), channel_id=1, source_target_pairs={{0,12},{1,13},{2,14},{3,15},{4,0},{5,1},{6,2},{7,3},{8,4},{9,5},{1... | collective-permute-start | bytes 786440 | tf_op jit(solution)/shard_map/ppermute | solution.py:38
  16.0 7.9 %collective-permute-start.4 = (bf16[128,1024]{1,0:T(8,128)(2,1)S(1)}, bf16[128,1024]{1,0:T(8,128)(2,1)S(1)}, u32[]{:S(2)}, u32[]{:S(2)}) collective-permute-start(bf16[128,1024]{1,0:T(8,128)(2,1)S(1)} %collective-permute-done.refs_1_.refs_17_), channel_id=1, source_target_pairs={{0,2},{1,3},{2,0},{3,1},{4,6},{5,7},{6,4},{7,5},{8,10},{9,11},{10,... | collective-permute-start | bytes 786440 | tf_op jit(solution)/shard_map/ppermute | solution.py:38
  17.6 12.0 %collective-permute-start.5 = (bf16[128,1024]{1,0:T(8,128)(2,1)S(1)}, bf16[128,1024]{1,0:T(8,128)(2,1)S(1)}, u32[]{:S(2)}, u32[]{:S(2)}) collective-permute-start(bf16[128,1024]{1,0:T(8,128)(2,1)S(1)} %collective-permute-done.1.refs_2_.refs_18_), channel_id=1, source_target_pairs={{0,2},{1,3},{2,0},{3,1},{4,6},{5,7},{6,4},{7,5},{8,10},{9,11},{10,... | collective-permute-start | bytes 786440 | tf_op jit(solution)/shard_map/ppermute | solution.py:38
  20.2 10.2 %collective-permute-start.8 = (bf16[128,1024]{1,0:T(8,128)(2,1)S(1)}, bf16[128,1024]{1,0:T(8,128)(2,1)S(1)}, u32[]{:S(2)}, u32[]{:S(2)}) collective-permute-start(bf16[128,1024]{1,0:T(8,128)(2,1)S(1)} %collective-permute-done.refs_1_.refs_17_), channel_id=1, source_target_pairs={{0,1},{1,0},{2,3},{3,2},{4,5},{5,4},{6,7},{7,6},{8,9},{9,8},{10,11... | collective-permute-start | bytes 786440 | tf_op jit(solution)/shard_map/ppermute | solution.py:38
  23.0 7.5 %collective-permute-start.9 = (bf16[128,1024]{1,0:T(8,128)(2,1)S(1)}, bf16[128,1024]{1,0:T(8,128)(2,1)S(1)}, u32[]{:S(2)}, u32[]{:S(2)}) collective-permute-start(bf16[128,1024]{1,0:T(8,128)(2,1)S(1)} %collective-permute-done.1.refs_2_.refs_18_), channel_id=1, source_target_pairs={{0,1},{1,0},{2,3},{3,2},{4,5},{5,4},{6,7},{7,6},{8,9},{9,8},{10,11... | collective-permute-start | bytes 786440 | tf_op jit(solution)/shard_map/ppermute | solution.py:38
  40.5 21.4 %collective-permute-start.18 = (bf16[128,512]{1,0:T(8,128)(2,1)S(1)}, bf16[128,512]{1,0:T(8,128)(2,1)S(1)}, u32[]{:S(2)}, u32[]{:S(2)}) collective-permute-start(bf16[128,512]{1,0:T(8,128)(2,1)S(1)} %get-tuple-element.31), channel_id=1, source_target_pairs={{0,16},{16,32},{32,48},{48,0},{64,80},{80,96},{96,112},{112,64},{1... | collective-permute-start | bytes 393224 | tf_op jit(solution)/shard_map/ppermute | solution.py:249
  43.6 20.8 %collective-permute-start.19 = (bf16[128,512]{1,0:T(8,128)(2,1)S(1)}, bf16[128,512]{1,0:T(8,128)(2,1)S(1)}, u32[]{:S(2)}, u32[]{:S(2)}) collective-permute-start(bf16[128,512]{1,0:T(8,128)(2,1)S(1)} %get-tuple-element.32), channel_id=1, source_target_pairs={{0,32},{16,48},{32,0},{48,16},{64,96},{80,112},{96,64},{112,80},{1... | collective-permute-start | bytes 393224 | tf_op jit(solution)/shard_map/ppermute | solution.py:249
  48.5 15.9 %collective-permute-start.20 = (bf16[128,512]{1,0:T(8,128)(2,1)S(1)}, bf16[128,512]{1,0:T(8,128)(2,1)S(1)}, u32[]{:S(2)}, u32[]{:S(2)}) collective-permute-start(bf16[128,512]{1,0:T(8,128)(2,1)S(1)} %get-tuple-element.33), channel_id=1, source_target_pairs={{0,48},{16,0},{32,16},{48,32},{64,112},{80,64},{96,80},{112,96},{1... | collective-permute-start | bytes 393224 | tf_op jit(solution)/shard_map/ppermute | solution.py:249
  59.8 12.4 %collective-permute-start.15 = (bf16[128,512]{1,0:T(8,128)(2,1)S(1)}, bf16[128,512]{1,0:T(8,128)(2,1)S(1)}, u32[]{:S(2)}, u32[]{:S(2)}) collective-permute-start(bf16[128,512]{1,0:T(8,128)(2,1)S(1)} %get-tuple-element.27), channel_id=1, source_target_pairs={{0,16},{16,32},{32,48},{48,0},{64,80},{80,96},{96,112},{112,64},{1... | collective-permute-start | bytes 393224 | tf_op jit(solution)/shard_map/ppermute | solution.py:249
  59.8 13.6 %collective-permute-start.16 = (bf16[128,512]{1,0:T(8,128)(2,1)S(1)}, bf16[128,512]{1,0:T(8,128)(2,1)S(1)}, u32[]{:S(2)}, u32[]{:S(2)}) collective-permute-start(bf16[128,512]{1,0:T(8,128)(2,1)S(1)} %get-tuple-element.28), channel_id=1, source_target_pairs={{0,32},{16,48},{32,0},{48,16},{64,96},{80,112},{96,64},{112,80},{1... | collective-permute-start | bytes 393224 | tf_op jit(solution)/shard_map/ppermute | solution.py:249
  61.9 15.6 %collective-permute-start.17 = (bf16[128,512]{1,0:T(8,128)(2,1)S(1)}, bf16[128,512]{1,0:T(8,128)(2,1)S(1)}, u32[]{:S(2)}, u32[]{:S(2)}) collective-permute-start(bf16[128,512]{1,0:T(8,128)(2,1)S(1)} %get-tuple-element.29), channel_id=1, source_target_pairs={{0,48},{16,0},{32,16},{48,32},{64,112},{80,64},{96,80},{112,96},{1... | collective-permute-start | bytes 393224 | tf_op jit(solution)/shard_map/ppermute | solution.py:249
  64.5 13.1 %collective-permute-start.23 = (bf16[128,512]{1,0:T(8,128)(2,1)S(1)}, bf16[128,512]{1,0:T(8,128)(2,1)S(1)}, u32[]{:S(2)}, u32[]{:S(2)}) collective-permute-start(bf16[128,512]{1,0:T(8,128)(2,1)S(1)} %row_total.3), channel_id=1, source_target_pairs={{0,192},{16,208},{32,224},{48,240},{64,0},{80,16},{96,32},{112,48}... | collective-permute-start | bytes 393224 | tf_op jit(solution)/shard_map/ppermute | solution.py:267
  67.5 10.1 %collective-permute-start.22 = (bf16[128,512]{1,0:T(8,128)(2,1)S(1)}, bf16[128,512]{1,0:T(8,128)(2,1)S(1)}, u32[]{:S(2)}, u32[]{:S(2)}) collective-permute-start(bf16[128,512]{1,0:T(8,128)(2,1)S(1)} %row_total.3), channel_id=1, source_target_pairs={{0,128},{16,144},{32,160},{48,176},{64,192},{80,208},{96,224},{112... | collective-permute-start | bytes 393224 | tf_op jit(solution)/shard_map/ppermute | solution.py:267
  81.1 8.4 %collective-permute-start.27 = (bf16[128,512]{1,0:T(8,128)(2,1)S(1)}, bf16[128,512]{1,0:T(8,128)(2,1)S(1)}, u32[]{:S(2)}, u32[]{:S(2)}) collective-permute-start(bf16[128,512]{1,0:T(8,128)(2,1)S(1)} %row_total.2), channel_id=1, source_target_pairs={{0,64},{16,80},{32,96},{48,112},{64,128},{80,144},{96,160},{112,17... | collective-permute-start | bytes 393224 | tf_op jit(solution)/shard_map/ppermute | solution.py:267
  81.8 11.5 %collective-permute-start.24 = (bf16[128,512]{1,0:T(8,128)(2,1)S(1)}, bf16[128,512]{1,0:T(8,128)(2,1)S(1)}, u32[]{:S(2)}, u32[]{:S(2)}) collective-permute-start(bf16[128,512]{1,0:T(8,128)(2,1)S(1)} %get-tuple-element.39), channel_id=1, source_target_pairs={{0,16},{16,32},{32,48},{48,0},{64,80},{80,96},{96,112},{112,64},{1... | collective-permute-start | bytes 393224 | tf_op jit(solution)/shard_map/ppermute | solution.py:249
  82.5 13.6 %collective-permute-start.25 = (bf16[128,512]{1,0:T(8,128)(2,1)S(1)}, bf16[128,512]{1,0:T(8,128)(2,1)S(1)}, u32[]{:S(2)}, u32[]{:S(2)}) collective-permute-start(bf16[128,512]{1,0:T(8,128)(2,1)S(1)} %get-tuple-element.40), channel_id=1, source_target_pairs={{0,32},{16,48},{32,0},{48,16},{64,96},{80,112},{96,64},{112,80},{1... | collective-permute-start | bytes 393224 | tf_op jit(solution)/shard_map/ppermute | solution.py:249
  84.6 21.1 %collective-permute-start.26 = (bf16[128,512]{1,0:T(8,128)(2,1)S(1)}, bf16[128,512]{1,0:T(8,128)(2,1)S(1)}, u32[]{:S(2)}, u32[]{:S(2)}) collective-permute-start(bf16[128,512]{1,0:T(8,128)(2,1)S(1)} %get-tuple-element.41), channel_id=1, source_target_pairs={{0,48},{16,0},{32,16},{48,32},{64,112},{80,64},{96,80},{112,96},{1... | collective-permute-start | bytes 393224 | tf_op jit(solution)/shard_map/ppermute | solution.py:249
  89.8 15.9 %collective-permute-start.30 = (bf16[128,512]{1,0:T(8,128)(2,1)S(1)}, bf16[128,512]{1,0:T(8,128)(2,1)S(1)}, u32[]{:S(2)}, u32[]{:S(2)}) collective-permute-start(bf16[128,512]{1,0:T(8,128)(2,1)S(1)} %get-tuple-element.44), channel_id=1, source_target_pairs={{0,16},{16,32},{32,48},{48,0},{64,80},{80,96},{96,112},{112,64},{1... | collective-permute-start | bytes 393224 | tf_op jit(solution)/shard_map/ppermute | solution.py:249
  91.4 14.2 %collective-permute-start.31 = (bf16[128,512]{1,0:T(8,128)(2,1)S(1)}, bf16[128,512]{1,0:T(8,128)(2,1)S(1)}, u32[]{:S(2)}, u32[]{:S(2)}) collective-permute-start(bf16[128,512]{1,0:T(8,128)(2,1)S(1)} %get-tuple-element.45), channel_id=1, source_target_pairs={{0,32},{16,48},{32,0},{48,16},{64,96},{80,112},{96,64},{112,80},{1... | collective-permute-start | bytes 393224 | tf_op jit(solution)/shard_map/ppermute | solution.py:249
  93.3 15.2 %collective-permute-start.32 = (bf16[128,512]{1,0:T(8,128)(2,1)S(1)}, bf16[128,512]{1,0:T(8,128)(2,1)S(1)}, u32[]{:S(2)}, u32[]{:S(2)}) collective-permute-start(bf16[128,512]{1,0:T(8,128)(2,1)S(1)} %get-tuple-element.46), channel_id=1, source_target_pairs={{0,48},{16,0},{32,16},{48,32},{64,112},{80,64},{96,80},{112,96},{1... | collective-permute-start | bytes 393224 | tf_op jit(solution)/shard_map/ppermute | solution.py:249
  (12 other events, 75.8 us)

commit v6 on v5

--- a/solution.py
+++ b/solution.py
@@ -13,7 +13,6 @@
 HEAD_SIZE = 128
 TOK = 128
 SPANS = 16
-TRACE = SPANS * TOK
 WIDTH = KEY_VALUE_HEADS * HEAD_SIZE
 RING = 4
 PAIR = 2 * HEAD_SIZE
@@ -23,7 +22,9 @@
 CHUNKS = 2
 PART = KEY_VALUE_HEADS // CHUNKS
 
-UNITS = [(dx, dz, dc) for dc in range(2) for dz in range(2) for dx in range(4)]
+EARLY = [(0, 0, 0), (0, 0, 1), (0, 1, 0), (1, 0, 0), (3, 0, 0), (0, 1, 1)]
+MIDDLE = [(1, 0, 1), (3, 0, 1), (2, 0, 0), (1, 1, 0), (3, 1, 0), (2, 0, 1)]
+LATE = [(1, 1, 1), (3, 1, 1), (2, 1, 0), (2, 1, 1)]
 
 
 def ctx_pairs(dx, dz, dc):
@@ -80,39 +81,47 @@
     for dz in range(2):
         for dx in range(4):
             held[dx, dz, 1] = ctx_move(held[dx, dz, 0], 0, 0, 1)
-    return [held[unit] for unit in UNITS]
-
-
-def attention_kernel(span_map, ctx, section, q_ref, *refs):
-    k_refs, v_refs = refs[:SPANS], refs[SPANS : 2 * SPANS]
-    o_refs = refs[2 * SPANS : 2 * SPANS + RING]
-    keys, vals, eye = refs[2 * SPANS + RING :]
+    return held
+
+
+def attention_kernel(units, base, first, last, span_map, ctx, section, q_ref, *refs):
+    count = len(units)
+    k_refs, v_refs, refs = refs[:count], refs[count : 2 * count], refs[2 * count :]
+    if not first:
+        (sums_in, peak_in), refs = refs[:2], refs[2:]
+    if last:
+        o_refs, refs = refs[:RING], refs[RING:]
+    else:
+        (sums_out, peak_out), refs = refs[:2], refs[2:]
+    keys, vals, eye = refs
+    group = base + pl.program_id(0)
 
     @pl.when(pl.program_id(0) == 0)
     def _():
         key_row = lax.broadcasted_iota(jnp.int32, (TOK, TOK), 0)
         query_row = lax.broadcasted_iota(jnp.int32, (TOK, TOK), 1)
         eye[...] = jnp.where(key_row == query_row, 1.0, 0.0).astype(jnp.bfloat16)
-        vals[:, HEAD_SIZE:] = jnp.ones((TRACE, HEAD_SIZE), jnp.bfloat16)
+        vals[:, HEAD_SIZE:] = jnp.ones((count * TOK, HEAD_SIZE), jnp.bfloat16)
         me = ctx[0]
         my_span = span_map[me]
         x, z, c = me // 4, me // 2 % 2, me % 2
-        for block, (dx, dz, dc) in enumerate(UNITS):
+        for block, (dx, dz, dc) in enumerate(units):
             source = (x + 4 - dx) % 4 * 4 + (z + dz) % 2 * 2 + (c + dc) % 2
             ahead = (span_map[source] - my_span) * TOK + key_row - query_row
             keys[block * TOK : (block + 1) * TOK, HEAD_SIZE:] = jnp.where(
                 ahead > 0, HIDDEN, 0.0
             ).astype(jnp.bfloat16)
 
-    for block in range(SPANS):
+    for block in range(count):
         rows = slice(block * TOK, (block + 1) * TOK)
         keys[rows, :HEAD_SIZE] = k_refs[block][...]
         vals[rows, :HEAD_SIZE] = v_refs[block][...]
     one_hot = eye[...]
     place = section[0] % RING
     for steps in range(RING):
-        first = pl.multiple_of((place + steps) % RING * PAIR, PAIR)
-        q = q_ref[:, pl.ds(first, PAIR)]
+        slab = (place + steps) % RING if last else steps
+        tile = group * RING + slab
+        q = q_ref[:, pl.ds(pl.multiple_of(slab * PAIR, PAIR), PAIR)]
         q = jnp.concatenate(
             [
                 jnp.concatenate([q[:, :HEAD_SIZE], one_hot], axis=1),
@@ -124,42 +133,74 @@
             q, keys[...], (((1,), (1,)), ((), ())), preferred_element_type=jnp.float32
         )
         peak = jnp.max(scores, axis=1, keepdims=True)
+        if not first:
+            before = peak_in[tile]
+            peak = jnp.maximum(peak, before[:, :1])
         weights = jnp.exp2((scores - peak) * EXP2_SCALE).astype(jnp.bfloat16)
         mixed = jnp.dot(weights, vals[...], preferred_element_type=jnp.float32)
-        result = (mixed[:, :HEAD_SIZE] / mixed[:, HEAD_SIZE:]).astype(jnp.bfloat16)
-        o_refs[steps][:, :HEAD_SIZE] = result[:TOK]
-        o_refs[steps][:, HEAD_SIZE:] = result[TOK:]
-
-
-def attention(span_map, ctx, section, queries, units, chunk):
-    base = chunk * PART
-    slab = jax.ShapeDtypeStruct((TOK, PART * PAIR), jnp.bfloat16)
-    return pl.pallas_call(
-        attention_kernel,
+        if not first:
+            mixed = mixed + sums_in[tile] * jnp.exp2((before[:, :1] - peak) * EXP2_SCALE)
+        if last:
+            result = (mixed[:, :HEAD_SIZE] / mixed[:, HEAD_SIZE:]).astype(jnp.bfloat16)
+            o_refs[steps][:, :HEAD_SIZE] = result[:TOK]
+            o_refs[steps][:, HEAD_SIZE:] = result[TOK:]
+        else:
+            sums_out[tile] = mixed
+            peak_out[tile] = jnp.broadcast_to(peak, (2 * TOK, HEAD_SIZE))
+
+
+def attention(span_map, ctx, section, queries, held, names, state, chunk):
+    first, last = state is None, chunk is not None
+    base, parts = (chunk * PART, PART) if last else (0, KEY_VALUE_HEADS)
+    count = len(names)
+    units = [held[name] for name in names]
+    whole = pl.BlockSpec(memory_space=pltpu.VMEM)
+    tiles = KEY_VALUE_HEADS * RING
+    if last:
+        out_specs = [pl.BlockSpec((TOK, PAIR), lambda g, *_: (0, g))] * RING
+        out_shape = [jax.ShapeDtypeStruct((TOK, PART * PAIR), jnp.bfloat16)] * RING
+    else:
+        out_specs = [whole] * 2
+        out_shape = [
+            jax.ShapeDtypeStruct((tiles, 2 * TOK, PAIR), jnp.float32),
+            jax.ShapeDtypeStruct((tiles, 2 * TOK, HEAD_SIZE), jnp.float32),
+        ]
+    return pl.pallas_call(
+        functools.partial(attention_kernel, names, base, first, last),
         grid_spec=pltpu.PrefetchScalarGridSpec(
             num_scalar_prefetch=3,
-            grid=(PART,),
+            grid=(parts,),
             in_specs=[pl.BlockSpec((TOK, GROUP * HEAD_SIZE), lambda g, *_: (0, base + g))]
-            + [pl.BlockSpec((TOK, HEAD_SIZE), lambda g, *_: (0, base + g))] * SPANS
+            + [pl.BlockSpec((TOK, HEAD_SIZE), lambda g, *_: (0, base + g))] * count
             + [pl.BlockSpec((TOK, HEAD_SIZE), lambda g, *_: (0, KEY_VALUE_HEADS + base + g))]
-            * SPANS,
-            out_specs=[pl.BlockSpec((TOK, PAIR), lambda g, *_: (0, g))] * RING,
+            * count
+            + ([] if first else [whole] * 2),
+            out_specs=out_specs,
             scratch_shapes=[
-                pltpu.VMEM((TRACE, PAIR), jnp.bfloat16),
-                pltpu.VMEM((TRACE, PAIR), jnp.bfloat16),
+                pltpu.VMEM((count * TOK, PAIR), jnp.bfloat16),
+                pltpu.VMEM((count * TOK, PAIR), jnp.bfloat16),
                 pltpu.VMEM((TOK, TOK), jnp.bfloat16),
             ],
         ),
-        out_shape=[slab] * RING,
+        out_shape=out_shape,
+        input_output_aliases={}
+        if first or last
+        else {4 + 2 * count: 0, 5 + 2 * count: 1},
         compiler_params=pltpu.CompilerParams(vmem_limit_bytes=VMEM_LIMIT),
         cost_estimate=pl.CostEstimate(
-            flops=PART * GROUP * TOK * TRACE * PAIR * 2 * 2,
-            bytes_accessed=PART * (TRACE * PAIR + GROUP * TOK * PAIR) * 2,
-            transcendentals=PART * GROUP * TOK * TRACE,
+            flops=parts * GROUP * TOK * count * TOK * PAIR * 2 * 2,
+            bytes_accessed=parts * (count * TOK + GROUP * TOK) * PAIR * 2,
+            transcendentals=parts * GROUP * TOK * count * TOK,
         ),
         name="attention",
     )(
-        pinned(span_map), ctx, section, pinned(queries), *units, *units
+        pinned(span_map),
+        ctx,
+        section,
+        pinned(queries),
+        *units,
+        *units,
+        *([] if first else state),
     )
 
 
@@ -253,11 +294,11 @@
 def body(queries, keys, values, residual, span_map):
     ctx = lax.axis_index("ctx")[None]
     section = lax.axis_index("section")[None]
-    units = gather(keys, values)
-    slabs = [
-        turn(attention(span_map, ctx, section, queries[0], units, chunk))
-        for chunk in range(CHUNKS)
-    ]
+    held = gather(keys, values)
+    attend = functools.partial(attention, span_map, ctx, section, queries[0], held)
+    state = attend(EARLY, None, None)
+    state = attend(MIDDLE, state, None)
+    slabs = [turn(attend(LATE, state, chunk)) for chunk in range(CHUNKS)]
     finished, sums = [], None
     for chunk in range(CHUNKS):
         total = row_total(slabs[chunk])

time: 110 us -> 114 us (1.036)
  the two profiles are of different devices: /device:TPU:1 before, /device:TPU:2 now
where the time goes in v6:
time: 114 us
  starting transfers between devices  52.8 us (46%)
  waiting for transfers between devices  30.9 us (27%)
  Pallas kernels  28 us (25%)
  local copies, waits for them, and re-layouts  1.81 us (2%)
    ppermute x12, starting transfers between devices, turn(): lax.ppermute(slabs[steps], 'section', turn_pairs(steps))  29.8 us
    pallas_call x4, Pallas kernels, attention(): pl.pallas_call(functools.partial(attention_kernel, names, base, first, la...  26.2 us
    ppermute x12, waiting for transfers between devices, turn(): lax.ppermute(slabs[steps], 'section', turn_pairs(steps))  19.5 us
    ppermute x6, starting transfers between devices, body(): lax.ppermute(total, 'section', climb_pairs(s))  13.4 us
    ppermute x15, waiting for transfers between devices, ctx_move(): return lax.ppermute(unit, 'ctx', ctx_pairs(dx, dz, dc))  11.3 us
    ppermute x15, starting transfers between devices, ctx_move(): return lax.ppermute(unit, 'ctx', ctx_pairs(dx, dz, dc))  9.54 us
  transfers between devices with their start and end apart: 33, of which 12 were waited for; matrix products, arithmetic and copies ran while one was open for 0% of the time, Pallas kernels for 19%

profile of v6, /device:TPU:2, one launch (start us, length us, event | category | flops | bytes accessed | tf_op | source)
XLA Modules:
  0.0 113.6 jit_solution(1473979450595156305)
XLA Ops:
  1.8 2.0 %collective-permute-start.3 = (bf16[128,1024]{1,0:T(8,128)(2,1)S(1)}, bf16[128,1024]{1,0:T(8,128)(2,1)S(1)}, u32[]{:S(2)}, u32[]{:S(2)}) collective-permute-start(bf16[128,1024]{1,0:T(8,128)(2,1)S(1)} %join.1.refs_0_.refs_6_), channel_id=1, source_target_pairs={{0,2},{1,3},{2,0},{3,1},{4,6},{5,7},{6,4},{7,5},{8,10},{9,11},{10,... | collective-permute-start | bytes 786440 | tf_op jit(solution)/shard_map/ppermute | solution.py:39
  5.9 4.3 %collective-permute-done.3.refs_2_.refs_8_ = bf16[128,1024]{1,0:T(8,128)(2,1)S(1)} collective-permute-done((bf16[128,1024]{1,0:T(8,128)(2,1)S(1)}, bf16[128,1024]{1,0:T(8,128)(2,1)S(1)}, u32[]{:S(2)}, u32[]{:S(2)}) %collective-permute-start.3) | collective-permute-done | bytes 262176 | tf_op jit(solution)/shard_map/ppermute | solution.py:39
  14.5 4.3 %collective-permute-done.6.refs_2_.refs_8_ = bf16[128,1024]{1,0:T(8,128)(2,1)S(1)} collective-permute-done((bf16[128,1024]{1,0:T(8,128)(2,1)S(1)}, bf16[128,1024]{1,0:T(8,128)(2,1)S(1)}, u32[]{:S(2)}, u32[]{:S(2)}) %collective-permute-start.6) | collective-permute-done | bytes 262176 | tf_op jit(solution)/shard_map/ppermute | solution.py:39
  21.8 7.8 %attention.4 = (f32[16,256,256]{2,1,0:T(8,128)S(1)}, f32[16,256,128]{2,1,0:T(8,128)S(1)}) custom-call(s32[16]{0:T(128)} %span_map.7, s32[1]{0:T(128)} %bitcast.1.ctx, s32[1]{0:T(128)} %bitcast.section, bf16[128,4096]{1,0:T(8,128)(2,1)} %bitcast.3, bf16[128,1024]{1,0:T(8,128)(2,1)S(1)} %join.1.refs_0_.refs_6_, ...), custom_call_target="tpu_custom_call" | custom-call | flops 3221225472 | bytes 3670016 | tf_op jit(solution)/shard_map/attention/pallas_call | solution.py:168
  30.6 8.9 %attention.5 = (f32[16,256,256]{2,1,0:T(8,128)S(1)}, f32[16,256,128]{2,1,0:T(8,128)S(1)}) custom-call(s32[16]{0:T(128)} %span_map.7, s32[1]{0:T(128)} %bitcast.1.ctx, s32[1]{0:T(128)} %bitcast.section, bf16[128,4096]{1,0:T(8,128)(2,1)} %bitcast.4, ...), custom_call_target="tpu_custom_call", output_to_operand_aliasing={{0}: (16, {}), {1}: (17, {})} | custom-call | flops 3221225472 | bytes 3670016 | tf_op jit(solution)/shard_map/attention/pallas_call | solution.py:168
  39.5 4.7 %attention.7 = (bf16[128,512]{1,0:T(8,128)(2,1)S(1)}, bf16[128,512]{1,0:T(8,128)(2,1)S(1)}, bf16[128,512]{1,0:T(8,128)(2,1)S(1)}, bf16[128,512]{1,0:T(8,128)(2,1)S(1)}) custom-call(s32[16]{0:T(128)} %span_map.7, s32[1]{0:T(128)} %bitcast.1.ctx, s32[1]{0:T(128)} %bitcast.section, bf16[128,4096]{1,0:T(8,128)(2,1)} %bitcast.5, ...), custom_call_target="tpu_custom_call" | custom-call | flops 1073741824 | bytes 1572864 | tf_op jit(solution)/shard_map/attention/pallas_call | solution.py:168
  44.3 3.4 %collective-permute-start.18 = (bf16[128,512]{1,0:T(8,128)(2,1)S(1)}, bf16[128,512]{1,0:T(8,128)(2,1)S(1)}, u32[]{:S(2)}, u32[]{:S(2)}) collective-permute-start(bf16[128,512]{1,0:T(8,128)(2,1)S(1)} %get-tuple-element.39), channel_id=1, source_target_pairs={{0,16},{16,32},{32,48},{48,0},{64,80},{80,96},{96,112},{112,64},{1... | collective-permute-start | bytes 393224 | tf_op jit(solution)/shard_map/ppermute | solution.py:290
  47.6 4.5 %collective-permute-start.19 = (bf16[128,512]{1,0:T(8,128)(2,1)S(1)}, bf16[128,512]{1,0:T(8,128)(2,1)S(1)}, u32[]{:S(2)}, u32[]{:S(2)}) collective-permute-start(bf16[128,512]{1,0:T(8,128)(2,1)S(1)} %get-tuple-element.40), channel_id=1, source_target_pairs={{0,32},{16,48},{32,0},{48,16},{64,96},{80,112},{96,64},{112,80},{1... | collective-permute-start | bytes 393224 | tf_op jit(solution)/shard_map/ppermute | solution.py:290
  52.1 2.7 %collective-permute-start.20 = (bf16[128,512]{1,0:T(8,128)(2,1)S(1)}, bf16[128,512]{1,0:T(8,128)(2,1)S(1)}, u32[]{:S(2)}, u32[]{:S(2)}) collective-permute-start(bf16[128,512]{1,0:T(8,128)(2,1)S(1)} %get-tuple-element.41), channel_id=1, source_target_pairs={{0,48},{16,0},{32,16},{48,32},{64,112},{80,64},{96,80},{112,96},{1... | collective-permute-start | bytes 393224 | tf_op jit(solution)/shard_map/ppermute | solution.py:290
  54.8 4.7 %attention.6 = (bf16[128,512]{1,0:T(8,128)(2,1)S(1)}, bf16[128,512]{1,0:T(8,128)(2,1)S(1)}, bf16[128,512]{1,0:T(8,128)(2,1)S(1)}, bf16[128,512]{1,0:T(8,128)(2,1)S(1)}) custom-call(s32[16]{0:T(128)} %span_map.7, s32[1]{0:T(128)} %bitcast.1.ctx, s32[1]{0:T(128)} %bitcast.section, bf16[128,4096]{1,0:T(8,128)(2,1)} %bitcast.6, ...), custom_call_target="tpu_custom_call" | custom-call | flops 1073741824 | bytes 1572864 | tf_op jit(solution)/shard_map/attention/pallas_call | solution.py:168
  59.9 2.2 %collective-permute-start.16 = (bf16[128,512]{1,0:T(8,128)(2,1)S(1)}, bf16[128,512]{1,0:T(8,128)(2,1)S(1)}, u32[]{:S(2)}, u32[]{:S(2)}) collective-permute-start(bf16[128,512]{1,0:T(8,128)(2,1)S(1)} %get-tuple-element.36), channel_id=1, source_target_pairs={{0,32},{16,48},{32,0},{48,16},{64,96},{80,112},{96,64},{112,80},{1... | collective-permute-start | bytes 393224 | tf_op jit(solution)/shard_map/ppermute | solution.py:290
  62.1 2.7 %collective-permute-start.17 = (bf16[128,512]{1,0:T(8,128)(2,1)S(1)}, bf16[128,512]{1,0:T(8,128)(2,1)S(1)}, u32[]{:S(2)}, u32[]{:S(2)}) collective-permute-start(bf16[128,512]{1,0:T(8,128)(2,1)S(1)} %get-tuple-element.37), channel_id=1, source_target_pairs={{0,48},{16,0},{32,16},{48,32},{64,112},{80,64},{96,80},{112,96},{1... | collective-permute-start | bytes 393224 | tf_op jit(solution)/shard_map/ppermute | solution.py:290
  66.5 2.9 %collective-permute-start.22 = (bf16[128,512]{1,0:T(8,128)(2,1)S(1)}, bf16[128,512]{1,0:T(8,128)(2,1)S(1)}, u32[]{:S(2)}, u32[]{:S(2)}) collective-permute-start(bf16[128,512]{1,0:T(8,128)(2,1)S(1)} %row_total.3), channel_id=1, source_target_pairs={{0,128},{16,144},{32,160},{48,176},{64,192},{80,208},{96,224},{112... | collective-permute-start | bytes 393224 | tf_op jit(solution)/shard_map/ppermute | solution.py:308
  70.8 3.0 %collective-permute-start.23 = (bf16[128,512]{1,0:T(8,128)(2,1)S(1)}, bf16[128,512]{1,0:T(8,128)(2,1)S(1)}, u32[]{:S(2)}, u32[]{:S(2)}) collective-permute-start(bf16[128,512]{1,0:T(8,128)(2,1)S(1)} %row_total.3), channel_id=1, source_target_pairs={{0,192},{16,208},{32,224},{48,240},{64,0},{80,16},{96,32},{112,48}... | collective-permute-start | bytes 393224 | tf_op jit(solution)/shard_map/ppermute | solution.py:308
  73.7 3.3 %collective-permute-done.17.d.refs_3_ = bf16[128,512]{1,0:T(8,128)(2,1)S(1)} collective-permute-done((bf16[128,512]{1,0:T(8,128)(2,1)S(1)}, bf16[128,512]{1,0:T(8,128)(2,1)S(1)}, u32[]{:S(2)}, u32[]{:S(2)}) %collective-permute-start.17) | collective-permute-done | bytes 131104 | tf_op jit(solution)/shard_map/ppermute | solution.py:290
  79.1 2.9 %collective-permute-start.28 = (bf16[128,512]{1,0:T(8,128)(2,1)S(1)}, bf16[128,512]{1,0:T(8,128)(2,1)S(1)}, u32[]{:S(2)}, u32[]{:S(2)}) collective-permute-start(bf16[128,512]{1,0:T(8,128)(2,1)S(1)} %row_total.2), channel_id=1, source_target_pairs={{0,128},{16,144},{32,160},{48,176},{64,192},{80,208},{96,224},{112... | collective-permute-start | bytes 393224 | tf_op jit(solution)/shard_map/ppermute | solution.py:308
  83.3 2.6 %collective-permute-start.24 = (bf16[128,512]{1,0:T(8,128)(2,1)S(1)}, bf16[128,512]{1,0:T(8,128)(2,1)S(1)}, u32[]{:S(2)}, u32[]{:S(2)}) collective-permute-start(bf16[128,512]{1,0:T(8,128)(2,1)S(1)} %get-tuple-element.47), channel_id=1, source_target_pairs={{0,16},{16,32},{32,48},{48,0},{64,80},{80,96},{96,112},{112,64},{1... | collective-permute-start | bytes 393224 | tf_op jit(solution)/shard_map/ppermute | solution.py:290
  85.9 2.2 %collective-permute-start.25 = (bf16[128,512]{1,0:T(8,128)(2,1)S(1)}, bf16[128,512]{1,0:T(8,128)(2,1)S(1)}, u32[]{:S(2)}, u32[]{:S(2)}) collective-permute-start(bf16[128,512]{1,0:T(8,128)(2,1)S(1)} %get-tuple-element.48), channel_id=1, source_target_pairs={{0,32},{16,48},{32,0},{48,16},{64,96},{80,112},{96,64},{112,80},{1... | collective-permute-start | bytes 393224 | tf_op jit(solution)/shard_map/ppermute | solution.py:290
  88.2 2.5 %collective-permute-start.26 = (bf16[128,512]{1,0:T(8,128)(2,1)S(1)}, bf16[128,512]{1,0:T(8,128)(2,1)S(1)}, u32[]{:S(2)}, u32[]{:S(2)}) collective-permute-start(bf16[128,512]{1,0:T(8,128)(2,1)S(1)} %get-tuple-element.49), channel_id=1, source_target_pairs={{0,48},{16,0},{32,16},{48,32},{64,112},{80,64},{96,80},{112,96},{1... | collective-permute-start | bytes 393224 | tf_op jit(solution)/shard_map/ppermute | solution.py:290
  91.4 3.7 %collective-permute-start.31 = (bf16[128,512]{1,0:T(8,128)(2,1)S(1)}, bf16[128,512]{1,0:T(8,128)(2,1)S(1)}, u32[]{:S(2)}, u32[]{:S(2)}) collective-permute-start(bf16[128,512]{1,0:T(8,128)(2,1)S(1)} %get-tuple-element.53), channel_id=1, source_target_pairs={{0,32},{16,48},{32,0},{48,16},{64,96},{80,112},{96,64},{112,80},{1... | collective-permute-start | bytes 393224 | tf_op jit(solution)/shard_map/ppermute | solution.py:290
  95.4 2.5 %collective-permute-start.32 = (bf16[128,512]{1,0:T(8,128)(2,1)S(1)}, bf16[128,512]{1,0:T(8,128)(2,1)S(1)}, u32[]{:S(2)}, u32[]{:S(2)}) collective-permute-start(bf16[128,512]{1,0:T(8,128)(2,1)S(1)} %get-tuple-element.54), channel_id=1, source_target_pairs={{0,48},{16,0},{32,16},{48,32},{64,112},{80,64},{96,80},{112,96},{1... | collective-permute-start | bytes 393224 | tf_op jit(solution)/shard_map/ppermute | solution.py:290
  97.9 2.3 %collective-permute-done.25.refs_2_ = bf16[128,512]{1,0:T(8,128)(2,1)S(1)} collective-permute-done((bf16[128,512]{1,0:T(8,128)(2,1)S(1)}, bf16[128,512]{1,0:T(8,128)(2,1)S(1)}, u32[]{:S(2)}, u32[]{:S(2)}) %collective-permute-start.25) | collective-permute-done | bytes 131104 | tf_op jit(solution)/shard_map/ppermute | solution.py:290
  101.5 5.7 %collective-permute-done.30.refs_5_ = bf16[128,512]{1,0:T(8,128)(2,1)S(1)} collective-permute-done((bf16[128,512]{1,0:T(8,128)(2,1)S(1)}, bf16[128,512]{1,0:T(8,128)(2,1)S(1)}, u32[]{:S(2)}, u32[]{:S(2)}) %collective-permute-start.30) | collective-permute-done | bytes 131104 | tf_op jit(solution)/shard_map/ppermute | solution.py:290
  108.5 4.0 %collective-permute-done.32.refs_7_ = bf16[128,512]{1,0:T(8,128)(2,1)S(1)} collective-permute-done((bf16[128,512]{1,0:T(8,128)(2,1)S(1)}, bf16[128,512]{1,0:T(8,128)(2,1)S(1)}, u32[]{:S(2)}, u32[]{:S(2)}) %collective-permute-start.32) | collective-permute-done | bytes 131104 | tf_op jit(solution)/shard_map/ppermute | solution.py:290
  (58 shorter events, 23.6 us)
Async XLA Ops:
  13.5 16.2 %collective-permute-start.4 = (bf16[128,1024]{1,0:T(8,128)(2,1)S(1)}, bf16[128,1024]{1,0:T(8,128)(2,1)S(1)}, u32[]{:S(2)}, u32[]{:S(2)}) collective-permute-start(bf16[128,1024]{1,0:T(8,128)(2,1)S(1)} %collective-permute-done.3.refs_2_.refs_8_), channel_id=1, source_target_pairs={{0,12},{1,13},{2,14},{3,15},{4,0},{5,1},{6,2},{7,3},{8,4},{9,5},{1... | collective-permute-start | bytes 786440 | tf_op jit(solution)/shard_map/ppermute | solution.py:39
  14.0 15.8 %collective-permute-start.9 = (bf16[128,1024]{1,0:T(8,128)(2,1)S(1)}, bf16[128,1024]{1,0:T(8,128)(2,1)S(1)}, u32[]{:S(2)}, u32[]{:S(2)}) collective-permute-start(bf16[128,1024]{1,0:T(8,128)(2,1)S(1)} %collective-permute-done.refs_3_.refs_9_), channel_id=1, source_target_pairs={{0,1},{1,0},{2,3},{3,2},{4,5},{5,4},{6,7},{7,6},{8,9},{9,8},{10,11... | collective-permute-start | bytes 786440 | tf_op jit(solution)/shard_map/ppermute | solution.py:39
  14.0 16.6 %collective-permute-start.11 = (bf16[128,1024]{1,0:T(8,128)(2,1)S(1)}, bf16[128,1024]{1,0:T(8,128)(2,1)S(1)}, u32[]{:S(2)}, u32[]{:S(2)}) collective-permute-start(bf16[128,1024]{1,0:T(8,128)(2,1)S(1)} %collective-permute-done.10.refs_4_.refs_10_), channel_id=1, source_target_pairs={{0,1},{1,0},{2,3},{3,2},{4,5},{5,4},{6,7},{7,6},{8,9},{9,8},{10,11... | collective-permute-start | bytes 786440 | tf_op jit(solution)/shard_map/ppermute | solution.py:39
  18.9 11.7 %collective-permute-start.12 = (bf16[128,1024]{1,0:T(8,128)(2,1)S(1)}, bf16[128,1024]{1,0:T(8,128)(2,1)S(1)}, u32[]{:S(2)}, u32[]{:S(2)}) collective-permute-start(bf16[128,1024]{1,0:T(8,128)(2,1)S(1)} %collective-permute-done.6.refs_2_.refs_8_), channel_id=1, source_target_pairs={{0,1},{1,0},{2,3},{3,2},{4,5},{5,4},{6,7},{7,6},{8,9},{9,8},{10,11... | collective-permute-start | bytes 786440 | tf_op jit(solution)/shard_map/ppermute | solution.py:39
  20.1 10.2 %collective-permute-start.7 = (bf16[128,1024]{1,0:T(8,128)(2,1)S(1)}, bf16[128,1024]{1,0:T(8,128)(2,1)S(1)}, u32[]{:S(2)}, u32[]{:S(2)}) collective-permute-start(bf16[128,1024]{1,0:T(8,128)(2,1)S(1)} %collective-permute-done.6.refs_2_.refs_8_), channel_id=1, source_target_pairs={{0,2},{1,3},{2,0},{3,1},{4,6},{5,7},{6,4},{7,5},{8,10},{9,11},{10,... | collective-permute-start | bytes 786440 | tf_op jit(solution)/shard_map/ppermute | solution.py:39
  29.7 9.8 %collective-permute-start.2 = (bf16[128,1024]{1,0:T(8,128)(2,1)S(1)}, bf16[128,1024]{1,0:T(8,128)(2,1)S(1)}, u32[]{:S(2)}, u32[]{:S(2)}) collective-permute-start(bf16[128,1024]{1,0:T(8,128)(2,1)S(1)} %collective-permute-done.1.refs_3_.refs_9_), channel_id=1, source_target_pairs={{0,1},{1,0},{2,3},{3,2},{4,5},{5,4},{6,7},{7,6},{8,9},{9,8},{10,11... | collective-permute-start | bytes 786440 | tf_op jit(solution)/shard_map/ppermute | solution.py:39
  29.8 9.7 %collective-permute-start.5 = (bf16[128,1024]{1,0:T(8,128)(2,1)S(1)}, bf16[128,1024]{1,0:T(8,128)(2,1)S(1)}, u32[]{:S(2)}, u32[]{:S(2)}) collective-permute-start(bf16[128,1024]{1,0:T(8,128)(2,1)S(1)} %collective-permute-done.4.refs_4_.refs_10_), channel_id=1, source_target_pairs={{0,1},{1,0},{2,3},{3,2},{4,5},{5,4},{6,7},{7,6},{8,9},{9,8},{10,11... | collective-permute-start | bytes 786440 | tf_op jit(solution)/shard_map/ppermute | solution.py:39
  30.3 9.2 %collective-permute-start.8 = (bf16[128,1024]{1,0:T(8,128)(2,1)S(1)}, bf16[128,1024]{1,0:T(8,128)(2,1)S(1)}, u32[]{:S(2)}, u32[]{:S(2)}) collective-permute-start(bf16[128,1024]{1,0:T(8,128)(2,1)S(1)} %collective-permute-done.7.refs_2_.refs_6_), channel_id=1, source_target_pairs={{0,1},{1,0},{2,3},{3,2},{4,5},{5,4},{6,7},{7,6},{8,9},{9,8},{10,11... | collective-permute-start | bytes 786440 | tf_op jit(solution)/shard_map/ppermute | solution.py:39
  44.3 17.8 %collective-permute-start.18 = (bf16[128,512]{1,0:T(8,128)(2,1)S(1)}, bf16[128,512]{1,0:T(8,128)(2,1)S(1)}, u32[]{:S(2)}, u32[]{:S(2)}) collective-permute-start(bf16[128,512]{1,0:T(8,128)(2,1)S(1)} %get-tuple-element.39), channel_id=1, source_target_pairs={{0,16},{16,32},{32,48},{48,0},{64,80},{80,96},{96,112},{112,64},{1... | collective-permute-start | bytes 393224 | tf_op jit(solution)/shard_map/ppermute | solution.py:290
  47.6 17.1 %collective-permute-start.19 = (bf16[128,512]{1,0:T(8,128)(2,1)S(1)}, bf16[128,512]{1,0:T(8,128)(2,1)S(1)}, u32[]{:S(2)}, u32[]{:S(2)}) collective-permute-start(bf16[128,512]{1,0:T(8,128)(2,1)S(1)} %get-tuple-element.40), channel_id=1, source_target_pairs={{0,32},{16,48},{32,0},{48,16},{64,96},{80,112},{96,64},{112,80},{1... | collective-permute-start | bytes 393224 | tf_op jit(solution)/shard_map/ppermute | solution.py:290
  52.1 12.6 %collective-permute-start.20 = (bf16[128,512]{1,0:T(8,128)(2,1)S(1)}, bf16[128,512]{1,0:T(8,128)(2,1)S(1)}, u32[]{:S(2)}, u32[]{:S(2)}) collective-permute-start(bf16[128,512]{1,0:T(8,128)(2,1)S(1)} %get-tuple-element.41), channel_id=1, source_target_pairs={{0,48},{16,0},{32,16},{48,32},{64,112},{80,64},{96,80},{112,96},{1... | collective-permute-start | bytes 393224 | tf_op jit(solution)/shard_map/ppermute | solution.py:290
  59.5 11.2 %collective-permute-start.15 = (bf16[128,512]{1,0:T(8,128)(2,1)S(1)}, bf16[128,512]{1,0:T(8,128)(2,1)S(1)}, u32[]{:S(2)}, u32[]{:S(2)}) collective-permute-start(bf16[128,512]{1,0:T(8,128)(2,1)S(1)} %get-tuple-element.35), channel_id=1, source_target_pairs={{0,16},{16,32},{32,48},{48,0},{64,80},{80,96},{96,112},{112,64},{1... | collective-permute-start | bytes 393224 | tf_op jit(solution)/shard_map/ppermute | solution.py:290
  59.9 13.9 %collective-permute-start.16 = (bf16[128,512]{1,0:T(8,128)(2,1)S(1)}, bf16[128,512]{1,0:T(8,128)(2,1)S(1)}, u32[]{:S(2)}, u32[]{:S(2)}) collective-permute-start(bf16[128,512]{1,0:T(8,128)(2,1)S(1)} %get-tuple-element.36), channel_id=1, source_target_pairs={{0,32},{16,48},{32,0},{48,16},{64,96},{80,112},{96,64},{112,80},{1... | collective-permute-start | bytes 393224 | tf_op jit(solution)/shard_map/ppermute | solution.py:290
  62.1 14.9 %collective-permute-start.17 = (bf16[128,512]{1,0:T(8,128)(2,1)S(1)}, bf16[128,512]{1,0:T(8,128)(2,1)S(1)}, u32[]{:S(2)}, u32[]{:S(2)}) collective-permute-start(bf16[128,512]{1,0:T(8,128)(2,1)S(1)} %get-tuple-element.37), channel_id=1, source_target_pairs={{0,48},{16,0},{32,16},{48,32},{64,112},{80,64},{96,80},{112,96},{1... | collective-permute-start | bytes 393224 | tf_op jit(solution)/shard_map/ppermute | solution.py:290
  64.8 12.3 %collective-permute-start.21 = (bf16[128,512]{1,0:T(8,128)(2,1)S(1)}, bf16[128,512]{1,0:T(8,128)(2,1)S(1)}, u32[]{:S(2)}, u32[]{:S(2)}) collective-permute-start(bf16[128,512]{1,0:T(8,128)(2,1)S(1)} %row_total.3), channel_id=1, source_target_pairs={{0,64},{16,80},{32,96},{48,112},{64,128},{80,144},{96,160},{112,17... | collective-permute-start | bytes 393224 | tf_op jit(solution)/shard_map/ppermute | solution.py:308
  66.5 10.6 %collective-permute-start.22 = (bf16[128,512]{1,0:T(8,128)(2,1)S(1)}, bf16[128,512]{1,0:T(8,128)(2,1)S(1)}, u32[]{:S(2)}, u32[]{:S(2)}) collective-permute-start(bf16[128,512]{1,0:T(8,128)(2,1)S(1)} %row_total.3), channel_id=1, source_target_pairs={{0,128},{16,144},{32,160},{48,176},{64,192},{80,208},{96,224},{112... | collective-permute-start | bytes 393224 | tf_op jit(solution)/shard_map/ppermute | solution.py:308
  77.4 10.8 %collective-permute-start.27 = (bf16[128,512]{1,0:T(8,128)(2,1)S(1)}, bf16[128,512]{1,0:T(8,128)(2,1)S(1)}, u32[]{:S(2)}, u32[]{:S(2)}) collective-permute-start(bf16[128,512]{1,0:T(8,128)(2,1)S(1)} %row_total.2), channel_id=1, source_target_pairs={{0,64},{16,80},{32,96},{48,112},{64,128},{80,144},{96,160},{112,17... | collective-permute-start | bytes 393224 | tf_op jit(solution)/shard_map/ppermute | solution.py:308
  79.1 11.6 %collective-permute-start.28 = (bf16[128,512]{1,0:T(8,128)(2,1)S(1)}, bf16[128,512]{1,0:T(8,128)(2,1)S(1)}, u32[]{:S(2)}, u32[]{:S(2)}) collective-permute-start(bf16[128,512]{1,0:T(8,128)(2,1)S(1)} %row_total.2), channel_id=1, source_target_pairs={{0,128},{16,144},{32,160},{48,176},{64,192},{80,208},{96,224},{112... | collective-permute-start | bytes 393224 | tf_op jit(solution)/shard_map/ppermute | solution.py:308
  83.3 12.1 %collective-permute-start.24 = (bf16[128,512]{1,0:T(8,128)(2,1)S(1)}, bf16[128,512]{1,0:T(8,128)(2,1)S(1)}, u32[]{:S(2)}, u32[]{:S(2)}) collective-permute-start(bf16[128,512]{1,0:T(8,128)(2,1)S(1)} %get-tuple-element.47), channel_id=1, source_target_pairs={{0,16},{16,32},{32,48},{48,0},{64,80},{80,96},{96,112},{112,64},{1... | collective-permute-start | bytes 393224 | tf_op jit(solution)/shard_map/ppermute | solution.py:290
  85.9 14.2 %collective-permute-start.25 = (bf16[128,512]{1,0:T(8,128)(2,1)S(1)}, bf16[128,512]{1,0:T(8,128)(2,1)S(1)}, u32[]{:S(2)}, u32[]{:S(2)}) collective-permute-start(bf16[128,512]{1,0:T(8,128)(2,1)S(1)} %get-tuple-element.48), channel_id=1, source_target_pairs={{0,32},{16,48},{32,0},{48,16},{64,96},{80,112},{96,64},{112,80},{1... | collective-permute-start | bytes 393224 | tf_op jit(solution)/shard_map/ppermute | solution.py:290
  88.2 13.3 %collective-permute-start.26 = (bf16[128,512]{1,0:T(8,128)(2,1)S(1)}, bf16[128,512]{1,0:T(8,128)(2,1)S(1)}, u32[]{:S(2)}, u32[]{:S(2)}) collective-permute-start(bf16[128,512]{1,0:T(8,128)(2,1)S(1)} %get-tuple-element.49), channel_id=1, source_target_pairs={{0,48},{16,0},{32,16},{48,32},{64,112},{80,64},{96,80},{112,96},{1... | collective-permute-start | bytes 393224 | tf_op jit(solution)/shard_map/ppermute | solution.py:290
  90.9 16.3 %collective-permute-start.30 = (bf16[128,512]{1,0:T(8,128)(2,1)S(1)}, bf16[128,512]{1,0:T(8,128)(2,1)S(1)}, u32[]{:S(2)}, u32[]{:S(2)}) collective-permute-start(bf16[128,512]{1,0:T(8,128)(2,1)S(1)} %get-tuple-element.52), channel_id=1, source_target_pairs={{0,16},{16,32},{32,48},{48,0},{64,80},{80,96},{96,112},{112,64},{1... | collective-permute-start | bytes 393224 | tf_op jit(solution)/shard_map/ppermute | solution.py:290
  91.4 17.1 %collective-permute-start.31 = (bf16[128,512]{1,0:T(8,128)(2,1)S(1)}, bf16[128,512]{1,0:T(8,128)(2,1)S(1)}, u32[]{:S(2)}, u32[]{:S(2)}) collective-permute-start(bf16[128,512]{1,0:T(8,128)(2,1)S(1)} %get-tuple-element.53), channel_id=1, source_target_pairs={{0,32},{16,48},{32,0},{48,16},{64,96},{80,112},{96,64},{112,80},{1... | collective-permute-start | bytes 393224 | tf_op jit(solution)/shard_map/ppermute | solution.py:290
  95.4 17.2 %collective-permute-start.32 = (bf16[128,512]{1,0:T(8,128)(2,1)S(1)}, bf16[128,512]{1,0:T(8,128)(2,1)S(1)}, u32[]{:S(2)}, u32[]{:S(2)}) collective-permute-start(bf16[128,512]{1,0:T(8,128)(2,1)S(1)} %get-tuple-element.54), channel_id=1, source_target_pairs={{0,48},{16,0},{32,16},{48,32},{64,112},{80,64},{96,80},{112,96},{1... | collective-permute-start | bytes 393224 | tf_op jit(solution)/shard_map/ppermute | solution.py:290
  (12 other events, 92.4 us)
